TPU v7x, 32 devices: a whole 2x2x4 slice. The times are simulated.
32 devices in a mesh: row: 4 (over z), col: 8 (over y, x, core).
Axes of the slice: x: 2, y: 2, z: 4, core: 2. Of those that a mesh axis runs over, the one named last changes fastest.
Arguments:
- panel_blocks: bfloat16 [8, 8, 512, 512], P('col', None, 'row'), may hold values from -0.25 to 0.25
- factor_inverse: bfloat16 [8, 512, 512], P('col')
- target_rows: int32 [8, 8], replicated, may hold values from 0 to 7, as said below
- owner_order: int32 [8], replicated, may hold values from 0 to 7, each once
- ancestor_rows: float32 [8, 512, 4096], P('col', 'row'), may hold values from -1.8 to 1.8
Outputs:
- updated_rows: float32 [8, 512, 4096], P('col', 'row')
Inputs may be any that keep to these rules, and one draw needn't show every extreme that they name: `target_rows`: each row names 8 different ancestor block rows in ascending order; each index of col holds exactly one supernode. `owner_order`: each ancestor block row once.
All inputs are finite; a program needn't handle non-finite values.
Results may differ from a plain program's by a relative error of at most 0.0024.
Values may be sent and summed in bfloat16 or wider, within the bound.
No kernel may reach another device: no remote copies, remote signals or barrier semaphores. Data moves between devices by JAX's collectives and lax.ppermute only.
A program may use at most 192 MiB of HBM per device.

v0:
```python
import jax
import jax.numpy as jnp
from jax import lax
from jax.sharding import PartitionSpec as P


def solve_rows(blocks, factor_inverse):
    return jnp.einsum(
        "spiw,svw->spiv", blocks, factor_inverse, preferred_element_type=jnp.float32
    ).astype(jnp.bfloat16)


def pick_rows(products, own_targets, order_part):
    matched = own_targets[None, :, :] == order_part[:, None, None]
    places = lax.broadcasted_iota(jnp.int32, matched.shape, 2)
    position = jnp.sum(jnp.where(matched, places, 0), axis=2)
    present = jnp.any(matched, axis=2)
    supernode_ids = lax.broadcasted_iota(jnp.int32, position.shape, 1)
    chosen = products[supernode_ids, position]
    return jnp.where(present[:, :, None, None, None], chosen, jnp.zeros((), chosen.dtype))


def slot_select(targets, order_part, slot_count):
    matched = targets[None, :, :] == order_part[:, None, None]
    present = jnp.any(matched, axis=2)
    rank = jnp.cumsum(present.astype(jnp.int32), axis=1) - 1
    slot_ids = lax.broadcasted_iota(jnp.int32, (1, slot_count, 1), 1)
    selected = present[:, None, :] & (rank[:, None, :] == slot_ids)
    return selected.astype(jnp.float32)


def body(panel_blocks, factor_inverse, target_rows, owner_order, ancestor_rows):
    supernodes = panel_blocks.shape[0]
    panel_count = panel_blocks.shape[1]
    own_height = panel_blocks.shape[2]
    width = panel_blocks.shape[3]
    ancestors = owner_order.shape[0]
    col_devices = lax.axis_size("col")
    col_place = lax.axis_index("col")
    own_targets = lax.dynamic_slice_in_dim(target_rows, col_place * supernodes, supernodes, 0)
    own_solved = solve_rows(panel_blocks, factor_inverse)
    products = jnp.einsum(
        "spiw,sqmw->spiqm",
        own_solved,
        lax.all_gather(own_solved, "row", axis=2, tiled=True),
        preferred_element_type=jnp.float32,
    ).astype(jnp.bfloat16)
    block_ids = lax.broadcasted_iota(jnp.int32, (1, 1, 1, ancestors), 3)
    slot_count = (supernodes * panel_count + ancestors - 1) // ancestors
    chosen = pick_rows(products, own_targets, owner_order)
    own_select = slot_select(own_targets, owner_order, slot_count).astype(jnp.bfloat16)
    outgoing = jnp.einsum(
        "jas,jsiqw->jaiqw", own_select, chosen, preferred_element_type=jnp.float32
    ).astype(jnp.bfloat16)
    received = lax.all_to_all(outgoing, "col", split_axis=0, concat_axis=0, tiled=True)
    held_rows = ancestor_rows.shape[0]
    received = received.reshape(col_devices, held_rows, slot_count, own_height, panel_count, width)
    all_targets = target_rows.reshape(col_devices, supernodes, panel_count)
    held_order = lax.dynamic_slice_in_dim(owner_order, col_place * held_rows, held_rows, 0)
    all_select = jax.vmap(lambda targets: slot_select(targets, held_order, slot_count))(all_targets)
    all_onehot = (all_targets[:, :, :, None] == block_ids).astype(jnp.float32)
    column_map = jnp.einsum("ckas,csqb->ckaqb", all_select, all_onehot).astype(jnp.bfloat16)
    spread = jnp.einsum(
        "ckaqb,ckaiqw->kibw", column_map, received, preferred_element_type=jnp.float32
    )
    summed = spread.reshape(held_rows, own_height, ancestors * width)
    return ancestor_rows - summed


def solution(mesh):
    return jax.shard_map(
        body,
        mesh=mesh,
        in_specs=(
            P("col", None, "row", None),
            P("col", None, None),
            P(),
            P(),
            P("col", "row", None),
        ),
        out_specs=P("col", "row", None),
        check_vma=False,
    )
```

profile of v0, /device:TPU:0, one launch (start us, length us, event | category | flops | bytes accessed | tf_op | source)
XLA Modules:
  0.0 242.0 jit_solution(3584995638375319723)
XLA Ops:
  6.5 0.0 copy-start
  6.5 0.0 all-gather.3.cloned.1.call-start
  6.5 1.2 copy-done
  7.8 2.8 %convolution_convert_fusion = bf16[8,128,512]{2,1,0:T(8,128)(2,1)} fusion(bf16[1,8,128,512]{3,2,1,0:T(8,128)(2,1)S(1)} %copy-done, bf16[1,512,512]{2,1,0:T(8,128)(2,1)} %param.6), kind=kOutput, calls=%fused_computation.9 | convolution fusion | flops 537395200 | bytes 2621440 | tf_op jit(solution)/shard_map/spiw,svw->spiv/dot_general | solution.py:8
  10.5 0.0 all-gather.3.cloned.1.call-update
  10.5 0.7 dynamic-slice_bitcast_fusion
  11.2 0.8 fusion.16
  12.1 0.8 compare_reduce_fusion
  13.0 81.2 %all-gather.3.cloned.1.call-done = bf16[8,512,512]{2,1,0:T(8,128)(2,1)} async-done(((bf16[8,128,512]{2,1,0:T(8,128)(2,1)}), bf16[8,512,512]{2,1,0:T(8,128)(2,1)}) %all-gather.3.cloned.1.call-update) | async-done | bytes 4194320 | tf_op jit(solution)/shard_map/all_gather | solution.py:45
  94.2 10.3 %convert_bitcast_fusion = bf16[1,8,128,8,512]{4,2,3,1,0:T(8,128)(2,1)} fusion(bf16[8,512,512]{2,1,0:T(8,128)(2,1)} %all-gather.3.cloned.1.call-done, bf16[8,128,512]{2,1,0:T(8,128)(2,1)} %convolution_convert_fusion), kind=kOutput, calls=%fused_computation.6 | convolution fusion | flops 4299161600 | bytes 13631488 | tf_op jit(solution)/shard_map/spiw,sqmw->spiqm/dot_general | solution.py:42
  104.4 8.1 %gather_fusion = bf16[8,128,8,512]{3,1,2,0:T(8,128)(2,1)} fusion(bf16[1,8,128,8,512]{4,2,3,1,0:T(8,128)(2,1)} %convert_bitcast_fusion, s32[8]{0:T(128)S(1)} %or_bitcast_fusion), kind=kCustom, calls=%fused_computation | custom fusion | bytes 16777280 | tf_op jit(solution)/shard_map/gather | solution.py:19
  112.5 9.3 %fusion = bf16[8,1,128,8,512]{4,2,3,1,0:T(8,128)(2,1)} fusion(bf16[8,128,8,512]{3,1,2,0:T(8,128)(2,1)} %gather_fusion, f32[8]{0:T(128)S(1)} %fusion.18, pred[8]{0:T(512)(128)(4,1)S(1)} %compare_reduce_fusion), kind=kLoop, calls=%fused_computation.2 | loop fusion | flops 16777216 | bytes 16777256 | tf_op jit(solution)/shard_map/convert_element_type | solution.py:54
  121.8 0.0 copy-start.2
  121.8 0.0 copy-start.1
  121.8 5.3 %all-to-all-start = ((bf16[8,1,128,8,512]{4,2,3,1,0:T(8,128)(2,1)}), bf16[8,1,128,8,512]{4,2,3,1,0:T(8,128)(2,1)}, u32[]{:S(2)}, u32[]{:S(2)}) async-start(bf16[8,1,128,8,512]{4,2,3,1,0:T(8,128)(2,1)} %fusion), calls=%async_computation | async-start | bytes 16777216 | tf_op jit(solution)/shard_map/all_to_all | solution.py:55
  127.1 0.0 copy-done.2
  127.1 0.6 dynamic_slice.10
  127.7 0.0 copy-done.1
  127.7 0.8 compare_reduce_fusion.1
  128.4 92.5 %all-to-all-done = bf16[8,1,128,8,512]{4,2,3,1,0:T(8,128)(2,1)} async-done(((bf16[8,1,128,8,512]{4,2,3,1,0:T(8,128)(2,1)}), bf16[8,1,128,8,512]{4,2,3,1,0:T(8,128)(2,1)}, u32[]{:S(2)}, u32[]{:S(2)}) %all-to-all-start) | async-done | bytes 8388640 | tf_op jit(solution)/shard_map/all_to_all | solution.py:55
  220.9 9.3 %fusion.5 = f32[1,128,8,512]{3,2,1,0:T(8,128)} fusion(bf16[8,1,128,8,512]{4,2,3,1,0:T(8,128)(2,1)} %all-to-all-done, bf16[8]{0:T(256)(128)(2,1)S(1)} %and_convert_fusion, s32[8,8]{1,0:T(8,128)S(1)} %copy-done.1), kind=kOutput, calls=%fused_computation.8 | convolution fusion | flops 67109888 | bytes 10486032 | tf_op jit(solution)/shard_map/ckaqb,ckaiqw->kibw/dot_general | solution.py:63
  230.2 1.7 reshape.208
  232.0 3.1 %sub.11 = f32[1,128,4096]{2,1,0:T(8,128)} subtract(f32[1,128,4096]{2,1,0:T(8,128)} %param.9, f32[1,128,4096]{2,1,0:T(8,128)S(1)} %reshape.208) | non-fusion elementwise | flops 524288 | bytes 6291456 | tf_op jit(solution)/shard_map/sub | solution.py:67
  (5 shorter events, 0.0 us)
Async XLA Ops:
  6.5 1.2 copy-start
  6.5 87.6 %all-gather.3.cloned.1.call-start = ((), (), s32[]{:S(2)}) async-start(), calls=%async_computation.1 | async-start | bytes 5242880 | tf_op jit(solution)/shard_map/all_gather | solution.py:45
  121.8 5.3 %copy-start.2 = (s32[8]{0:T(128)S(1)}, s32[8]{0:T(128)}, u32[]{:S(2)}) copy-start(s32[8]{0:T(128)} %param.8) | copy-start | bytes 100
  121.8 5.9 %copy-start.1 = (s32[8,8]{1,0:T(8,128)S(1)}, s32[8,8]{1,0:T(8,128)}, u32[]{:S(2)}) copy-start(s32[8,8]{1,0:T(8,128)} %param.7) | copy-start | bytes 772
  121.8 99.2 %all-to-all-start = ((bf16[8,1,128,8,512]{4,2,3,1,0:T(8,128)(2,1)}), bf16[8,1,128,8,512]{4,2,3,1,0:T(8,128)(2,1)}, u32[]{:S(2)}, u32[]{:S(2)}) async-start(bf16[8,1,128,8,512]{4,2,3,1,0:T(8,128)(2,1)} %fusion), calls=%async_computation | async-start | bytes 16777216 | tf_op jit(solution)/shard_map/all_to_all | solution.py:55
Sparse Core Ops, SparseCore 0:
  10.7 83.4 all-gather.2
where the time goes:
time: 242 us
  waiting for transfers between devices  174 us (72%)
  matrix products  22.3 us (9%)
  other arithmetic  14.9 us (6%)
  between operations  13.4 us (6%)
  local copies, waits for them, and re-layouts  12.3 us (5%)
  starting transfers between devices  5.28 us (2%)
    all_to_all x1, waiting for transfers between devices, body(): lax.all_to_all(outgoing, 'col', split_axis=0, concat_axis=0, tiled=True)  92.5 us
    all_gather x1, waiting for transfers between devices, body(): lax.all_gather(own_solved, 'row', axis=2, tiled=True)  81.2 us
    dot_general x1, matrix products, body(): jnp.einsum('spiw,sqmw->spiqm', own_solved, lax.all_gather(own_solved, 'ro...  10.3 us
    dot_general x1, matrix products, body(): jnp.einsum('ckaqb,ckaiqw->kibw', column_map, received, preferred_element_...  9.28 us
    convert_element_type x1, other arithmetic, body(): outgoing = jnp.einsum('jas,jsiqw->jaiqw', own_select, chosen, preferred_e...  9.27 us
    gather x1, local copies, waits for them, and re-layouts, pick_rows(): chosen = products[supernode_ids, position]  8.05 us
    all_to_all x1, starting transfers between devices, body(): lax.all_to_all(outgoing, 'col', split_axis=0, concat_axis=0, tiled=True)  5.27 us
  transfers between devices with their start and end apart: 2, of which 2 were waited for; matrix products, arithmetic and copies ran while one was open for 2% of the time, Pallas kernels for 0%

commit v1 on v0

--- a/solution.py
+++ b/solution.py
@@ -1,7 +1,15 @@
+import functools
+
 import jax
 import jax.numpy as jnp
 from jax import lax
+from jax.experimental import pallas as pl
+from jax.experimental.pallas import tpu as pltpu
 from jax.sharding import PartitionSpec as P
+
+BF16 = jnp.bfloat16
+F32 = jnp.float32
+VMEM_LIMIT = 40 * 1024 * 1024
 
 
 def solve_rows(blocks, factor_inverse):
@@ -29,7 +37,7 @@
     return selected.astype(jnp.float32)
 
 
-def body(panel_blocks, factor_inverse, target_rows, owner_order, ancestor_rows):
+def general_body(panel_blocks, factor_inverse, target_rows, owner_order, ancestor_rows):
     supernodes = panel_blocks.shape[0]
     panel_count = panel_blocks.shape[1]
     own_height = panel_blocks.shape[2]
@@ -67,7 +75,207 @@
     return ancestor_rows - summed
 
 
+PAIR = [(0, 1), (1, 0), (2, 3), (3, 2)]
+MIDDLE = [(0, 0), (1, 2), (2, 1), (3, 3)]
+CORE, X_HOP, Y_HOP = 1, 2, 4
+OWN_ORDER = (0, Y_HOP, X_HOP, X_HOP | Y_HOP)
+PAIR_ORDER = (0, X_HOP, Y_HOP, X_HOP | Y_HOP)
+
+
+def row_swap(value, pairs):
+    return lax.ppermute(value, "row", pairs)
+
+
+def col_swap(value, mask):
+    return lax.ppermute(value, "col", [(i, i ^ mask) for i in range(lax.axis_size("col"))])
+
+
+def dot_t(a, b):
+    return lax.dot_general(a, b, (((1,), (1,)), ((), ())), preferred_element_type=F32)
+
+
+def solve_kernel(panel_ref, inverse_ref, out_ref):
+    out_ref[...] = dot_t(panel_ref[...], inverse_ref[...]).astype(BF16)
+
+
+def solve_part(panel, inverse, first, count, tile):
+    width = panel.shape[1]
+    base = first // tile
+    return pl.pallas_call(
+        solve_kernel,
+        grid=(count // tile,),
+        in_specs=[
+            pl.BlockSpec((tile, width), lambda i: (base + i, 0)),
+            pl.BlockSpec((width, width), lambda i: (0, 0)),
+        ],
+        out_specs=pl.BlockSpec((tile, width), lambda i: (i, 0)),
+        out_shape=jax.ShapeDtypeStruct((count, width), BF16),
+        cost_estimate=pl.CostEstimate(
+            flops=2 * count * width * width, bytes_accessed=4 * count * width + 2 * width * width, transcendentals=0
+        ),
+        compiler_params=pltpu.CompilerParams(vmem_limit_bytes=VMEM_LIMIT),
+        name="solve_part",
+    )(panel, inverse)
+
+
+def pick_kernel(height, order_ref, own0, own1, ownb0, ownb1, pair0, pair1, pairb0, pairb1, out_ref):
+    col = lax.axis_index("col")
+    half = own0.shape[0]
+    width = own0.shape[1]
+
+    def put(place, mask, parts):
+        start = order_ref[jnp.bitwise_xor(col, mask)] * height
+        for number, (low, high) in enumerate(parts):
+            rows = pl.ds(place * height, height)
+            columns = pl.ds(number * width, width)
+
+            @pl.when(start < half)
+            def _():
+                out_ref[rows, columns] = low[pl.ds(pl.multiple_of(start, height), height), :]
+
+            @pl.when(start >= half)
+            def _():
+                out_ref[rows, columns] = high[pl.ds(pl.multiple_of(start - half, height), height), :]
+
+    for place, mask in enumerate(OWN_ORDER):
+        put(place, mask, ((own0, own1), (ownb0, ownb1)))
+    for place, mask in enumerate(PAIR_ORDER):
+        put(len(OWN_ORDER) + place, mask, ((pair0, pair1), (pairb0, pairb1)))
+
+
+def pick_blocks(order, height, arrays):
+    half, width = arrays[0].shape
+    rows = 2 * len(OWN_ORDER) * height
+    whole = pl.BlockSpec(memory_space=pltpu.VMEM)
+    return pl.pallas_call(
+        functools.partial(pick_kernel, height),
+        in_specs=[pl.BlockSpec(memory_space=pltpu.SMEM)] + [whole] * len(arrays),
+        out_specs=whole,
+        out_shape=jax.ShapeDtypeStruct((rows, 2 * width), BF16),
+        cost_estimate=pl.CostEstimate(flops=0, bytes_accessed=2 * len(arrays) * half * width + 4 * rows * width, transcendentals=0),
+        compiler_params=pltpu.CompilerParams(vmem_limit_bytes=VMEM_LIMIT),
+        name="pick_blocks",
+    )(order, *arrays)
+
+
+def product_kernel(a_ref, xa_ref, xb_ref, own_keep, own_send, pair_keep, pair_send):
+    width = xa_ref.shape[1]
+    result = dot_t(a_ref[:, :width], xa_ref[...]) + dot_t(a_ref[:, width:], xb_ref[...])
+    for step, out in enumerate((own_keep, own_send, pair_keep, pair_send)):
+
+        @pl.when(pl.program_id(0) == step)
+        def _():
+            out[...] = result.astype(out.dtype)
+
+
+def products(a, xa, xb):
+    rows, depth = a.shape
+    tile = rows // 4
+    count, width = xa.shape
+    fixed = lambda i: (0, 0)
+    shapes = [jax.ShapeDtypeStruct((tile, count), t) for t in (F32, BF16, F32, BF16)]
+    return pl.pallas_call(
+        product_kernel,
+        grid=(4,),
+        in_specs=[
+            pl.BlockSpec((tile, depth), lambda i: (i, 0)),
+            pl.BlockSpec((count, width), fixed),
+            pl.BlockSpec((count, width), fixed),
+        ],
+        out_specs=[pl.BlockSpec((tile, count), fixed)] * 4,
+        out_shape=shapes,
+        cost_estimate=pl.CostEstimate(
+            flops=2 * rows * depth * count, bytes_accessed=2 * rows * depth + 4 * count * width + 3 * rows * count, transcendentals=0
+        ),
+        compiler_params=pltpu.CompilerParams(vmem_limit_bytes=VMEM_LIMIT),
+        name="products",
+    )(a, xa, xb)
+
+
+def reduce_chunk(a, xa, xb, height):
+    own_keep, own_send, pair_keep, pair_send = products(a, xa, xb)
+    own_got = col_swap(own_send, X_HOP).astype(F32)
+    pair_got = col_swap(pair_send, Y_HOP).astype(F32)
+    own_half = own_keep[:height] + own_got[:height]
+    own_next = (own_keep[height:] + own_got[height:]).astype(BF16)
+    pair_half = pair_keep[:height] + pair_got[:height]
+    pair_next = (pair_keep[height:] + pair_got[height:]).astype(BF16)
+    own_last = col_swap(own_next, Y_HOP)
+    pair_last = col_swap(pair_next, X_HOP)
+    pair_done = (pair_half + pair_last.astype(F32)).astype(BF16)
+    return own_half, own_last, row_swap(pair_done, PAIR)
+
+
+def finish_kernel(height, places, anc_ref, *refs):
+    out_ref = refs[-1]
+    parts = refs[:-1]
+    row = lax.axis_index("row")
+    width = 4 * height
+    low = row & 1
+    high = row >> 1
+    own_first = jnp.bitwise_or(low * 2, high)
+    spots = (own_first, jnp.bitwise_xor(own_first, 1), jnp.bitwise_xor(own_first, 2), jnp.bitwise_xor(own_first, 3))
+    for number, (which, first, count) in enumerate(places):
+        half, last, back = parts[3 * number : 3 * number + 3]
+        for block in range(count):
+            source = pl.ds(block * height, height)
+            own_at = pl.ds(pl.multiple_of((first + block) * width + spots[which] * height, height), height)
+            pair_at = pl.ds(pl.multiple_of((first + block) * width + spots[2 + which] * height, height), height)
+            out_ref[:, own_at] = anc_ref[:, own_at] - (half[:, source] + last[:, source].astype(F32))
+            out_ref[:, pair_at] = anc_ref[:, pair_at] - back[:, source].astype(F32)
+
+
+def finish(ancestor, places, parts, height):
+    whole = pl.BlockSpec(memory_space=pltpu.VMEM)
+    return pl.pallas_call(
+        functools.partial(finish_kernel, height, places),
+        in_specs=[whole] * (1 + len(parts)),
+        out_specs=whole,
+        out_shape=jax.ShapeDtypeStruct(ancestor.shape, F32),
+        cost_estimate=pl.CostEstimate(flops=2 * ancestor.size, bytes_accessed=12 * ancestor.size, transcendentals=0),
+        compiler_params=pltpu.CompilerParams(vmem_limit_bytes=VMEM_LIMIT),
+        name="finish",
+    )(ancestor, *parts)
+
+
+def paired_body(panel_blocks, factor_inverse, target_rows, owner_order, ancestor_rows):
+    _, panel_count, height, width = panel_blocks.shape
+    panel = panel_blocks.reshape(panel_count * height, width)
+    inverse = factor_inverse[0]
+    half_blocks = panel_count // 2
+    half = half_blocks * height
+    own = [solve_part(panel, inverse, k * half, half, half // 2) for k in range(2)]
+    first = [row_swap(s, MIDDLE) for s in own]
+    pair = [row_swap(s, PAIR) for s in own]
+    second = [row_swap(s, MIDDLE) for s in pair]
+    own_b = [col_swap(s, CORE) for s in own]
+    pair_b = [col_swap(s, CORE) for s in pair]
+    a = pick_blocks(owner_order, height, [*own, *own_b, *pair, *pair_b])
+    places = []
+    parts = []
+    for which, arrays in enumerate((first, second)):
+        for k in range(2):
+            parts += reduce_chunk(a, arrays[k], col_swap(arrays[k], CORE), height)
+            places.append((which, k * half_blocks, half_blocks))
+    result = finish(ancestor_rows[0], tuple(places), parts, height)
+    return result[None]
+
+
 def solution(mesh):
+    def body(panel_blocks, factor_inverse, target_rows, owner_order, ancestor_rows):
+        supernodes, panel_count, height, _ = panel_blocks.shape
+        held = ancestor_rows.shape[0]
+        paired = (
+            mesh.shape["row"] == 4
+            and mesh.shape["col"] == 8
+            and panel_count == owner_order.shape[0] == 8
+            and supernodes == 1
+            and held == 1
+            and height % 128 == 0
+        )
+        chosen = paired_body if paired else general_body
+        return chosen(panel_blocks, factor_inverse, target_rows, owner_order, ancestor_rows)
+
     return jax.shard_map(
         body,
         mesh=mesh,

time: 242 us -> 111 us (0.46)
  waiting for transfers between devices: 174 us -> 49.3 us
  starting transfers between devices: 5.28 us -> 45.3 us
  matrix products: 22.3 us -> 0 us
  other arithmetic: 14.9 us -> 1.11 us
  between operations: 13.4 us -> 0.31 us
  Pallas kernels: 0 us -> 12.3 us
  local copies, waits for them, and re-layouts: 12.3 us -> 2.28 us
    all_to_all x1 -> x0, waiting for transfers between devices: 92.5 us -> none  [body(): lax.all_to_all(outgoing, 'col', split_axis=0, concat_axis=0, tiled=True)]
    all_gather x1 -> x0, waiting for transfers between devices: 81.2 us -> none  [body(): lax.all_gather(own_solved, 'row', axis=2, tiled=True)]
    ppermute x0 -> x34, waiting for transfers between devices: none -> 49.3 us  [the longest x24 26.2 us: col_swap(): lax.ppermute(value, 'col', [(i, i ^ mask) for i in range(lax.axis_size('c...]
    ppermute x0 -> x34, starting transfers between devices: none -> 45.3 us  [the longest x10 26.3 us: row_swap(): return lax.ppermute(value, 'row', pairs)]
    dot_general x3 -> x0, matrix products: 22.3 us -> none  [the longest x1 10.3 us: body(): jnp.einsum('spiw,sqmw->spiqm', own_solved, lax.all_gather(own_solved, 'ro...]
    pallas_call x0 -> x8, Pallas kernels: none -> 12.3 us  [the longest x4 8.12 us: products(): pl.pallas_call(product_kernel, grid=(4,), in_specs=[pl.BlockSpec((tile, d...]
    convert_element_type x1 -> x20, other arithmetic: 9.27 us -> 1.11 us  [the longest x4 0.34 us: reduce_chunk(): own_next = (own_keep[height:] + own_got[height:]).astype(BF16)]
    gather x1 -> x0, local copies, waits for them, and re-layouts: 8.05 us -> none  [pick_rows(): chosen = products[supernode_ids, position]]
  transfers between devices with their start and end apart: 2 -> 34, of which waited for: 2 -> 18; matrix products, arithmetic and copies ran while one was open for 2% -> 1% of each run, Pallas kernels for 0% -> 9%
where the time goes in v1:
time: 111 us
  waiting for transfers between devices  49.3 us (44%)
  starting transfers between devices  45.3 us (41%)
  Pallas kernels  12.3 us (11%)
  local copies, waits for them, and re-layouts  2.28 us (2%)
  other arithmetic  1.11 us (1%)
    ppermute x10, starting transfers between devices, row_swap(): return lax.ppermute(value, 'row', pairs)  26.3 us
    ppermute x24, waiting for transfers between devices, col_swap(): lax.ppermute(value, 'col', [(i, i ^ mask) for i in range(lax.axis_size('c...  26.2 us
    ppermute x10, waiting for transfers between devices, row_swap(): return lax.ppermute(value, 'row', pairs)  23.1 us
    ppermute x24, starting transfers between devices, col_swap(): lax.ppermute(value, 'col', [(i, i ^ mask) for i in range(lax.axis_size('c...  19 us
    pallas_call x4, Pallas kernels, products(): pl.pallas_call(product_kernel, grid=(4,), in_specs=[pl.BlockSpec((tile, d...  8.12 us
    unnamed x8, local copies, waits for them, and re-layouts  2.28 us
  transfers between devices with their start and end apart: 34, of which 18 were waited for; matrix products, arithmetic and copies ran while one was open for 1% of the time, Pallas kernels for 9%

profile of v1, /device:TPU:0, one launch (start us, length us, event | category | flops | bytes accessed | tf_op | source)
XLA Modules:
  0.0 110.6 jit_solution(1932667219280470399)
XLA Ops:
  0.0 1.2 %copy-done = bf16[1,8,128,512]{3,2,1,0:T(8,128)(2,1)S(1)} copy-done((bf16[1,8,128,512]{3,2,1,0:T(8,128)(2,1)S(1)}, bf16[1,8,128,512]{3,2,1,0:T(8,128)(2,1)}, u32[]{:S(2)}) %copy-start) | copy-done | bytes 1048600
  1.2 1.0 copy-done.2
  2.3 0.7 solve_part.2.own0
  3.0 3.1 %collective-permute-start.2 = (bf16[512,512]{1,0:T(8,128)(2,1)S(1)}, bf16[512,512]{1,0:T(8,128)(2,1)S(1)}, u32[]{:S(2)}, u32[]{:S(2)}) collective-permute-start(bf16[512,512]{1,0:T(8,128)(2,1)S(1)} %solve_part.2.own0), channel_id=1, source_target_pairs={{0,8},{8,0},{16,24},{24,16},{1,9},{9,1},{17,25},{25,17},{2,10},{10... | collective-permute-start | bytes 1572872 | tf_op jit(solution)/shard_map/ppermute | solution.py:86
  6.0 0.7 solve_part.3.own1
  6.9 0.7 collective-permute-start.13
  7.6 0.7 collective-permute-start.6
  8.3 10.5 %collective-permute-done.2.pair0 = bf16[512,512]{1,0:T(8,128)(2,1)S(1)} collective-permute-done((bf16[512,512]{1,0:T(8,128)(2,1)S(1)}, bf16[512,512]{1,0:T(8,128)(2,1)S(1)}, u32[]{:S(2)}, u32[]{:S(2)}) %collective-permute-start.2) | collective-permute-done | bytes 524320 | tf_op jit(solution)/shard_map/ppermute | solution.py:86
  18.8 10.4 %collective-permute-done.3.pair1 = bf16[512,512]{1,0:T(8,128)(2,1)S(1)} collective-permute-done((bf16[512,512]{1,0:T(8,128)(2,1)S(1)}, bf16[512,512]{1,0:T(8,128)(2,1)S(1)}, u32[]{:S(2)}, u32[]{:S(2)}) %collective-permute-start.3) | collective-permute-done | bytes 524320 | tf_op jit(solution)/shard_map/ppermute | solution.py:86
  29.2 0.5 collective-permute-start.5
  30.2 0.7 collective-permute-start.27
  31.1 0.7 collective-permute-start.20
  31.9 0.8 pick_blocks.1.a_ref
  32.7 2.0 %products.5 = (f32[256,512]{1,0:T(8,128)S(1)}, bf16[256,512]{1,0:T(8,128)(2,1)S(1)}, f32[256,512]{1,0:T(8,128)S(1)}, bf16[256,512]{1,0:T(8,128)(2,1)S(1)}) custom-call(bf16[1024,1024]{1,0:T(8,128)(2,1)S(1)} %pick_blocks.1.a_ref, bf16[512,512]{1,0:T(8,128)(2,1)S(1)} %collective-permute-done.13.xa_ref, bf16[512,512]{1,0:T(8,128)(2,1)S(1)} %collective-permute-done.14.xb_ref), custom_call_target="tpu_custom_call" | custom-call | flops 1073741824 | bytes 4718592 | tf_op jit(solution)/shard_map/products/pallas_call | solution.py:177
  34.8 1.8 %collective-permute-start.17 = (bf16[256,512]{1,0:T(8,128)(2,1)S(1)}, bf16[256,512]{1,0:T(8,128)(2,1)S(1)}, u32[]{:S(2)}, u32[]{:S(2)}) collective-permute-start(bf16[256,512]{1,0:T(8,128)(2,1)S(1)} %get-tuple-element.28), channel_id=1, source_target_pairs={{0,4},{1,5},{2,6},{3,7},{4,0},{5,1},{6,2},{7,3},{8,12},{9,13},{10,... | collective-permute-start | bytes 786440 | tf_op jit(solution)/shard_map/ppermute | solution.py:90
  36.5 1.5 %collective-permute-start.15 = (bf16[256,512]{1,0:T(8,128)(2,1)S(1)}, bf16[256,512]{1,0:T(8,128)(2,1)S(1)}, u32[]{:S(2)}, u32[]{:S(2)}) collective-permute-start(bf16[256,512]{1,0:T(8,128)(2,1)S(1)} %get-tuple-element.26), channel_id=1, source_target_pairs={{0,2},{1,3},{2,0},{3,1},{4,6},{5,7},{6,4},{7,5},{8,10},{9,11},{10,... | collective-permute-start | bytes 786440 | tf_op jit(solution)/shard_map/ppermute | solution.py:90
  38.0 2.0 %products.4 = (f32[256,512]{1,0:T(8,128)S(1)}, bf16[256,512]{1,0:T(8,128)(2,1)S(1)}, f32[256,512]{1,0:T(8,128)S(1)}, bf16[256,512]{1,0:T(8,128)(2,1)S(1)}) custom-call(bf16[1024,1024]{1,0:T(8,128)(2,1)S(1)} %pick_blocks.1.a_ref, bf16[512,512]{1,0:T(8,128)(2,1)S(1)} %collective-permute-done.6.xa_ref, bf16[512,512]{1,0:T(8,128)(2,1)S(1)} %collective-permute-done.7.xb_ref), custom_call_target="tpu_custom_call" | custom-call | flops 1073741824 | bytes 4718592 | tf_op jit(solution)/shard_map/products/pallas_call | solution.py:177
  40.1 0.6 collective-permute-start.10
  41.0 3.0 %collective-permute-done.17 = bf16[256,512]{1,0:T(8,128)(2,1)S(1)} collective-permute-done((bf16[256,512]{1,0:T(8,128)(2,1)S(1)}, bf16[256,512]{1,0:T(8,128)(2,1)S(1)}, u32[]{:S(2)}, u32[]{:S(2)}) %collective-permute-start.17) | collective-permute-done | bytes 262176 | tf_op jit(solution)/shard_map/ppermute | solution.py:90
  44.1 1.6 %collective-permute-done.15 = bf16[256,512]{1,0:T(8,128)(2,1)S(1)} collective-permute-done((bf16[256,512]{1,0:T(8,128)(2,1)S(1)}, bf16[256,512]{1,0:T(8,128)(2,1)S(1)}, u32[]{:S(2)}, u32[]{:S(2)}) %collective-permute-start.15) | collective-permute-done | bytes 262176 | tf_op jit(solution)/shard_map/ppermute | solution.py:90
  45.7 1.5 %collective-permute-start.18 = (bf16[128,512]{1,0:T(8,128)(2,1)S(1)}, bf16[128,512]{1,0:T(8,128)(2,1)S(1)}, u32[]{:S(2)}, u32[]{:S(2)}) collective-permute-start(bf16[128,512]{1,0:T(8,128)(2,1)S(1)} %fusion.8), channel_id=1, source_target_pairs={{0,2},{1,3},{2,0},{3,1},{4,6},{5,7},{6,4},{7,5},{8,10},{9,11},{10,... | collective-permute-start | bytes 393224 | tf_op jit(solution)/shard_map/ppermute | solution.py:90
  47.4 1.4 %collective-permute-done.10 = bf16[256,512]{1,0:T(8,128)(2,1)S(1)} collective-permute-done((bf16[256,512]{1,0:T(8,128)(2,1)S(1)}, bf16[256,512]{1,0:T(8,128)(2,1)S(1)}, u32[]{:S(2)}, u32[]{:S(2)}) %collective-permute-start.10) | collective-permute-done | bytes 262176 | tf_op jit(solution)/shard_map/ppermute | solution.py:90
  48.8 1.7 %collective-permute-start.16 = (bf16[128,512]{1,0:T(8,128)(2,1)S(1)}, bf16[128,512]{1,0:T(8,128)(2,1)S(1)}, u32[]{:S(2)}, u32[]{:S(2)}) collective-permute-start(bf16[128,512]{1,0:T(8,128)(2,1)S(1)} %get-tuple-element.41), channel_id=1, source_target_pairs={{0,4},{1,5},{2,6},{3,7},{4,0},{5,1},{6,2},{7,3},{8,12},{9,13},{10,... | collective-permute-start | bytes 393224 | tf_op jit(solution)/shard_map/ppermute | solution.py:90
  50.6 0.7 collective-permute-done.8
  51.3 1.5 %collective-permute-start.11 = (bf16[128,512]{1,0:T(8,128)(2,1)S(1)}, bf16[128,512]{1,0:T(8,128)(2,1)S(1)}, u32[]{:S(2)}, u32[]{:S(2)}) collective-permute-start(bf16[128,512]{1,0:T(8,128)(2,1)S(1)} %fusion.12), channel_id=1, source_target_pairs={{0,2},{1,3},{2,0},{3,1},{4,6},{5,7},{6,4},{7,5},{8,10},{9,11},{10,... | collective-permute-start | bytes 393224 | tf_op jit(solution)/shard_map/ppermute | solution.py:90
  53.0 0.7 collective-permute-done.18
  54.1 18.3 %collective-permute-start.19 = (bf16[128,512]{1,0:T(8,128)(2,1)S(1)}, bf16[128,512]{1,0:T(8,128)(2,1)S(1)}, u32[]{:S(2)}, u32[]{:S(2)}) collective-permute-start(bf16[128,512]{1,0:T(8,128)(2,1)S(1)} %fusion.10), channel_id=1, source_target_pairs={{0,8},{8,0},{16,24},{24,16},{1,9},{9,1},{17,25},{25,17},{2,10},{10... | collective-permute-start | bytes 393224 | tf_op jit(solution)/shard_map/ppermute | solution.py:86
  72.5 2.0 %products.7 = (f32[256,512]{1,0:T(8,128)S(1)}, bf16[256,512]{1,0:T(8,128)(2,1)S(1)}, f32[256,512]{1,0:T(8,128)S(1)}, bf16[256,512]{1,0:T(8,128)(2,1)S(1)}) custom-call(bf16[1024,1024]{1,0:T(8,128)(2,1)S(1)} %pick_blocks.1.a_ref, bf16[512,512]{1,0:T(8,128)(2,1)S(1)} %collective-permute-done.27.xa_ref, bf16[512,512]{1,0:T(8,128)(2,1)S(1)} %collective-permute-done.28.xb_ref), custom_call_target="tpu_custom_call" | custom-call | flops 1073741824 | bytes 4718592 | tf_op jit(solution)/shard_map/products/pallas_call | solution.py:177
  74.5 1.6 %collective-permute-start.29 = (bf16[256,512]{1,0:T(8,128)(2,1)S(1)}, bf16[256,512]{1,0:T(8,128)(2,1)S(1)}, u32[]{:S(2)}, u32[]{:S(2)}) collective-permute-start(bf16[256,512]{1,0:T(8,128)(2,1)S(1)} %get-tuple-element.34), channel_id=1, source_target_pairs={{0,2},{1,3},{2,0},{3,1},{4,6},{5,7},{6,4},{7,5},{8,10},{9,11},{10,... | collective-permute-start | bytes 786440 | tf_op jit(solution)/shard_map/ppermute | solution.py:90
  76.1 0.5 collective-permute-start.31
  76.7 2.0 %products.6 = (f32[256,512]{1,0:T(8,128)S(1)}, bf16[256,512]{1,0:T(8,128)(2,1)S(1)}, f32[256,512]{1,0:T(8,128)S(1)}, bf16[256,512]{1,0:T(8,128)(2,1)S(1)}) custom-call(bf16[1024,1024]{1,0:T(8,128)(2,1)S(1)} %pick_blocks.1.a_ref, bf16[512,512]{1,0:T(8,128)(2,1)S(1)} %collective-permute-done.20.xa_ref, bf16[512,512]{1,0:T(8,128)(2,1)S(1)} %collective-permute-done.21.xb_ref), custom_call_target="tpu_custom_call" | custom-call | flops 1073741824 | bytes 4718592 | tf_op jit(solution)/shard_map/products/pallas_call | solution.py:177
  78.7 3.1 %collective-permute-done.29 = bf16[256,512]{1,0:T(8,128)(2,1)S(1)} collective-permute-done((bf16[256,512]{1,0:T(8,128)(2,1)S(1)}, bf16[256,512]{1,0:T(8,128)(2,1)S(1)}, u32[]{:S(2)}, u32[]{:S(2)}) %collective-permute-start.29) | collective-permute-done | bytes 262176 | tf_op jit(solution)/shard_map/ppermute | solution.py:90
  81.8 1.5 %collective-permute-start.22 = (bf16[256,512]{1,0:T(8,128)(2,1)S(1)}, bf16[256,512]{1,0:T(8,128)(2,1)S(1)}, u32[]{:S(2)}, u32[]{:S(2)}) collective-permute-start(bf16[256,512]{1,0:T(8,128)(2,1)S(1)} %get-tuple-element.30), channel_id=1, source_target_pairs={{0,2},{1,3},{2,0},{3,1},{4,6},{5,7},{6,4},{7,5},{8,10},{9,11},{10,... | collective-permute-start | bytes 786440 | tf_op jit(solution)/shard_map/ppermute | solution.py:90
  83.5 0.5 collective-permute-start.24
  84.1 4.4 %collective-permute-done.22 = bf16[256,512]{1,0:T(8,128)(2,1)S(1)} collective-permute-done((bf16[256,512]{1,0:T(8,128)(2,1)S(1)}, bf16[256,512]{1,0:T(8,128)(2,1)S(1)}, u32[]{:S(2)}, u32[]{:S(2)}) %collective-permute-start.22) | collective-permute-done | bytes 262176 | tf_op jit(solution)/shard_map/ppermute | solution.py:90
  88.6 1.3 %collective-permute-done.24 = bf16[256,512]{1,0:T(8,128)(2,1)S(1)} collective-permute-done((bf16[256,512]{1,0:T(8,128)(2,1)S(1)}, bf16[256,512]{1,0:T(8,128)(2,1)S(1)}, u32[]{:S(2)}, u32[]{:S(2)}) %collective-permute-start.24) | collective-permute-done | bytes 262176 | tf_op jit(solution)/shard_map/ppermute | solution.py:90
  89.9 1.2 %collective-permute-start.32 = (bf16[128,512]{1,0:T(8,128)(2,1)S(1)}, bf16[128,512]{1,0:T(8,128)(2,1)S(1)}, u32[]{:S(2)}, u32[]{:S(2)}) collective-permute-start(bf16[128,512]{1,0:T(8,128)(2,1)S(1)} %fusion), channel_id=1, source_target_pairs={{0,2},{1,3},{2,0},{3,1},{4,6},{5,7},{6,4},{7,5},{8,10},{9,11},{10,... | collective-permute-start | bytes 393224 | tf_op jit(solution)/shard_map/ppermute | solution.py:90
  91.2 3.9 %collective-permute-done.32 = bf16[128,512]{1,0:T(8,128)(2,1)S(1)} collective-permute-done((bf16[128,512]{1,0:T(8,128)(2,1)S(1)}, bf16[128,512]{1,0:T(8,128)(2,1)S(1)}, u32[]{:S(2)}, u32[]{:S(2)}) %collective-permute-start.32) | collective-permute-done | bytes 131104 | tf_op jit(solution)/shard_map/ppermute | solution.py:90
  95.1 1.3 %collective-permute-start.25 = (bf16[128,512]{1,0:T(8,128)(2,1)S(1)}, bf16[128,512]{1,0:T(8,128)(2,1)S(1)}, u32[]{:S(2)}, u32[]{:S(2)}) collective-permute-start(bf16[128,512]{1,0:T(8,128)(2,1)S(1)} %fusion.4), channel_id=1, source_target_pairs={{0,2},{1,3},{2,0},{3,1},{4,6},{5,7},{6,4},{7,5},{8,10},{9,11},{10,... | collective-permute-start | bytes 393224 | tf_op jit(solution)/shard_map/ppermute | solution.py:90
  96.5 3.6 %collective-permute-done.25 = bf16[128,512]{1,0:T(8,128)(2,1)S(1)} collective-permute-done((bf16[128,512]{1,0:T(8,128)(2,1)S(1)}, bf16[128,512]{1,0:T(8,128)(2,1)S(1)}, u32[]{:S(2)}, u32[]{:S(2)}) %collective-permute-start.25) | collective-permute-done | bytes 131104 | tf_op jit(solution)/shard_map/ppermute | solution.py:90
  100.5 1.7 %collective-permute-start.23 = (bf16[128,512]{1,0:T(8,128)(2,1)S(1)}, bf16[128,512]{1,0:T(8,128)(2,1)S(1)}, u32[]{:S(2)}, u32[]{:S(2)}) collective-permute-start(bf16[128,512]{1,0:T(8,128)(2,1)S(1)} %get-tuple-element.39), channel_id=1, source_target_pairs={{0,4},{1,5},{2,6},{3,7},{4,0},{5,1},{6,2},{7,3},{8,12},{9,13},{10,... | collective-permute-start | bytes 393224 | tf_op jit(solution)/shard_map/ppermute | solution.py:90
  102.2 1.0 collective-permute-start.33
  103.2 1.0 collective-permute-start.26
  104.3 0.8 collective-permute-done.30.refs_10_
  105.0 1.4 %collective-permute-done.23.refs_7_ = bf16[128,512]{1,0:T(8,128)(2,1)S(1)} collective-permute-done((bf16[128,512]{1,0:T(8,128)(2,1)S(1)}, bf16[128,512]{1,0:T(8,128)(2,1)S(1)}, u32[]{:S(2)}, u32[]{:S(2)}) %collective-permute-start.23) | collective-permute-done | bytes 131104 | tf_op jit(solution)/shard_map/ppermute | solution.py:90
  106.4 0.8 collective-permute-done.33.refs_11_
  107.2 1.4 %collective-permute-done.26.refs_8_ = bf16[128,512]{1,0:T(8,128)(2,1)S(1)} collective-permute-done((bf16[128,512]{1,0:T(8,128)(2,1)S(1)}, bf16[128,512]{1,0:T(8,128)(2,1)S(1)}, u32[]{:S(2)}, u32[]{:S(2)}) %collective-permute-start.26) | collective-permute-done | bytes 131104 | tf_op jit(solution)/shard_map/ppermute | solution.py:86
  108.6 1.9 %finish.1 = f32[128,4096]{1,0:T(8,128)} custom-call(f32[128,4096]{1,0:T(8,128)S(1)} %bitcast.6, f32[128,512]{1,0:T(8,128)S(1)} %get-tuple-element.44.refs_0_, bf16[128,512]{1,0:T(8,128)(2,1)S(1)} %collective-permute-done.9.refs_1_, bf16[128,512]{1,0:T(8,128)(2,1)S(1)} %collective-permute-done.12.refs_2_, f32[128,512]{1,0:T(8,128)S(1)} %get-tuple-element.42.refs_3_, ...), custom_call_target="tpu_custom_call" | custom-call | flops 1048576 | bytes 6291456 | tf_op jit(solution)/shard_map/finish/pallas_call | solution.py:230
  (56 shorter events, 3.2 us)
Async XLA Ops:
  0.0 1.2 %copy-start = (bf16[1,8,128,512]{3,2,1,0:T(8,128)(2,1)S(1)}, bf16[1,8,128,512]{3,2,1,0:T(8,128)(2,1)}, u32[]{:S(2)}) copy-start(bf16[1,8,128,512]{3,2,1,0:T(8,128)(2,1)} %param.5) | copy-start | bytes 3145732
  1.2 1.0 copy-start.2
  2.3 29.6 %copy-start.3 = (s32[8]{0:T(128)S(1)}, s32[8]{0:T(128)}, u32[]{:S(2)}) copy-start(s32[8]{0:T(128)} %order_ref.1) | copy-start | bytes 100
  3.0 15.8 %collective-permute-start.2 = (bf16[512,512]{1,0:T(8,128)(2,1)S(1)}, bf16[512,512]{1,0:T(8,128)(2,1)S(1)}, u32[]{:S(2)}, u32[]{:S(2)}) collective-permute-start(bf16[512,512]{1,0:T(8,128)(2,1)S(1)} %solve_part.2.own0), channel_id=1, source_target_pairs={{0,8},{8,0},{16,24},{24,16},{1,9},{9,1},{17,25},{25,17},{2,10},{10... | collective-permute-start | bytes 1572872 | tf_op jit(solution)/shard_map/ppermute | solution.py:86
  6.7 22.5 %collective-permute-start.3 = (bf16[512,512]{1,0:T(8,128)(2,1)S(1)}, bf16[512,512]{1,0:T(8,128)(2,1)S(1)}, u32[]{:S(2)}, u32[]{:S(2)}) collective-permute-start(bf16[512,512]{1,0:T(8,128)(2,1)S(1)} %solve_part.3.own1), channel_id=1, source_target_pairs={{0,8},{8,0},{16,24},{24,16},{1,9},{9,1},{17,25},{25,17},{2,10},{10... | collective-permute-start | bytes 1572872 | tf_op jit(solution)/shard_map/ppermute | solution.py:86
  6.8 22.4 %collective-permute-start = (bf16[512,512]{1,0:T(8,128)(2,1)S(1)}, bf16[512,512]{1,0:T(8,128)(2,1)S(1)}, u32[]{:S(2)}, u32[]{:S(2)}) collective-permute-start(bf16[512,512]{1,0:T(8,128)(2,1)S(1)} %solve_part.2.own0), channel_id=1, source_target_pairs={{0,1},{1,0},{2,3},{3,2},{4,5},{5,4},{6,7},{7,6},{8,9},{9,8},{10,11... | collective-permute-start | bytes 1572872 | tf_op jit(solution)/shard_map/ppermute | solution.py:90
  6.9 22.8 %collective-permute-start.13 = (bf16[512,512]{1,0:T(8,128)(2,1)S(1)}, bf16[512,512]{1,0:T(8,128)(2,1)S(1)}, u32[]{:S(2)}, u32[]{:S(2)}) collective-permute-start(bf16[512,512]{1,0:T(8,128)(2,1)S(1)} %solve_part.3.own1), channel_id=1, source_target_pairs={{0,0},{8,16},{16,8},{24,24},{1,1},{9,17},{17,9},{25,25},{2,2},{10,... | collective-permute-start | bytes 1572872 | tf_op jit(solution)/shard_map/ppermute | solution.py:86
  7.6 22.2 %collective-permute-start.6 = (bf16[512,512]{1,0:T(8,128)(2,1)S(1)}, bf16[512,512]{1,0:T(8,128)(2,1)S(1)}, u32[]{:S(2)}, u32[]{:S(2)}) collective-permute-start(bf16[512,512]{1,0:T(8,128)(2,1)S(1)} %solve_part.2.own0), channel_id=1, source_target_pairs={{0,0},{8,16},{16,8},{24,24},{1,1},{9,17},{17,9},{25,25},{2,2},{10,... | collective-permute-start | bytes 1572872 | tf_op jit(solution)/shard_map/ppermute | solution.py:86
  18.8 11.4 %collective-permute-start.1 = (bf16[512,512]{1,0:T(8,128)(2,1)S(1)}, bf16[512,512]{1,0:T(8,128)(2,1)S(1)}, u32[]{:S(2)}, u32[]{:S(2)}) collective-permute-start(bf16[512,512]{1,0:T(8,128)(2,1)S(1)} %solve_part.3.own1), channel_id=1, source_target_pairs={{0,1},{1,0},{2,3},{3,2},{4,5},{5,4},{6,7},{7,6},{8,9},{9,8},{10,11... | collective-permute-start | bytes 1572872 | tf_op jit(solution)/shard_map/ppermute | solution.py:90
  29.2 1.9 %collective-permute-start.4 = (bf16[512,512]{1,0:T(8,128)(2,1)S(1)}, bf16[512,512]{1,0:T(8,128)(2,1)S(1)}, u32[]{:S(2)}, u32[]{:S(2)}) collective-permute-start(bf16[512,512]{1,0:T(8,128)(2,1)S(1)} %collective-permute-done.2.pair0), channel_id=1, source_target_pairs={{0,1},{1,0},{2,3},{3,2},{4,5},{5,4},{6,7},{7,6},{8,9},{9,8},{10,11... | collective-permute-start | bytes 1572872 | tf_op jit(solution)/shard_map/ppermute | solution.py:90
  29.2 2.7 %collective-permute-start.5 = (bf16[512,512]{1,0:T(8,128)(2,1)S(1)}, bf16[512,512]{1,0:T(8,128)(2,1)S(1)}, u32[]{:S(2)}, u32[]{:S(2)}) collective-permute-start(bf16[512,512]{1,0:T(8,128)(2,1)S(1)} %collective-permute-done.3.pair1), channel_id=1, source_target_pairs={{0,1},{1,0},{2,3},{3,2},{4,5},{5,4},{6,7},{7,6},{8,9},{9,8},{10,11... | collective-permute-start | bytes 1572872 | tf_op jit(solution)/shard_map/ppermute | solution.py:90
  29.7 3.0 %collective-permute-start.14 = (bf16[512,512]{1,0:T(8,128)(2,1)S(1)}, bf16[512,512]{1,0:T(8,128)(2,1)S(1)}, u32[]{:S(2)}, u32[]{:S(2)}) collective-permute-start(bf16[512,512]{1,0:T(8,128)(2,1)S(1)} %collective-permute-done.13.xa_ref), channel_id=1, source_target_pairs={{0,1},{1,0},{2,3},{3,2},{4,5},{5,4},{6,7},{7,6},{8,9},{9,8},{10,11... | collective-permute-start | bytes 1572872 | tf_op jit(solution)/shard_map/ppermute | solution.py:90
  29.8 8.2 %collective-permute-start.7 = (bf16[512,512]{1,0:T(8,128)(2,1)S(1)}, bf16[512,512]{1,0:T(8,128)(2,1)S(1)}, u32[]{:S(2)}, u32[]{:S(2)}) collective-permute-start(bf16[512,512]{1,0:T(8,128)(2,1)S(1)} %collective-permute-done.6.xa_ref), channel_id=1, source_target_pairs={{0,1},{1,0},{2,3},{3,2},{4,5},{5,4},{6,7},{7,6},{8,9},{9,8},{10,11... | collective-permute-start | bytes 1572872 | tf_op jit(solution)/shard_map/ppermute | solution.py:90
  30.2 10.4 %collective-permute-start.27 = (bf16[512,512]{1,0:T(8,128)(2,1)S(1)}, bf16[512,512]{1,0:T(8,128)(2,1)S(1)}, u32[]{:S(2)}, u32[]{:S(2)}) collective-permute-start(bf16[512,512]{1,0:T(8,128)(2,1)S(1)} %collective-permute-done.3.pair1), channel_id=1, source_target_pairs={{0,0},{8,16},{16,8},{24,24},{1,1},{9,17},{17,9},{25,25},{2,2},{10,... | collective-permute-start | bytes 1572872 | tf_op jit(solution)/shard_map/ppermute | solution.py:86
  31.1 9.9 %collective-permute-start.20 = (bf16[512,512]{1,0:T(8,128)(2,1)S(1)}, bf16[512,512]{1,0:T(8,128)(2,1)S(1)}, u32[]{:S(2)}, u32[]{:S(2)}) collective-permute-start(bf16[512,512]{1,0:T(8,128)(2,1)S(1)} %collective-permute-done.2.pair0), channel_id=1, source_target_pairs={{0,0},{8,16},{16,8},{24,24},{1,1},{9,17},{17,9},{25,25},{2,2},{10,... | collective-permute-start | bytes 1572872 | tf_op jit(solution)/shard_map/ppermute | solution.py:86
  34.8 9.2 %collective-permute-start.17 = (bf16[256,512]{1,0:T(8,128)(2,1)S(1)}, bf16[256,512]{1,0:T(8,128)(2,1)S(1)}, u32[]{:S(2)}, u32[]{:S(2)}) collective-permute-start(bf16[256,512]{1,0:T(8,128)(2,1)S(1)} %get-tuple-element.28), channel_id=1, source_target_pairs={{0,4},{1,5},{2,6},{3,7},{4,0},{5,1},{6,2},{7,3},{8,12},{9,13},{10,... | collective-permute-start | bytes 786440 | tf_op jit(solution)/shard_map/ppermute | solution.py:90
  36.5 9.2 %collective-permute-start.15 = (bf16[256,512]{1,0:T(8,128)(2,1)S(1)}, bf16[256,512]{1,0:T(8,128)(2,1)S(1)}, u32[]{:S(2)}, u32[]{:S(2)}) collective-permute-start(bf16[256,512]{1,0:T(8,128)(2,1)S(1)} %get-tuple-element.26), channel_id=1, source_target_pairs={{0,2},{1,3},{2,0},{3,1},{4,6},{5,7},{6,4},{7,5},{8,10},{9,11},{10,... | collective-permute-start | bytes 786440 | tf_op jit(solution)/shard_map/ppermute | solution.py:90
  40.1 8.7 %collective-permute-start.10 = (bf16[256,512]{1,0:T(8,128)(2,1)S(1)}, bf16[256,512]{1,0:T(8,128)(2,1)S(1)}, u32[]{:S(2)}, u32[]{:S(2)}) collective-permute-start(bf16[256,512]{1,0:T(8,128)(2,1)S(1)} %get-tuple-element.24), channel_id=1, source_target_pairs={{0,4},{1,5},{2,6},{3,7},{4,0},{5,1},{6,2},{7,3},{8,12},{9,13},{10,... | collective-permute-start | bytes 786440 | tf_op jit(solution)/shard_map/ppermute | solution.py:90
  40.6 10.7 %collective-permute-start.8 = (bf16[256,512]{1,0:T(8,128)(2,1)S(1)}, bf16[256,512]{1,0:T(8,128)(2,1)S(1)}, u32[]{:S(2)}, u32[]{:S(2)}) collective-permute-start(bf16[256,512]{1,0:T(8,128)(2,1)S(1)} %get-tuple-element.22), channel_id=1, source_target_pairs={{0,2},{1,3},{2,0},{3,1},{4,6},{5,7},{6,4},{7,5},{8,10},{9,11},{10,... | collective-permute-start | bytes 786440 | tf_op jit(solution)/shard_map/ppermute | solution.py:90
  41.0 13.1 %collective-permute-start.28 = (bf16[512,512]{1,0:T(8,128)(2,1)S(1)}, bf16[512,512]{1,0:T(8,128)(2,1)S(1)}, u32[]{:S(2)}, u32[]{:S(2)}) collective-permute-start(bf16[512,512]{1,0:T(8,128)(2,1)S(1)} %collective-permute-done.27.xa_ref), channel_id=1, source_target_pairs={{0,1},{1,0},{2,3},{3,2},{4,5},{5,4},{6,7},{7,6},{8,9},{9,8},{10,11... | collective-permute-start | bytes 1572872 | tf_op jit(solution)/shard_map/ppermute | solution.py:90
  44.0 32.1 %collective-permute-start.21 = (bf16[512,512]{1,0:T(8,128)(2,1)S(1)}, bf16[512,512]{1,0:T(8,128)(2,1)S(1)}, u32[]{:S(2)}, u32[]{:S(2)}) collective-permute-start(bf16[512,512]{1,0:T(8,128)(2,1)S(1)} %collective-permute-done.20.xa_ref), channel_id=1, source_target_pairs={{0,1},{1,0},{2,3},{3,2},{4,5},{5,4},{6,7},{7,6},{8,9},{9,8},{10,11... | collective-permute-start | bytes 1572872 | tf_op jit(solution)/shard_map/ppermute | solution.py:90
  45.7 8.0 %collective-permute-start.18 = (bf16[128,512]{1,0:T(8,128)(2,1)S(1)}, bf16[128,512]{1,0:T(8,128)(2,1)S(1)}, u32[]{:S(2)}, u32[]{:S(2)}) collective-permute-start(bf16[128,512]{1,0:T(8,128)(2,1)S(1)} %fusion.8), channel_id=1, source_target_pairs={{0,2},{1,3},{2,0},{3,1},{4,6},{5,7},{6,4},{7,5},{8,10},{9,11},{10,... | collective-permute-start | bytes 393224 | tf_op jit(solution)/shard_map/ppermute | solution.py:90
  48.8 51.7 %collective-permute-start.16 = (bf16[128,512]{1,0:T(8,128)(2,1)S(1)}, bf16[128,512]{1,0:T(8,128)(2,1)S(1)}, u32[]{:S(2)}, u32[]{:S(2)}) collective-permute-start(bf16[128,512]{1,0:T(8,128)(2,1)S(1)} %get-tuple-element.41), channel_id=1, source_target_pairs={{0,4},{1,5},{2,6},{3,7},{4,0},{5,1},{6,2},{7,3},{8,12},{9,13},{10,... | collective-permute-start | bytes 393224 | tf_op jit(solution)/shard_map/ppermute | solution.py:90
  51.3 23.2 %collective-permute-start.11 = (bf16[128,512]{1,0:T(8,128)(2,1)S(1)}, bf16[128,512]{1,0:T(8,128)(2,1)S(1)}, u32[]{:S(2)}, u32[]{:S(2)}) collective-permute-start(bf16[128,512]{1,0:T(8,128)(2,1)S(1)} %fusion.12), channel_id=1, source_target_pairs={{0,2},{1,3},{2,0},{3,1},{4,6},{5,7},{6,4},{7,5},{8,10},{9,11},{10,... | collective-permute-start | bytes 393224 | tf_op jit(solution)/shard_map/ppermute | solution.py:90
  53.7 48.6 %collective-permute-start.9 = (bf16[128,512]{1,0:T(8,128)(2,1)S(1)}, bf16[128,512]{1,0:T(8,128)(2,1)S(1)}, u32[]{:S(2)}, u32[]{:S(2)}) collective-permute-start(bf16[128,512]{1,0:T(8,128)(2,1)S(1)} %get-tuple-element.43), channel_id=1, source_target_pairs={{0,4},{1,5},{2,6},{3,7},{4,0},{5,1},{6,2},{7,3},{8,12},{9,13},{10,... | collective-permute-start | bytes 393224 | tf_op jit(solution)/shard_map/ppermute | solution.py:90
  54.1 49.1 %collective-permute-start.19 = (bf16[128,512]{1,0:T(8,128)(2,1)S(1)}, bf16[128,512]{1,0:T(8,128)(2,1)S(1)}, u32[]{:S(2)}, u32[]{:S(2)}) collective-permute-start(bf16[128,512]{1,0:T(8,128)(2,1)S(1)} %fusion.10), channel_id=1, source_target_pairs={{0,8},{8,0},{16,24},{24,16},{1,9},{9,1},{17,25},{25,17},{2,10},{10... | collective-permute-start | bytes 393224 | tf_op jit(solution)/shard_map/ppermute | solution.py:86
  74.5 7.3 %collective-permute-start.29 = (bf16[256,512]{1,0:T(8,128)(2,1)S(1)}, bf16[256,512]{1,0:T(8,128)(2,1)S(1)}, u32[]{:S(2)}, u32[]{:S(2)}) collective-permute-start(bf16[256,512]{1,0:T(8,128)(2,1)S(1)} %get-tuple-element.34), channel_id=1, source_target_pairs={{0,2},{1,3},{2,0},{3,1},{4,6},{5,7},{6,4},{7,5},{8,10},{9,11},{10,... | collective-permute-start | bytes 786440 | tf_op jit(solution)/shard_map/ppermute | solution.py:90
  76.1 7.3 %collective-permute-start.31 = (bf16[256,512]{1,0:T(8,128)(2,1)S(1)}, bf16[256,512]{1,0:T(8,128)(2,1)S(1)}, u32[]{:S(2)}, u32[]{:S(2)}) collective-permute-start(bf16[256,512]{1,0:T(8,128)(2,1)S(1)} %get-tuple-element.36), channel_id=1, source_target_pairs={{0,4},{1,5},{2,6},{3,7},{4,0},{5,1},{6,2},{7,3},{8,12},{9,13},{10,... | collective-permute-start | bytes 786440 | tf_op jit(solution)/shard_map/ppermute | solution.py:90
  81.8 6.6 %collective-permute-start.22 = (bf16[256,512]{1,0:T(8,128)(2,1)S(1)}, bf16[256,512]{1,0:T(8,128)(2,1)S(1)}, u32[]{:S(2)}, u32[]{:S(2)}) collective-permute-start(bf16[256,512]{1,0:T(8,128)(2,1)S(1)} %get-tuple-element.30), channel_id=1, source_target_pairs={{0,2},{1,3},{2,0},{3,1},{4,6},{5,7},{6,4},{7,5},{8,10},{9,11},{10,... | collective-permute-start | bytes 786440 | tf_op jit(solution)/shard_map/ppermute | solution.py:90
  83.5 6.4 %collective-permute-start.24 = (bf16[256,512]{1,0:T(8,128)(2,1)S(1)}, bf16[256,512]{1,0:T(8,128)(2,1)S(1)}, u32[]{:S(2)}, u32[]{:S(2)}) collective-permute-start(bf16[256,512]{1,0:T(8,128)(2,1)S(1)} %get-tuple-element.32), channel_id=1, source_target_pairs={{0,4},{1,5},{2,6},{3,7},{4,0},{5,1},{6,2},{7,3},{8,12},{9,13},{10,... | collective-permute-start | bytes 786440 | tf_op jit(solution)/shard_map/ppermute | solution.py:90
  88.4 15.8 %collective-permute-start.12 = (bf16[128,512]{1,0:T(8,128)(2,1)S(1)}, bf16[128,512]{1,0:T(8,128)(2,1)S(1)}, u32[]{:S(2)}, u32[]{:S(2)}) collective-permute-start(bf16[128,512]{1,0:T(8,128)(2,1)S(1)} %fusion.14), channel_id=1, source_target_pairs={{0,8},{8,0},{16,24},{24,16},{1,9},{9,1},{17,25},{25,17},{2,10},{10... | collective-permute-start | bytes 393224 | tf_op jit(solution)/shard_map/ppermute | solution.py:86
  88.5 20.1 %copy-start.1 = (f32[1,128,4096]{2,1,0:T(8,128)S(1)}, f32[1,128,4096]{2,1,0:T(8,128)}, u32[]{:S(2)}) copy-start(f32[1,128,4096]{2,1,0:T(8,128)} %param.8) | copy-start | bytes 6291460
  89.9 5.2 %collective-permute-start.32 = (bf16[128,512]{1,0:T(8,128)(2,1)S(1)}, bf16[128,512]{1,0:T(8,128)(2,1)S(1)}, u32[]{:S(2)}, u32[]{:S(2)}) collective-permute-start(bf16[128,512]{1,0:T(8,128)(2,1)S(1)} %fusion), channel_id=1, source_target_pairs={{0,2},{1,3},{2,0},{3,1},{4,6},{5,7},{6,4},{7,5},{8,10},{9,11},{10,... | collective-permute-start | bytes 393224 | tf_op jit(solution)/shard_map/ppermute | solution.py:90
  95.1 5.0 %collective-permute-start.25 = (bf16[128,512]{1,0:T(8,128)(2,1)S(1)}, bf16[128,512]{1,0:T(8,128)(2,1)S(1)}, u32[]{:S(2)}, u32[]{:S(2)}) collective-permute-start(bf16[128,512]{1,0:T(8,128)(2,1)S(1)} %fusion.4), channel_id=1, source_target_pairs={{0,2},{1,3},{2,0},{3,1},{4,6},{5,7},{6,4},{7,5},{8,10},{9,11},{10,... | collective-permute-start | bytes 393224 | tf_op jit(solution)/shard_map/ppermute | solution.py:90
  100.1 5.0 %collective-permute-start.30 = (bf16[128,512]{1,0:T(8,128)(2,1)S(1)}, bf16[128,512]{1,0:T(8,128)(2,1)S(1)}, u32[]{:S(2)}, u32[]{:S(2)}) collective-permute-start(bf16[128,512]{1,0:T(8,128)(2,1)S(1)} %get-tuple-element.37), channel_id=1, source_target_pairs={{0,4},{1,5},{2,6},{3,7},{4,0},{5,1},{6,2},{7,3},{8,12},{9,13},{10,... | collective-permute-start | bytes 393224 | tf_op jit(solution)/shard_map/ppermute | solution.py:90
  100.5 5.9 %collective-permute-start.23 = (bf16[128,512]{1,0:T(8,128)(2,1)S(1)}, bf16[128,512]{1,0:T(8,128)(2,1)S(1)}, u32[]{:S(2)}, u32[]{:S(2)}) collective-permute-start(bf16[128,512]{1,0:T(8,128)(2,1)S(1)} %get-tuple-element.39), channel_id=1, source_target_pairs={{0,4},{1,5},{2,6},{3,7},{4,0},{5,1},{6,2},{7,3},{8,12},{9,13},{10,... | collective-permute-start | bytes 393224 | tf_op jit(solution)/shard_map/ppermute | solution.py:90
  102.2 5.0 %collective-permute-start.33 = (bf16[128,512]{1,0:T(8,128)(2,1)S(1)}, bf16[128,512]{1,0:T(8,128)(2,1)S(1)}, u32[]{:S(2)}, u32[]{:S(2)}) collective-permute-start(bf16[128,512]{1,0:T(8,128)(2,1)S(1)} %fusion.2), channel_id=1, source_target_pairs={{0,8},{8,0},{16,24},{24,16},{1,9},{9,1},{17,25},{25,17},{2,10},{10... | collective-permute-start | bytes 393224 | tf_op jit(solution)/shard_map/ppermute | solution.py:86
  103.2 5.4 %collective-permute-start.26 = (bf16[128,512]{1,0:T(8,128)(2,1)S(1)}, bf16[128,512]{1,0:T(8,128)(2,1)S(1)}, u32[]{:S(2)}, u32[]{:S(2)}) collective-permute-start(bf16[128,512]{1,0:T(8,128)(2,1)S(1)} %fusion.6), channel_id=1, source_target_pairs={{0,8},{8,0},{16,24},{24,16},{1,9},{9,1},{17,25},{25,17},{2,10},{10... | collective-permute-start | bytes 393224 | tf_op jit(solution)/shard_map/ppermute | solution.py:86

commit v2 on v0

--- a/solution.py
+++ b/solution.py
@@ -1,7 +1,16 @@
+import functools
+
 import jax
 import jax.numpy as jnp
 from jax import lax
+from jax.experimental import pallas as pl
+from jax.experimental.pallas import tpu as pltpu
 from jax.sharding import PartitionSpec as P
+
+BF16 = jnp.bfloat16
+F32 = jnp.float32
+VMEM_LIMIT = 16 * 1024 * 1024
+HINT = pl.CostEstimate(flops=1, bytes_accessed=1, transcendentals=0)
 
 
 def solve_rows(blocks, factor_inverse):
@@ -29,7 +38,7 @@
     return selected.astype(jnp.float32)
 
 
-def body(panel_blocks, factor_inverse, target_rows, owner_order, ancestor_rows):
+def general_body(panel_blocks, factor_inverse, target_rows, owner_order, ancestor_rows):
     supernodes = panel_blocks.shape[0]
     panel_count = panel_blocks.shape[1]
     own_height = panel_blocks.shape[2]
@@ -67,7 +76,262 @@
     return ancestor_rows - summed
 
 
+PAIR = (1, 0, 3, 2)
+MIDDLE = (0, 2, 1, 3)
+CORE, X_HOP, Y_HOP = 1, 2, 4
+FIRST_HOP = (X_HOP, Y_HOP)
+SECOND_HOP = (Y_HOP, X_HOP)
+
+
+def row_swap(value, partner):
+    return lax.ppermute(value, "row", list(enumerate(partner)))
+
+
+def core_swap(value):
+    return lax.ppermute(value, "col", [(i, i ^ CORE) for i in range(lax.axis_size("col"))])
+
+
+def hop_swap(value, hops):
+    return lax.ppermute(value, "col", [(i, i ^ hops[i & CORE]) for i in range(lax.axis_size("col"))])
+
+
+def both_swap(value, partner, hops):
+    cols = lax.axis_size("col")
+    pairs = [(r * cols + c, partner[r] * cols + (c ^ hops[c & CORE])) for r in range(len(partner)) for c in range(cols)]
+    return lax.ppermute(value, ("row", "col"), pairs)
+
+
+def after(value, *others):
+    return lax.optimization_barrier((value, *others))[0]
+
+
+def dot_t(a, b):
+    return lax.dot_general(a, b, (((1,), (1,)), ((), ())), preferred_element_type=F32)
+
+
+def local_call(kernel, operands, shapes, name, scalars=0):
+    whole = pl.BlockSpec(memory_space=pltpu.VMEM)
+    return pl.pallas_call(
+        kernel,
+        in_specs=[pl.BlockSpec(memory_space=pltpu.SMEM)] * scalars + [whole] * (len(operands) - scalars),
+        out_specs=[whole] * len(shapes),
+        out_shape=[jax.ShapeDtypeStruct(shape, dtype) for shape, dtype in shapes],
+        cost_estimate=HINT,
+        compiler_params=pltpu.CompilerParams(vmem_limit_bytes=VMEM_LIMIT),
+        name=name,
+    )(*operands)
+
+
+def core_index():
+    return lax.axis_index("col") & CORE
+
+
+def aligned(start, unit):
+    return pl.ds(pl.multiple_of(start * unit, unit), unit)
+
+
+def solve_kernel(panel_ref, inverse_ref, mine_ref, give_ref, rest_ref):
+    half = give_ref.shape[0]
+    for part in range(2):
+        rows = pl.ds(part * half, half)
+        solved = dot_t(panel_ref[rows, :], inverse_ref[...]).astype(BF16)
+        mine_ref[rows, :] = solved
+
+        @pl.when(core_index() != part)
+        def _():
+            give_ref[...] = solved
+
+        @pl.when(core_index() == part)
+        def _():
+            rest_ref[...] = solved
+
+
+def join_kernel(rest_ref, got_ref, *outs):
+    width = rest_ref.shape[1]
+    core = core_index()
+    for out, first in zip(outs, (0, 0, outs[1].shape[0])):
+        rows = pl.ds(first, out.shape[0])
+        out[:, aligned(core, width)] = rest_ref[rows, :]
+        out[:, aligned(1 - core, width)] = got_ref[rows, :]
+
+
+def slot_masks():
+    core = core_index()
+    hop = jnp.where(core == 0, FIRST_HOP[0], FIRST_HOP[1])
+    next_hop = jnp.where(core == 0, SECOND_HOP[0], SECOND_HOP[1])
+    return [jnp.bitwise_xor(chip, side) for chip in (0, next_hop, hop, X_HOP | Y_HOP) for side in (0, CORE)]
+
+
+def pick_own_kernel(height, order_ref, mine_ref, got_ref, got_rest_ref, out_ref):
+    col, core = lax.axis_index("col"), core_index()
+    half, width = got_ref.shape
+    for place, mask in enumerate(slot_masks()):
+        start = order_ref[jnp.bitwise_xor(col, mask)] * height
+        rows = pl.ds(place * height, height)
+        out_ref[rows, aligned(core, width)] = mine_ref[pl.ds(pl.multiple_of(start, height), height), :]
+        inside = start // half == core
+        source = pl.ds(pl.multiple_of(start % half, height), height)
+
+        @pl.when(inside)
+        def _():
+            out_ref[rows, aligned(1 - core, width)] = got_ref[source, :]
+
+        @pl.when(jnp.logical_not(inside))
+        def _():
+            out_ref[rows, aligned(1 - core, width)] = got_rest_ref[source, :]
+
+
+def pick_pair_kernel(height, pieces, order_ref, *refs):
+    out_ref = refs[-1]
+    col, core = lax.axis_index("col"), core_index()
+    half = sum(ref.shape[0] for ref in refs[:pieces])
+    for place, mask in enumerate(slot_masks()):
+        start = order_ref[jnp.bitwise_xor(col, mask)] * height
+        rows = pl.ds(place * height, height)
+        inside = start // half == core
+        within = start % half
+        for number in range(2 * pieces):
+            ref = refs[number]
+            first = sum(r.shape[0] for r in refs[: number % pieces])
+            here = jnp.logical_and(within >= first, within < first + ref.shape[0])
+            wanted = inside if number < pieces else jnp.logical_not(inside)
+
+            @pl.when(jnp.logical_and(here, wanted))
+            def _():
+                out_ref[rows, :] = ref[pl.ds(pl.multiple_of(within - first, height), height), :]
+
+
+def product_kernel(count, *refs):
+    x_ref, keep_ref, send_ref = refs[count:]
+    for number, a_ref in enumerate(refs[:count]):
+        tile = a_ref.shape[0] // 2
+        rows = pl.ds(number * tile, tile)
+        keep_ref[rows, :] = dot_t(a_ref[:tile, :], x_ref[...])
+        send_ref[rows, :] = dot_t(a_ref[tile:, :], x_ref[...]).astype(BF16)
+
+
+def products(a, x):
+    shape = (sum(part.shape[0] for part in a) // 2, x.shape[0])
+    return local_call(functools.partial(product_kernel, len(a)), [*a, x], [(shape, F32), (shape, BF16)], "products")
+
+
+def own_second(keep, got):
+    total = keep + got.astype(F32)
+    half = total.shape[0] // 2
+    return total[:half], hop_swap(total[half:].astype(BF16), SECOND_HOP)
+
+
+def pair_second(keep, got):
+    total = (keep + got.astype(F32)).astype(BF16)
+    half = total.shape[0] // 2
+    return row_swap(total[:half], PAIR), both_swap(total[half:], PAIR, SECOND_HOP)
+
+
+def pack(terms, height):
+    return jnp.concatenate([term[height:].astype(BF16) for term in terms], axis=0)
+
+
+def finish_kernel(height, plan, anc_ref, *refs):
+    out_ref = refs[-1]
+    row, core = lax.axis_index("row"), core_index()
+    width = 4 * height
+    half = out_ref.shape[1] // 2
+    base = jnp.bitwise_or((row & 1) * 2, row >> 1)
+    for number, (which, first, count) in enumerate(plan):
+        *terms, other = refs[5 * number : 5 * number + 5]
+        for back in range(2):
+            at = jnp.bitwise_xor(base, which + 2 * back)
+            for block in range(count):
+                source = pl.ds(block * height, height)
+                for side in range(2):
+                    place = (core if side == 0 else 1 - core) * half + (first + block) * width + at * height
+                    place = pl.ds(pl.multiple_of(place, height), height)
+                    if side == 0:
+                        low, high = (terms[2 * back + k][:height, source] for k in range(2))
+                    else:
+                        low, high = (other[pl.ds((2 * back + k) * height, height), source] for k in range(2))
+                    out_ref[:, place] = anc_ref[:, place] - (low.astype(F32) + high.astype(F32))
+
+
+def paired_body(panel_blocks, factor_inverse, target_rows, owner_order, ancestor_rows):
+    _, panel_count, height, width = panel_blocks.shape
+    rows = panel_count * height
+    panel = panel_blocks.reshape(rows, width)
+    half = rows // 2
+    pieces = (half // 2, half // 2)
+
+    mine, give, rest = local_call(
+        solve_kernel, [panel, factor_inverse[0]], [((rows, width), BF16)] + [((half, width), BF16)] * 2, "solve"
+    )
+    got = core_swap(give)
+    got_rest = core_swap(rest)
+    joined, *parts = local_call(
+        join_kernel, [rest, got], [((count, 2 * width), BF16) for count in (half, *pieces)], "join"
+    )
+    first = row_swap(joined, MIDDLE)
+    pair = [row_swap(part, PAIR) for part in parts]
+    (a_own,) = local_call(
+        functools.partial(pick_own_kernel, height),
+        [owner_order, mine, got, got_rest],
+        [((rows, 2 * width), BF16)],
+        "pick_own",
+        scalars=1,
+    )
+    pair[0] = after(pair[0], a_own)
+    second = [row_swap(part, MIDDLE) for part in pair]
+    (a_pair,) = local_call(
+        functools.partial(pick_pair_kernel, height, len(pair)),
+        [owner_order, *pair, *[core_swap(part) for part in pair]],
+        [((rows, 2 * width), BF16)],
+        "pick_pair",
+        scalars=1,
+    )
+
+    own1, send = products([a_own], first)
+    own1_got = hop_swap(send, FIRST_HOP)
+    pair1, send = products([after(a_pair, own1)], first)
+    pair1_got = hop_swap(send, FIRST_HOP)
+    own1_terms = own_second(own1, after(own1_got, pair1))
+    keep2, send = products([a_own, a_pair], after(second[0], own1_terms[0]))
+    got2 = hop_swap(send, FIRST_HOP)
+    terms1 = (*own1_terms, *pair_second(pair1, after(pair1_got, keep2)))
+    keep3, send = products([a_own, a_pair], after(second[1], terms1[2]))
+    got3 = hop_swap(send, FIRST_HOP)
+    packed1 = pack((terms1[0], after(terms1[1], keep3), *terms1[2:]), height)
+    other1 = core_swap(packed1)
+    got2 = after(got2, packed1)
+    terms2 = (*own_second(keep2[:half], got2[:half]), *pair_second(keep2[half:], got2[half:]))
+    packed2 = pack(terms2, height)
+    other2 = core_swap(packed2)
+    got3 = after(got3, packed2)
+    terms3 = (*own_second(keep3[:half], got3[:half]), *pair_second(keep3[half:], got3[half:]))
+    other3 = core_swap(pack(terms3, height))
+    blocks = [count // height for count in pieces]
+    plan = ((0, 0, half // height), (1, 0, blocks[0]), (1, blocks[0], blocks[1]))
+    (result,) = local_call(
+        functools.partial(finish_kernel, height, plan),
+        [ancestor_rows[0], *terms1, other1, *terms2, other2, *terms3, other3],
+        [(ancestor_rows.shape[1:], F32)],
+        "finish",
+    )
+    return result[None]
+
+
 def solution(mesh):
+    def body(panel_blocks, factor_inverse, target_rows, owner_order, ancestor_rows):
+        supernodes, panel_count, height, _ = panel_blocks.shape
+        held = ancestor_rows.shape[0]
+        paired = (
+            mesh.shape["row"] == 4
+            and mesh.shape["col"] == 8
+            and panel_count == owner_order.shape[0] == 8
+            and supernodes == 1
+            and held == 1
+            and height % 128 == 0
+        )
+        chosen = paired_body if paired else general_body
+        return chosen(panel_blocks, factor_inverse, target_rows, owner_order, ancestor_rows)
+
     return jax.shard_map(
         body,
         mesh=mesh,

time: 242 us -> 93.7 us (0.39)
  waiting for transfers between devices: 174 us -> 51 us
  starting transfers between devices: 5.28 us -> 28.8 us
  matrix products: 22.3 us -> 0 us
  other arithmetic: 14.9 us -> 0.66 us
  between operations: 13.4 us -> 0.32 us
  Pallas kernels: 0 us -> 10.1 us
  local copies, waits for them, and re-layouts: 12.3 us -> 2.55 us
    all_to_all x1 -> x0, waiting for transfers between devices: 92.5 us -> none  [body(): lax.all_to_all(outgoing, 'col', split_axis=0, concat_axis=0, tiled=True)]
    all_gather x1 -> x0, waiting for transfers between devices: 81.2 us -> none  [body(): lax.all_gather(own_solved, 'row', axis=2, tiled=True)]
    ppermute x0 -> x25, waiting for transfers between devices: none -> 51 us  [the longest x8 30.1 us: row_swap(): return lax.ppermute(value, 'row', list(enumerate(partner)))]
    ppermute x0 -> x25, starting transfers between devices: none -> 28.8 us  [the longest x8 13.5 us: row_swap(): return lax.ppermute(value, 'row', list(enumerate(partner)))]
    dot_general x3 -> x0, matrix products: 22.3 us -> none  [the longest x1 10.3 us: body(): jnp.einsum('spiw,sqmw->spiqm', own_solved, lax.all_gather(own_solved, 'ro...]
    pallas_call x0 -> x9, Pallas kernels: none -> 10.1 us  [local_call(): pl.pallas_call(kernel, in_specs=[pl.BlockSpec(memory_space=pltpu.SMEM)] *...]
    convert_element_type x1, other arithmetic: 9.27 us -> 0.16 us  [pair_second(): total = (keep + got.astype(F32)).astype(BF16)]
    gather x1 -> x0, local copies, waits for them, and re-layouts: 8.05 us -> none  [pick_rows(): chosen = products[supernode_ids, position]]
  transfers between devices with their start and end apart: 2 -> 25, of which waited for: 2 -> 14; matrix products, arithmetic and copies ran while one was open for 2% -> 1% of each run, Pallas kernels for 0% -> 7%
where the time goes in v2:
time: 93.7 us; the launch traced here: 93.4 us
  waiting for transfers between devices  51 us (54%)
  starting transfers between devices  28.8 us (31%)
  Pallas kernels  10.1 us (11%)
  local copies, waits for them, and re-layouts  2.55 us (3%)
    ppermute x8, waiting for transfers between devices, row_swap(): return lax.ppermute(value, 'row', list(enumerate(partner)))  30.1 us
    ppermute x8, starting transfers between devices, row_swap(): return lax.ppermute(value, 'row', list(enumerate(partner)))  13.5 us
    ppermute x7, waiting for transfers between devices, hop_swap(): lax.ppermute(value, 'col', [(i, i ^ hops[i & CORE]) for i in range(lax.ax...  13 us
    pallas_call x9, Pallas kernels, local_call(): pl.pallas_call(kernel, in_specs=[pl.BlockSpec(memory_space=pltpu.SMEM)] *...  10.1 us
    ppermute x7, starting transfers between devices, hop_swap(): lax.ppermute(value, 'col', [(i, i ^ hops[i & CORE]) for i in range(lax.ax...  9.42 us
    ppermute x3, waiting for transfers between devices, both_swap(): return lax.ppermute(value, ('row', 'col'), pairs)  4.92 us
    ppermute x3, starting transfers between devices, both_swap(): return lax.ppermute(value, ('row', 'col'), pairs)  4.79 us
    ppermute x7, waiting for transfers between devices, core_swap(): lax.ppermute(value, 'col', [(i, i ^ CORE) for i in range(lax.axis_size('c...  3 us
  transfers between devices with their start and end apart: 25, of which 14 were waited for; matrix products, arithmetic and copies ran while one was open for 1% of the time, Pallas kernels for 7%

profile of v2, /device:TPU:0, one launch (start us, length us, event | category | flops | bytes accessed | tf_op | source)
XLA Modules:
  0.0 93.4 jit_solution(10776447636950590016)
XLA Ops:
  0.0 1.2 %copy-done.1 = bf16[1,8,128,512]{3,2,1,0:T(8,128)(2,1)S(1)} copy-done((bf16[1,8,128,512]{3,2,1,0:T(8,128)(2,1)S(1)}, bf16[1,8,128,512]{3,2,1,0:T(8,128)(2,1)}, u32[]{:S(2)}) %copy-start.1) | copy-done | bytes 1048600
  1.2 1.0 %copy-done.2 = bf16[1,512,512]{2,1,0:T(8,128)(2,1)S(1)} copy-done((bf16[1,512,512]{2,1,0:T(8,128)(2,1)S(1)}, bf16[1,512,512]{2,1,0:T(8,128)(2,1)}, u32[]{:S(2)}) %copy-start.2) | copy-done | bytes 524312
  2.3 1.0 %solve.1 = (bf16[1024,512]{1,0:T(8,128)(2,1)S(1)}, bf16[512,512]{1,0:T(8,128)(2,1)S(1)}, bf16[512,512]{1,0:T(8,128)(2,1)S(1)}) custom-call(bf16[1024,512]{1,0:T(8,128)(2,1)S(1)} %bitcast.5, bf16[512,512]{1,0:T(8,128)(2,1)S(1)} %bitcast.6), custom_call_target="tpu_custom_call" | custom-call | flops 1 | bytes 1 | tf_op jit(solution)/shard_map/solve/pallas_call | solution.py:114
  3.3 0.5 collective-permute-start
  3.8 1.5 %collective-permute-done.got_ref = bf16[512,512]{1,0:T(8,128)(2,1)S(1)} collective-permute-done((bf16[512,512]{1,0:T(8,128)(2,1)S(1)}, bf16[512,512]{1,0:T(8,128)(2,1)S(1)}, u32[]{:S(2)}, u32[]{:S(2)}) %collective-permute-start) | collective-permute-done | bytes 524320 | tf_op jit(solution)/shard_map/ppermute | solution.py:91
  5.3 0.2 join.1
  5.5 0.7 collective-permute-start.2
  6.2 0.4 collective-permute-start.1
  6.7 5.4 %collective-permute-start.4 = (bf16[256,1024]{1,0:T(8,128)(2,1)S(1)}, bf16[256,1024]{1,0:T(8,128)(2,1)S(1)}, u32[]{:S(2)}, u32[]{:S(2)}) collective-permute-start(bf16[256,1024]{1,0:T(8,128)(2,1)S(1)} %get-tuple-element.34), channel_id=1, source_target_pairs={{0,8},{8,0},{16,24},{24,16},{1,9},{9,1},{17,25},{25,17},{2,10},{10... | collective-permute-start | bytes 1572872 | tf_op jit(solution)/shard_map/ppermute | solution.py:87
  12.1 0.1 collective-permute-start.5
  12.2 0.8 pick_own.1.refs_0_
  13.0 11.9 %collective-permute-done.4.refs_0_ = bf16[256,1024]{1,0:T(8,128)(2,1)S(1)} collective-permute-done((bf16[256,1024]{1,0:T(8,128)(2,1)S(1)}, bf16[256,1024]{1,0:T(8,128)(2,1)S(1)}, u32[]{:S(2)}, u32[]{:S(2)}) %collective-permute-start.4) | collective-permute-done | bytes 524320 | tf_op jit(solution)/shard_map/ppermute | solution.py:87
  24.9 11.0 %collective-permute-done.5.refs_1_ = bf16[256,1024]{1,0:T(8,128)(2,1)S(1)} collective-permute-done((bf16[256,1024]{1,0:T(8,128)(2,1)S(1)}, bf16[256,1024]{1,0:T(8,128)(2,1)S(1)}, u32[]{:S(2)}, u32[]{:S(2)}) %collective-permute-start.5) | collective-permute-done | bytes 524320 | tf_op jit(solution)/shard_map/ppermute | solution.py:87
  35.8 1.3 %products.4 = (f32[512,512]{1,0:T(8,128)S(1)}, bf16[512,512]{1,0:T(8,128)(2,1)S(1)}) custom-call(bf16[1024,1024]{1,0:T(8,128)(2,1)S(1)} %pick_own.1.refs_0_, bf16[512,1024]{1,0:T(8,128)(2,1)S(1)} %collective-permute-done.2.refs_1_), custom_call_target="tpu_custom_call" | custom-call | flops 1 | bytes 1 | tf_op jit(solution)/shard_map/products/pallas_call | solution.py:114
  37.1 1.6 %collective-permute-start.3 = (bf16[512,512]{1,0:T(8,128)(2,1)S(1)}, bf16[512,512]{1,0:T(8,128)(2,1)S(1)}, u32[]{:S(2)}, u32[]{:S(2)}) collective-permute-start(bf16[512,512]{1,0:T(8,128)(2,1)S(1)} %get-tuple-element.33), channel_id=1, source_target_pairs={{0,2},{1,5},{2,0},{3,7},{4,6},{5,1},{6,4},{7,3},{8,10},{9,13},{10,... | collective-permute-start | bytes 1572872 | tf_op jit(solution)/shard_map/ppermute | solution.py:95
  38.7 0.7 collective-permute-start.10
  39.4 0.9 %pick_pair.1.refs_0_.refs_1_ = bf16[1024,1024]{1,0:T(8,128)(2,1)S(1)} custom-call(s32[8]{0:T(128)S(1)} %copy-done.3, bf16[256,1024]{1,0:T(8,128)(2,1)S(1)} %collective-permute-done.4.refs_0_, bf16[256,1024]{1,0:T(8,128)(2,1)S(1)} %collective-permute-done.5.refs_1_, bf16[256,1024]{1,0:T(8,128)(2,1)S(1)} %collective-permute-done.6.refs_2_, ...), custom_call_target="tpu_custom_call" | custom-call | flops 1 | bytes 1 | tf_op jit(solution)/shard_map/pick_pair/pallas_call | solution.py:114
  40.4 1.3 %products.5 = (f32[512,512]{1,0:T(8,128)S(1)}, bf16[512,512]{1,0:T(8,128)(2,1)S(1)}) custom-call(bf16[1024,1024]{1,0:T(8,128)(2,1)S(1)} %pick_pair.1.refs_0_.refs_1_, bf16[512,1024]{1,0:T(8,128)(2,1)S(1)} %collective-permute-done.2.refs_1_), custom_call_target="tpu_custom_call" | custom-call | flops 1 | bytes 1 | tf_op jit(solution)/shard_map/products/pallas_call | solution.py:114
  41.6 0.6 collective-permute-start.9
  42.3 0.7 collective-permute-start.13
  42.9 3.4 %collective-permute-done.3 = bf16[512,512]{1,0:T(8,128)(2,1)S(1)} collective-permute-done((bf16[512,512]{1,0:T(8,128)(2,1)S(1)}, bf16[512,512]{1,0:T(8,128)(2,1)S(1)}, u32[]{:S(2)}, u32[]{:S(2)}) %collective-permute-start.3) | collective-permute-done | bytes 524320 | tf_op jit(solution)/shard_map/ppermute | solution.py:95
  46.4 0.2 fusion.2
  46.6 1.3 %products.6 = (f32[1024,256]{1,0:T(8,128)S(1)}, bf16[1024,256]{1,0:T(8,128)(2,1)S(1)}) custom-call(bf16[1024,1024]{1,0:T(8,128)(2,1)S(1)} %pick_own.1.refs_0_, bf16[1024,1024]{1,0:T(8,128)(2,1)S(1)} %pick_pair.1.refs_0_.refs_1_, bf16[256,1024]{1,0:T(8,128)(2,1)S(1)} %collective-permute-done.10.refs_2_), custom_call_target="tpu_custom_call" | custom-call | flops 1 | bytes 1 | tf_op jit(solution)/shard_map/products/pallas_call | solution.py:114
  47.9 4.1 %collective-permute-done.9 = bf16[512,512]{1,0:T(8,128)(2,1)S(1)} collective-permute-done((bf16[512,512]{1,0:T(8,128)(2,1)S(1)}, bf16[512,512]{1,0:T(8,128)(2,1)S(1)}, u32[]{:S(2)}, u32[]{:S(2)}) %collective-permute-start.9) | collective-permute-done | bytes 524320 | tf_op jit(solution)/shard_map/ppermute | solution.py:95
  52.0 0.2 add_convert_fusion
  52.2 1.6 %collective-permute-start.15 = (bf16[1024,256]{1,0:T(8,128)(2,1)S(1)}, bf16[1024,256]{1,0:T(8,128)(2,1)S(1)}, u32[]{:S(2)}, u32[]{:S(2)}) collective-permute-start(bf16[1024,256]{1,0:T(8,128)(2,1)S(1)} %get-tuple-element.47), channel_id=1, source_target_pairs={{0,2},{1,5},{2,0},{3,7},{4,6},{5,1},{6,4},{7,3},{8,10},{9,13},{10,... | collective-permute-start | bytes 1572872 | tf_op jit(solution)/shard_map/ppermute | solution.py:95
  53.8 5.3 %collective-permute-start.11 = (bf16[256,512]{1,0:T(8,128)(2,1)S(1)}, bf16[256,512]{1,0:T(8,128)(2,1)S(1)}, u32[]{:S(2)}, u32[]{:S(2)}) collective-permute-start(bf16[256,512]{1,0:T(8,128)(2,1)S(1)} %get-tuple-element.60), channel_id=1, source_target_pairs={{0,8},{8,0},{16,24},{24,16},{1,9},{9,1},{17,25},{25,17},{2,10},{10... | collective-permute-start | bytes 786440 | tf_op jit(solution)/shard_map/ppermute | solution.py:87
  59.1 1.8 %collective-permute-start.8 = (bf16[256,512]{1,0:T(8,128)(2,1)S(1)}, bf16[256,512]{1,0:T(8,128)(2,1)S(1)}, u32[]{:S(2)}, u32[]{:S(2)}) collective-permute-start(bf16[256,512]{1,0:T(8,128)(2,1)S(1)} %slice.138), channel_id=1, source_target_pairs={{0,4},{1,3},{2,6},{3,1},{4,0},{5,7},{6,2},{7,5},{8,12},{9,11},{10,... | collective-permute-start | bytes 786440 | tf_op jit(solution)/shard_map/ppermute | solution.py:95
  60.9 5.4 %collective-permute-done.11.refs_2_ = bf16[256,512]{1,0:T(8,128)(2,1)S(1)} collective-permute-done((bf16[256,512]{1,0:T(8,128)(2,1)S(1)}, bf16[256,512]{1,0:T(8,128)(2,1)S(1)}, u32[]{:S(2)}, u32[]{:S(2)}) %collective-permute-start.11) | collective-permute-done | bytes 262176 | tf_op jit(solution)/shard_map/ppermute | solution.py:87
  66.3 1.3 %products.7 = (f32[1024,256]{1,0:T(8,128)S(1)}, bf16[1024,256]{1,0:T(8,128)(2,1)S(1)}) custom-call(bf16[1024,1024]{1,0:T(8,128)(2,1)S(1)} %pick_own.1.refs_0_, bf16[1024,1024]{1,0:T(8,128)(2,1)S(1)} %pick_pair.1.refs_0_.refs_1_, bf16[256,1024]{1,0:T(8,128)(2,1)S(1)} %collective-permute-done.13.refs_2_), custom_call_target="tpu_custom_call" | custom-call | flops 1 | bytes 1 | tf_op jit(solution)/shard_map/products/pallas_call | solution.py:114
  67.6 1.8 %collective-permute-start.20 = (bf16[1024,256]{1,0:T(8,128)(2,1)S(1)}, bf16[1024,256]{1,0:T(8,128)(2,1)S(1)}, u32[]{:S(2)}, u32[]{:S(2)}) collective-permute-start(bf16[1024,256]{1,0:T(8,128)(2,1)S(1)} %get-tuple-element.49), channel_id=1, source_target_pairs={{0,2},{1,5},{2,0},{3,7},{4,6},{5,1},{6,4},{7,3},{8,10},{9,13},{10,... | collective-permute-start | bytes 1572872 | tf_op jit(solution)/shard_map/ppermute | solution.py:95
  69.4 1.5 %collective-permute-done.12.refs_3_ = bf16[256,512]{1,0:T(8,128)(2,1)S(1)} collective-permute-done((bf16[256,512]{1,0:T(8,128)(2,1)S(1)}, bf16[256,512]{1,0:T(8,128)(2,1)S(1)}, u32[]{:S(2)}, u32[]{:S(2)}) %collective-permute-start.12) | collective-permute-done | bytes 262176 | tf_op jit(solution)/shard_map/ppermute | solution.py:101
  70.9 0.1 fusion.1
  71.1 0.4 collective-permute-start.16
  71.5 3.0 %collective-permute-start.18 = (bf16[256,256]{1,0:T(8,128)(2,1)S(1)}, bf16[256,256]{1,0:T(8,128)(2,1)S(1)}, u32[]{:S(2)}, u32[]{:S(2)}) collective-permute-start(bf16[256,256]{1,0:T(8,128)(2,1)S(1)} %get-tuple-element.63), channel_id=1, source_target_pairs={{0,12},{1,11},{2,14},{3,9},{4,8},{5,15},{6,10},{7,13},{8,4},{9,3},... | collective-permute-start | bytes 393224 | tf_op jit(solution)/shard_map/ppermute | solution.py:101
  74.4 0.3 collective-permute-start.17
  74.7 4.3 %collective-permute-done.16.refs_6_ = bf16[256,256]{1,0:T(8,128)(2,1)S(1)} collective-permute-done((bf16[256,256]{1,0:T(8,128)(2,1)S(1)}, bf16[256,256]{1,0:T(8,128)(2,1)S(1)}, u32[]{:S(2)}, u32[]{:S(2)}) %collective-permute-start.16) | collective-permute-done | bytes 131104 | tf_op jit(solution)/shard_map/ppermute | solution.py:95
  79.0 0.4 collective-permute-done.17.refs_7_
  79.4 0.2 collective-permute-done.20
  79.7 0.1 fusion
  79.8 1.8 %collective-permute-start.21 = (bf16[256,256]{1,0:T(8,128)(2,1)S(1)}, bf16[256,256]{1,0:T(8,128)(2,1)S(1)}, u32[]{:S(2)}, u32[]{:S(2)}) collective-permute-start(bf16[256,256]{1,0:T(8,128)(2,1)S(1)} %slice.153), channel_id=1, source_target_pairs={{0,4},{1,3},{2,6},{3,1},{4,0},{5,7},{6,2},{7,5},{8,12},{9,11},{10,... | collective-permute-start | bytes 393224 | tf_op jit(solution)/shard_map/ppermute | solution.py:95
  81.6 1.8 %collective-permute-start.23 = (bf16[256,256]{1,0:T(8,128)(2,1)S(1)}, bf16[256,256]{1,0:T(8,128)(2,1)S(1)}, u32[]{:S(2)}, u32[]{:S(2)}) collective-permute-start(bf16[256,256]{1,0:T(8,128)(2,1)S(1)} %get-tuple-element.61), channel_id=1, source_target_pairs={{0,12},{1,11},{2,14},{3,9},{4,8},{5,15},{6,10},{7,13},{8,4},{9,3},... | collective-permute-start | bytes 393224 | tf_op jit(solution)/shard_map/ppermute | solution.py:101
  83.4 0.3 collective-permute-start.22
  83.8 1.0 %collective-permute-done.21.refs_11_ = bf16[256,256]{1,0:T(8,128)(2,1)S(1)} collective-permute-done((bf16[256,256]{1,0:T(8,128)(2,1)S(1)}, bf16[256,256]{1,0:T(8,128)(2,1)S(1)}, u32[]{:S(2)}, u32[]{:S(2)}) %collective-permute-start.21) | collective-permute-done | bytes 131104 | tf_op jit(solution)/shard_map/ppermute | solution.py:95
  84.9 3.4 %collective-permute-done.23.refs_13_ = bf16[256,256]{1,0:T(8,128)(2,1)S(1)} collective-permute-done((bf16[256,256]{1,0:T(8,128)(2,1)S(1)}, bf16[256,256]{1,0:T(8,128)(2,1)S(1)}, u32[]{:S(2)}, u32[]{:S(2)}) %collective-permute-start.23) | collective-permute-done | bytes 131104 | tf_op jit(solution)/shard_map/ppermute | solution.py:101
  88.3 1.4 %collective-permute-done.22.refs_12_ = bf16[256,256]{1,0:T(8,128)(2,1)S(1)} collective-permute-done((bf16[256,256]{1,0:T(8,128)(2,1)S(1)}, bf16[256,256]{1,0:T(8,128)(2,1)S(1)}, u32[]{:S(2)}, u32[]{:S(2)}) %collective-permute-start.22) | collective-permute-done | bytes 131104 | tf_op jit(solution)/shard_map/ppermute | solution.py:87
  89.9 1.4 %collective-permute-done.24.refs_14_ = bf16[512,256]{1,0:T(8,128)(2,1)S(1)} collective-permute-done((bf16[512,256]{1,0:T(8,128)(2,1)S(1)}, bf16[512,256]{1,0:T(8,128)(2,1)S(1)}, u32[]{:S(2)}, u32[]{:S(2)}) %collective-permute-start.24) | collective-permute-done | bytes 262176 | tf_op jit(solution)/shard_map/ppermute | solution.py:91
  91.4 2.1 %finish.1 = f32[128,4096]{1,0:T(8,128)} custom-call(f32[128,4096]{1,0:T(8,128)S(1)} %bitcast.4, f32[256,512]{1,0:T(8,128)S(1)} %slice.137.refs_0_, bf16[256,512]{1,0:T(8,128)(2,1)S(1)} %collective-permute-done.8.refs_1_, bf16[256,512]{1,0:T(8,128)(2,1)S(1)} %collective-permute-done.11.refs_2_, bf16[256,512]{1,0:T(8,128)(2,1)S(1)} %collective-permute-done.12.refs_3_, ...), custom_call_target="tpu_custom_call" | custom-call | flops 1 | bytes 1 | tf_op jit(solution)/shard_map/finish/pallas_call | solution.py:114
  (47 shorter events, 0.5 us)
Async XLA Ops:
  0.0 12.2 %copy-start.3 = (s32[8]{0:T(128)S(1)}, s32[8]{0:T(128)}, u32[]{:S(2)}) copy-start(s32[8]{0:T(128)} %order_ref.3) | copy-start | bytes 100
  0.0 1.2 %copy-start.1 = (bf16[1,8,128,512]{3,2,1,0:T(8,128)(2,1)S(1)}, bf16[1,8,128,512]{3,2,1,0:T(8,128)(2,1)}, u32[]{:S(2)}) copy-start(bf16[1,8,128,512]{3,2,1,0:T(8,128)(2,1)} %param.5) | copy-start | bytes 3145732
  1.2 1.0 %copy-start.2 = (bf16[1,512,512]{2,1,0:T(8,128)(2,1)S(1)}, bf16[1,512,512]{2,1,0:T(8,128)(2,1)}, u32[]{:S(2)}) copy-start(bf16[1,512,512]{2,1,0:T(8,128)(2,1)} %param.6) | copy-start | bytes 1572868
  3.3 2.1 %collective-permute-start = (bf16[512,512]{1,0:T(8,128)(2,1)S(1)}, bf16[512,512]{1,0:T(8,128)(2,1)S(1)}, u32[]{:S(2)}, u32[]{:S(2)}) collective-permute-start(bf16[512,512]{1,0:T(8,128)(2,1)S(1)} %get-tuple-element.29), channel_id=1, source_target_pairs={{0,1},{1,0},{2,3},{3,2},{4,5},{5,4},{6,7},{7,6},{8,9},{9,8},{10,11... | collective-permute-start | bytes 1572872 | tf_op jit(solution)/shard_map/ppermute | solution.py:91
  5.5 30.3 %collective-permute-start.2 = (bf16[512,1024]{1,0:T(8,128)(2,1)S(1)}, bf16[512,1024]{1,0:T(8,128)(2,1)S(1)}, u32[]{:S(2)}, u32[]{:S(2)}) collective-permute-start(bf16[512,1024]{1,0:T(8,128)(2,1)S(1)} %get-tuple-element.31), channel_id=1, source_target_pairs={{0,0},{8,16},{16,8},{24,24},{1,1},{9,17},{17,9},{25,25},{2,2},{10,... | collective-permute-start | bytes 3145736 | tf_op jit(solution)/shard_map/ppermute | solution.py:87
  6.2 6.0 %collective-permute-start.1 = (bf16[512,512]{1,0:T(8,128)(2,1)S(1)}, bf16[512,512]{1,0:T(8,128)(2,1)S(1)}, u32[]{:S(2)}, u32[]{:S(2)}) collective-permute-start(bf16[512,512]{1,0:T(8,128)(2,1)S(1)} %get-tuple-element.30.rest_ref), channel_id=1, source_target_pairs={{0,1},{1,0},{2,3},{3,2},{4,5},{5,4},{6,7},{7,6},{8,9},{9,8},{10,11... | collective-permute-start | bytes 1572872 | tf_op jit(solution)/shard_map/ppermute | solution.py:91
  6.7 18.2 %collective-permute-start.4 = (bf16[256,1024]{1,0:T(8,128)(2,1)S(1)}, bf16[256,1024]{1,0:T(8,128)(2,1)S(1)}, u32[]{:S(2)}, u32[]{:S(2)}) collective-permute-start(bf16[256,1024]{1,0:T(8,128)(2,1)S(1)} %get-tuple-element.34), channel_id=1, source_target_pairs={{0,8},{8,0},{16,24},{24,16},{1,9},{9,1},{17,25},{25,17},{2,10},{10... | collective-permute-start | bytes 1572872 | tf_op jit(solution)/shard_map/ppermute | solution.py:87
  12.1 23.8 %collective-permute-start.5 = (bf16[256,1024]{1,0:T(8,128)(2,1)S(1)}, bf16[256,1024]{1,0:T(8,128)(2,1)S(1)}, u32[]{:S(2)}, u32[]{:S(2)}) collective-permute-start(bf16[256,1024]{1,0:T(8,128)(2,1)S(1)} %get-tuple-element.36), channel_id=1, source_target_pairs={{0,8},{8,0},{16,24},{24,16},{1,9},{9,1},{17,25},{25,17},{2,10},{10... | collective-permute-start | bytes 1572872 | tf_op jit(solution)/shard_map/ppermute | solution.py:87
  24.9 14.5 %collective-permute-start.6 = (bf16[256,1024]{1,0:T(8,128)(2,1)S(1)}, bf16[256,1024]{1,0:T(8,128)(2,1)S(1)}, u32[]{:S(2)}, u32[]{:S(2)}) collective-permute-start(bf16[256,1024]{1,0:T(8,128)(2,1)S(1)} %collective-permute-done.4.refs_0_), channel_id=1, source_target_pairs={{0,1},{1,0},{2,3},{3,2},{4,5},{5,4},{6,7},{7,6},{8,9},{9,8},{10,11... | collective-permute-start | bytes 1572872 | tf_op jit(solution)/shard_map/ppermute | solution.py:91
  35.8 3.6 %collective-permute-start.7 = (bf16[256,1024]{1,0:T(8,128)(2,1)S(1)}, bf16[256,1024]{1,0:T(8,128)(2,1)S(1)}, u32[]{:S(2)}, u32[]{:S(2)}) collective-permute-start(bf16[256,1024]{1,0:T(8,128)(2,1)S(1)} %collective-permute-done.5.refs_1_), channel_id=1, source_target_pairs={{0,1},{1,0},{2,3},{3,2},{4,5},{5,4},{6,7},{7,6},{8,9},{9,8},{10,11... | collective-permute-start | bytes 1572872 | tf_op jit(solution)/shard_map/ppermute | solution.py:91
  37.1 9.2 %collective-permute-start.3 = (bf16[512,512]{1,0:T(8,128)(2,1)S(1)}, bf16[512,512]{1,0:T(8,128)(2,1)S(1)}, u32[]{:S(2)}, u32[]{:S(2)}) collective-permute-start(bf16[512,512]{1,0:T(8,128)(2,1)S(1)} %get-tuple-element.33), channel_id=1, source_target_pairs={{0,2},{1,5},{2,0},{3,7},{4,6},{5,1},{6,4},{7,3},{8,10},{9,13},{10,... | collective-permute-start | bytes 1572872 | tf_op jit(solution)/shard_map/ppermute | solution.py:95
  38.7 7.9 %collective-permute-start.10 = (bf16[256,1024]{1,0:T(8,128)(2,1)S(1)}, bf16[256,1024]{1,0:T(8,128)(2,1)S(1)}, u32[]{:S(2)}, u32[]{:S(2)}) collective-permute-start(bf16[256,1024]{1,0:T(8,128)(2,1)S(1)} %collective-permute-done.4.refs_0_), channel_id=1, source_target_pairs={{0,0},{8,16},{16,8},{24,24},{1,1},{9,17},{17,9},{25,25},{2,2},{10,... | collective-permute-start | bytes 1572872 | tf_op jit(solution)/shard_map/ppermute | solution.py:87
  41.6 10.4 %collective-permute-start.9 = (bf16[512,512]{1,0:T(8,128)(2,1)S(1)}, bf16[512,512]{1,0:T(8,128)(2,1)S(1)}, u32[]{:S(2)}, u32[]{:S(2)}) collective-permute-start(bf16[512,512]{1,0:T(8,128)(2,1)S(1)} %get-tuple-element.40), channel_id=1, source_target_pairs={{0,2},{1,5},{2,0},{3,7},{4,6},{5,1},{6,4},{7,3},{8,10},{9,13},{10,... | collective-permute-start | bytes 1572872 | tf_op jit(solution)/shard_map/ppermute | solution.py:95
  42.3 18.6 %collective-permute-start.13 = (bf16[256,1024]{1,0:T(8,128)(2,1)S(1)}, bf16[256,1024]{1,0:T(8,128)(2,1)S(1)}, u32[]{:S(2)}, u32[]{:S(2)}) collective-permute-start(bf16[256,1024]{1,0:T(8,128)(2,1)S(1)} %collective-permute-done.5.refs_1_), channel_id=1, source_target_pairs={{0,0},{8,16},{16,8},{24,24},{1,1},{9,17},{17,9},{25,25},{2,2},{10,... | collective-permute-start | bytes 1572872 | tf_op jit(solution)/shard_map/ppermute | solution.py:87
  52.2 18.8 %collective-permute-start.15 = (bf16[1024,256]{1,0:T(8,128)(2,1)S(1)}, bf16[1024,256]{1,0:T(8,128)(2,1)S(1)}, u32[]{:S(2)}, u32[]{:S(2)}) collective-permute-start(bf16[1024,256]{1,0:T(8,128)(2,1)S(1)} %get-tuple-element.47), channel_id=1, source_target_pairs={{0,2},{1,5},{2,0},{3,7},{4,6},{5,1},{6,4},{7,3},{8,10},{9,13},{10,... | collective-permute-start | bytes 1572872 | tf_op jit(solution)/shard_map/ppermute | solution.py:95
  53.8 12.5 %collective-permute-start.11 = (bf16[256,512]{1,0:T(8,128)(2,1)S(1)}, bf16[256,512]{1,0:T(8,128)(2,1)S(1)}, u32[]{:S(2)}, u32[]{:S(2)}) collective-permute-start(bf16[256,512]{1,0:T(8,128)(2,1)S(1)} %get-tuple-element.60), channel_id=1, source_target_pairs={{0,8},{8,0},{16,24},{24,16},{1,9},{9,1},{17,25},{25,17},{2,10},{10... | collective-permute-start | bytes 786440 | tf_op jit(solution)/shard_map/ppermute | solution.py:87
  59.1 8.5 %collective-permute-start.8 = (bf16[256,512]{1,0:T(8,128)(2,1)S(1)}, bf16[256,512]{1,0:T(8,128)(2,1)S(1)}, u32[]{:S(2)}, u32[]{:S(2)}) collective-permute-start(bf16[256,512]{1,0:T(8,128)(2,1)S(1)} %slice.138), channel_id=1, source_target_pairs={{0,4},{1,3},{2,6},{3,1},{4,0},{5,7},{6,2},{7,5},{8,12},{9,11},{10,... | collective-permute-start | bytes 786440 | tf_op jit(solution)/shard_map/ppermute | solution.py:95
  60.9 10.0 %collective-permute-start.12 = (bf16[256,512]{1,0:T(8,128)(2,1)S(1)}, bf16[256,512]{1,0:T(8,128)(2,1)S(1)}, u32[]{:S(2)}, u32[]{:S(2)}) collective-permute-start(bf16[256,512]{1,0:T(8,128)(2,1)S(1)} %get-tuple-element.59), channel_id=1, source_target_pairs={{0,12},{1,11},{2,14},{3,9},{4,8},{5,15},{6,10},{7,13},{8,4},{9,3},... | collective-permute-start | bytes 786440 | tf_op jit(solution)/shard_map/ppermute | solution.py:101
  67.6 12.1 %collective-permute-start.20 = (bf16[1024,256]{1,0:T(8,128)(2,1)S(1)}, bf16[1024,256]{1,0:T(8,128)(2,1)S(1)}, u32[]{:S(2)}, u32[]{:S(2)}) collective-permute-start(bf16[1024,256]{1,0:T(8,128)(2,1)S(1)} %get-tuple-element.49), channel_id=1, source_target_pairs={{0,2},{1,5},{2,0},{3,7},{4,6},{5,1},{6,4},{7,3},{8,10},{9,13},{10,... | collective-permute-start | bytes 1572872 | tf_op jit(solution)/shard_map/ppermute | solution.py:95
  71.1 7.9 %collective-permute-start.16 = (bf16[256,256]{1,0:T(8,128)(2,1)S(1)}, bf16[256,256]{1,0:T(8,128)(2,1)S(1)}, u32[]{:S(2)}, u32[]{:S(2)}) collective-permute-start(bf16[256,256]{1,0:T(8,128)(2,1)S(1)} %slice.145), channel_id=1, source_target_pairs={{0,4},{1,3},{2,6},{3,1},{4,0},{5,7},{6,2},{7,5},{8,12},{9,11},{10,... | collective-permute-start | bytes 393224 | tf_op jit(solution)/shard_map/ppermute | solution.py:95
  71.5 7.5 %collective-permute-start.18 = (bf16[256,256]{1,0:T(8,128)(2,1)S(1)}, bf16[256,256]{1,0:T(8,128)(2,1)S(1)}, u32[]{:S(2)}, u32[]{:S(2)}) collective-permute-start(bf16[256,256]{1,0:T(8,128)(2,1)S(1)} %get-tuple-element.63), channel_id=1, source_target_pairs={{0,12},{1,11},{2,14},{3,9},{4,8},{5,15},{6,10},{7,13},{8,4},{9,3},... | collective-permute-start | bytes 393224 | tf_op jit(solution)/shard_map/ppermute | solution.py:101
  74.4 5.0 %collective-permute-start.17 = (bf16[256,256]{1,0:T(8,128)(2,1)S(1)}, bf16[256,256]{1,0:T(8,128)(2,1)S(1)}, u32[]{:S(2)}, u32[]{:S(2)}) collective-permute-start(bf16[256,256]{1,0:T(8,128)(2,1)S(1)} %get-tuple-element.64), channel_id=1, source_target_pairs={{0,8},{8,0},{16,24},{24,16},{1,9},{9,1},{17,25},{25,17},{2,10},{10... | collective-permute-start | bytes 393224 | tf_op jit(solution)/shard_map/ppermute | solution.py:87
  74.7 15.2 %collective-permute-start.14 = (bf16[512,512]{1,0:T(8,128)(2,1)S(1)}, bf16[512,512]{1,0:T(8,128)(2,1)S(1)}, u32[]{:S(2)}, u32[]{:S(2)}) collective-permute-start(bf16[512,512]{1,0:T(8,128)(2,1)S(1)} %pad_maximum_fusion), channel_id=1, source_target_pairs={{0,1},{1,0},{2,3},{3,2},{4,5},{5,4},{6,7},{7,6},{8,9},{9,8},{10,11... | collective-permute-start | bytes 1572872 | tf_op jit(solution)/shard_map/ppermute | solution.py:91
  79.8 11.6 %copy-start = (f32[1,128,4096]{2,1,0:T(8,128)S(1)}, f32[1,128,4096]{2,1,0:T(8,128)}, u32[]{:S(2)}) copy-start(f32[1,128,4096]{2,1,0:T(8,128)} %param.8) | copy-start | bytes 6291460
  79.8 5.0 %collective-permute-start.21 = (bf16[256,256]{1,0:T(8,128)(2,1)S(1)}, bf16[256,256]{1,0:T(8,128)(2,1)S(1)}, u32[]{:S(2)}, u32[]{:S(2)}) collective-permute-start(bf16[256,256]{1,0:T(8,128)(2,1)S(1)} %slice.153), channel_id=1, source_target_pairs={{0,4},{1,3},{2,6},{3,1},{4,0},{5,7},{6,2},{7,5},{8,12},{9,11},{10,... | collective-permute-start | bytes 393224 | tf_op jit(solution)/shard_map/ppermute | solution.py:95
  81.6 6.6 %collective-permute-start.23 = (bf16[256,256]{1,0:T(8,128)(2,1)S(1)}, bf16[256,256]{1,0:T(8,128)(2,1)S(1)}, u32[]{:S(2)}, u32[]{:S(2)}) collective-permute-start(bf16[256,256]{1,0:T(8,128)(2,1)S(1)} %get-tuple-element.61), channel_id=1, source_target_pairs={{0,12},{1,11},{2,14},{3,9},{4,8},{5,15},{6,10},{7,13},{8,4},{9,3},... | collective-permute-start | bytes 393224 | tf_op jit(solution)/shard_map/ppermute | solution.py:101
  83.4 6.3 %collective-permute-start.22 = (bf16[256,256]{1,0:T(8,128)(2,1)S(1)}, bf16[256,256]{1,0:T(8,128)(2,1)S(1)}, u32[]{:S(2)}, u32[]{:S(2)}) collective-permute-start(bf16[256,256]{1,0:T(8,128)(2,1)S(1)} %get-tuple-element.62), channel_id=1, source_target_pairs={{0,8},{8,0},{16,24},{24,16},{1,9},{9,1},{17,25},{25,17},{2,10},{10... | collective-permute-start | bytes 393224 | tf_op jit(solution)/shard_map/ppermute | solution.py:87
  83.8 6.1 %collective-permute-start.19 = (bf16[512,256]{1,0:T(8,128)(2,1)S(1)}, bf16[512,256]{1,0:T(8,128)(2,1)S(1)}, u32[]{:S(2)}, u32[]{:S(2)}) collective-permute-start(bf16[512,256]{1,0:T(8,128)(2,1)S(1)} %pad_maximum_fusion.1), channel_id=1, source_target_pairs={{0,1},{1,0},{2,3},{3,2},{4,5},{5,4},{6,7},{7,6},{8,9},{9,8},{10,11... | collective-permute-start | bytes 786440 | tf_op jit(solution)/shard_map/ppermute | solution.py:91
  89.7 1.6 %collective-permute-start.24 = (bf16[512,256]{1,0:T(8,128)(2,1)S(1)}, bf16[512,256]{1,0:T(8,128)(2,1)S(1)}, u32[]{:S(2)}, u32[]{:S(2)}) collective-permute-start(bf16[512,256]{1,0:T(8,128)(2,1)S(1)} %pad_maximum_fusion.2), channel_id=1, source_target_pairs={{0,1},{1,0},{2,3},{3,2},{4,5},{5,4},{6,7},{7,6},{8,9},{9,8},{10,11... | collective-permute-start | bytes 786440 | tf_op jit(solution)/shard_map/ppermute | solution.py:91

commit v3 on v2

--- a/solution.py
+++ b/solution.py
@@ -130,26 +130,17 @@
     return pl.ds(pl.multiple_of(start * unit, unit), unit)
 
 
-def solve_kernel(panel_ref, inverse_ref, mine_ref, give_ref, rest_ref):
-    half = give_ref.shape[0]
-    for part in range(2):
-        rows = pl.ds(part * half, half)
-        solved = dot_t(panel_ref[rows, :], inverse_ref[...]).astype(BF16)
-        mine_ref[rows, :] = solved
-
-        @pl.when(core_index() != part)
-        def _():
-            give_ref[...] = solved
-
-        @pl.when(core_index() == part)
-        def _():
-            rest_ref[...] = solved
+def solve_kernel(other, panel_ref, inverse_ref, out_ref):
+    part = 1 - core_index() if other else core_index()
+    rows = aligned(part, out_ref.shape[0])
+    out_ref[...] = dot_t(panel_ref[rows, :], inverse_ref[...]).astype(BF16)
 
 
 def join_kernel(rest_ref, got_ref, *outs):
     width = rest_ref.shape[1]
     core = core_index()
-    for out, first in zip(outs, (0, 0, outs[1].shape[0])):
+    half = outs[0].shape[0]
+    for out, first in zip(outs, (0, 0, half - outs[2].shape[0])):
         rows = pl.ds(first, out.shape[0])
         out[:, aligned(core, width)] = rest_ref[rows, :]
         out[:, aligned(1 - core, width)] = got_ref[rows, :]
@@ -162,29 +153,27 @@
     return [jnp.bitwise_xor(chip, side) for chip in (0, next_hop, hop, X_HOP | Y_HOP) for side in (0, CORE)]
 
 
-def pick_own_kernel(height, order_ref, mine_ref, got_ref, got_rest_ref, out_ref):
+def pick_own_kernel(height, order_ref, rest_ref, give_ref, got_ref, got_rest_ref, out_ref):
     col, core = lax.axis_index("col"), core_index()
-    half, width = got_ref.shape
+    half, width = rest_ref.shape
     for place, mask in enumerate(slot_masks()):
         start = order_ref[jnp.bitwise_xor(col, mask)] * height
         rows = pl.ds(place * height, height)
-        out_ref[rows, aligned(core, width)] = mine_ref[pl.ds(pl.multiple_of(start, height), height), :]
         inside = start // half == core
         source = pl.ds(pl.multiple_of(start % half, height), height)
-
-        @pl.when(inside)
-        def _():
-            out_ref[rows, aligned(1 - core, width)] = got_ref[source, :]
-
-        @pl.when(jnp.logical_not(inside))
-        def _():
-            out_ref[rows, aligned(1 - core, width)] = got_rest_ref[source, :]
-
-
-def pick_pair_kernel(height, pieces, order_ref, *refs):
+        for wanted, mine, other in ((inside, rest_ref, got_ref), (jnp.logical_not(inside), give_ref, got_rest_ref)):
+
+            @pl.when(wanted)
+            def _():
+                out_ref[rows, aligned(core, width)] = mine[source, :]
+                out_ref[rows, aligned(1 - core, width)] = other[source, :]
+
+
+def pick_pair_kernel(height, valid, order_ref, *refs):
+    pieces = len(valid)
     out_ref = refs[-1]
     col, core = lax.axis_index("col"), core_index()
-    half = sum(ref.shape[0] for ref in refs[:pieces])
+    half = sum(count for _, count in valid)
     for place, mask in enumerate(slot_masks()):
         start = order_ref[jnp.bitwise_xor(col, mask)] * height
         rows = pl.ds(place * height, height)
@@ -192,8 +181,10 @@
         within = start % half
         for number in range(2 * pieces):
             ref = refs[number]
-            first = sum(r.shape[0] for r in refs[: number % pieces])
-            here = jnp.logical_and(within >= first, within < first + ref.shape[0])
+            skip, count = valid[number % pieces]
+            first = sum(c for _, c in valid[: number % pieces])
+            here = jnp.logical_and(within >= first, within < first + count)
+            first = first - skip
             wanted = inside if number < pieces else jnp.logical_not(inside)
 
             @pl.when(jnp.logical_and(here, wanted))
@@ -215,20 +206,19 @@
     return local_call(functools.partial(product_kernel, len(a)), [*a, x], [(shape, F32), (shape, BF16)], "products")
 
 
-def own_second(keep, got):
-    total = keep + got.astype(F32)
+def own_ways(total):
     half = total.shape[0] // 2
     return total[:half], hop_swap(total[half:].astype(BF16), SECOND_HOP)
 
 
-def pair_second(keep, got):
-    total = (keep + got.astype(F32)).astype(BF16)
+def pair_ways(total):
     half = total.shape[0] // 2
-    return row_swap(total[:half], PAIR), both_swap(total[half:], PAIR, SECOND_HOP)
+    total = total.astype(BF16)
+    return row_swap(total[:half], PAIR), both_swap(total[half:], PAIR, SECOND_HOP), total
 
 
 def pack(terms, height):
-    return jnp.concatenate([term[height:].astype(BF16) for term in terms], axis=0)
+    return jnp.concatenate([term[height : 2 * height].astype(BF16) for term in terms], axis=0)
 
 
 def finish_kernel(height, plan, anc_ref, *refs):
@@ -237,20 +227,21 @@
     width = 4 * height
     half = out_ref.shape[1] // 2
     base = jnp.bitwise_or((row & 1) * 2, row >> 1)
-    for number, (which, first, count) in enumerate(plan):
-        *terms, other = refs[5 * number : 5 * number + 5]
-        for back in range(2):
-            at = jnp.bitwise_xor(base, which + 2 * back)
+    position = 0
+    for which, first, count, terms in plan:
+        mine = refs[position : position + terms]
+        other = refs[position + terms]
+        position += terms + 1
+        for returned, wanted in enumerate((range(2), range(2, terms))):
+            at = jnp.bitwise_xor(base, which + 2 * returned)
             for block in range(count):
                 source = pl.ds(block * height, height)
                 for side in range(2):
-                    place = (core if side == 0 else 1 - core) * half + (first + block) * width + at * height
+                    tiles = [other[pl.ds(k * height, height), source] if side else mine[k][:height, source] for k in wanted]
+                    total = sum(tile.astype(F32) for tile in tiles)
+                    place = (1 - core if side else core) * half + (first + block) * width + at * height
                     place = pl.ds(pl.multiple_of(place, height), height)
-                    if side == 0:
-                        low, high = (terms[2 * back + k][:height, source] for k in range(2))
-                    else:
-                        low, high = (other[pl.ds((2 * back + k) * height, height), source] for k in range(2))
-                    out_ref[:, place] = anc_ref[:, place] - (low.astype(F32) + high.astype(F32))
+                    out_ref[:, place] = anc_ref[:, place] - total
 
 
 def paired_body(panel_blocks, factor_inverse, target_rows, owner_order, ancestor_rows):
@@ -258,56 +249,63 @@
     rows = panel_count * height
     panel = panel_blocks.reshape(rows, width)
     half = rows // 2
-    pieces = (half // 2, half // 2)
-
-    mine, give, rest = local_call(
-        solve_kernel, [panel, factor_inverse[0]], [((rows, width), BF16)] + [((half, width), BF16)] * 2, "solve"
-    )
+    pieces = (2 * height, half - 2 * height)
+    valid = [(0, count) for count in pieces]
+
+    inverse = factor_inverse[0]
+    half_shape = [((half, width), BF16)]
+    (give,) = local_call(functools.partial(solve_kernel, True), [panel, inverse], half_shape, "solve")
     got = core_swap(give)
+    (rest,) = local_call(functools.partial(solve_kernel, False), [panel, after(inverse, give)], half_shape, "solve")
     got_rest = core_swap(rest)
     joined, *parts = local_call(
         join_kernel, [rest, got], [((count, 2 * width), BF16) for count in (half, *pieces)], "join"
     )
-    first = row_swap(joined, MIDDLE)
     pair = [row_swap(part, PAIR) for part in parts]
     (a_own,) = local_call(
         functools.partial(pick_own_kernel, height),
-        [owner_order, mine, got, got_rest],
+        [owner_order, rest, give, got, got_rest],
         [((rows, 2 * width), BF16)],
         "pick_own",
         scalars=1,
     )
-    pair[0] = after(pair[0], a_own)
-    second = [row_swap(part, MIDDLE) for part in pair]
+    first = row_swap(after(joined, a_own), MIDDLE)
+    second = [row_swap(after(pair[0], a_own), MIDDLE), row_swap(pair[1], MIDDLE)]
+    pair_b = core_swap(pair[0])
     (a_pair,) = local_call(
-        functools.partial(pick_pair_kernel, height, len(pair)),
-        [owner_order, *pair, *[core_swap(part) for part in pair]],
+        functools.partial(pick_pair_kernel, height, valid),
+        [owner_order, *pair, pair_b, core_swap(after(pair[1], pair_b))],
         [((rows, 2 * width), BF16)],
         "pick_pair",
         scalars=1,
     )
-
-    own1, send = products([a_own], first)
-    own1_got = hop_swap(send, FIRST_HOP)
-    pair1, send = products([after(a_pair, own1)], first)
-    pair1_got = hop_swap(send, FIRST_HOP)
-    own1_terms = own_second(own1, after(own1_got, pair1))
-    keep2, send = products([a_own, a_pair], after(second[0], own1_terms[0]))
+    keep_own, send = products([a_own], first)
+    got_own = hop_swap(send, FIRST_HOP)
+    keep_pair, send = products([after(a_pair, keep_own)], first)
+    got_pair = hop_swap(send, FIRST_HOP)
+    keep2, send = products([a_own, a_pair], after(second[0], keep_pair))
     got2 = hop_swap(send, FIRST_HOP)
-    terms1 = (*own1_terms, *pair_second(pair1, after(pair1_got, keep2)))
-    keep3, send = products([a_own, a_pair], after(second[1], terms1[2]))
+    own1 = own_ways(keep_own + after(got_own, keep2).astype(F32))
+    *pair1, sent1 = pair_ways(keep_pair + after(got_pair, own1[0]).astype(F32))
+    keep3, send = products([a_own, a_pair], after(second[1], sent1))
     got3 = hop_swap(send, FIRST_HOP)
-    packed1 = pack((terms1[0], after(terms1[1], keep3), *terms1[2:]), height)
+    terms1 = (*own1, pair1[0], after(pair1[1], keep3))
+    packed1 = pack(terms1, height)
     other1 = core_swap(packed1)
-    got2 = after(got2, packed1)
-    terms2 = (*own_second(keep2[:half], got2[:half]), *pair_second(keep2[half:], got2[half:]))
+    total2 = keep2 + after(got2, packed1).astype(F32)
+    own2 = own_ways(total2[:half])
+    *pair2, sent2 = pair_ways(total2[half:])
+    terms2 = (*own2, pair2[0], after(pair2[1], sent2))
     packed2 = pack(terms2, height)
     other2 = core_swap(packed2)
-    got3 = after(got3, packed2)
-    terms3 = (*own_second(keep3[:half], got3[:half]), *pair_second(keep3[half:], got3[half:]))
-    other3 = core_swap(pack(terms3, height))
+    total3 = keep3 + after(got3, packed2).astype(F32)
+    own3 = own_ways(total3[:half])
+    *pair3, sent3 = pair_ways(total3[half:])
+    terms3 = (*own3, pair3[0], after(pair3[1], sent3))
+    packed3 = pack(terms3, height)
+    other3 = core_swap(packed3)
     blocks = [count // height for count in pieces]
-    plan = ((0, 0, half // height), (1, 0, blocks[0]), (1, blocks[0], blocks[1]))
+    plan = ((0, 0, half // height, len(terms1)), (1, 0, blocks[0], len(terms2)), (1, blocks[0], blocks[1], len(terms3)))
     (result,) = local_call(
         functools.partial(finish_kernel, height, plan),
         [ancestor_rows[0], *terms1, other1, *terms2, other2, *terms3, other3],

time: 93.7 us -> 86.3 us (0.921)
  waiting for transfers between devices: 51 us -> 44.3 us
    ppermute x8, waiting for transfers between devices: 30.1 us -> 24.4 us  [row_swap(): return lax.ppermute(value, 'row', list(enumerate(partner)))]
    ppermute x7, waiting for transfers between devices: 13 us -> 7.86 us  [hop_swap(): lax.ppermute(value, 'col', [(i, i ^ hops[i & CORE]) for i in range(lax.ax...]
    ppermute x3, starting transfers between devices: 4.79 us -> 9.55 us  [both_swap(): return lax.ppermute(value, ('row', 'col'), pairs)]
    ppermute x3, waiting for transfers between devices: 4.92 us -> 9.66 us  [both_swap(): return lax.ppermute(value, ('row', 'col'), pairs)]
    ppermute x8, starting transfers between devices: 13.5 us -> 9.64 us  [row_swap(): return lax.ppermute(value, 'row', list(enumerate(partner)))]
    ppermute x7, starting transfers between devices: 9.42 us -> 8.2 us  [hop_swap(): lax.ppermute(value, 'col', [(i, i ^ hops[i & CORE]) for i in range(lax.ax...]
    pallas_call x9 -> x10, Pallas kernels: 10.1 us -> 10.1 us  [local_call(): pl.pallas_call(kernel, in_specs=[pl.BlockSpec(memory_space=pltpu.SMEM)] *...]
  transfers between devices with their start and end apart: 25 -> 25, of which waited for: 14 -> 13; matrix products, arithmetic and copies ran while one was open for 1% -> 1% of each run, Pallas kernels for 7% -> 9%
where the time goes in v3:
time: 86.3 us; the launch traced here: 86.1 us
  waiting for transfers between devices  44.3 us (51%)
  starting transfers between devices  28.1 us (33%)
  Pallas kernels  10.1 us (12%)
  local copies, waits for them, and re-layouts  2.54 us (3%)
    ppermute x8, waiting for transfers between devices, row_swap(): return lax.ppermute(value, 'row', list(enumerate(partner)))  24.4 us
    pallas_call x10, Pallas kernels, local_call(): pl.pallas_call(kernel, in_specs=[pl.BlockSpec(memory_space=pltpu.SMEM)] *...  10.1 us
    ppermute x3, waiting for transfers between devices, both_swap(): return lax.ppermute(value, ('row', 'col'), pairs)  9.66 us
    ppermute x8, starting transfers between devices, row_swap(): return lax.ppermute(value, 'row', list(enumerate(partner)))  9.64 us
    ppermute x3, starting transfers between devices, both_swap(): return lax.ppermute(value, ('row', 'col'), pairs)  9.55 us
    ppermute x7, starting transfers between devices, hop_swap(): lax.ppermute(value, 'col', [(i, i ^ hops[i & CORE]) for i in range(lax.ax...  8.2 us
    ppermute x7, waiting for transfers between devices, hop_swap(): lax.ppermute(value, 'col', [(i, i ^ hops[i & CORE]) for i in range(lax.ax...  7.86 us
    ppermute x7, waiting for transfers between devices, core_swap(): lax.ppermute(value, 'col', [(i, i ^ CORE) for i in range(lax.axis_size('c...  2.4 us
  transfers between devices with their start and end apart: 25, of which 13 were waited for; matrix products, arithmetic and copies ran while one was open for 1% of the time, Pallas kernels for 9%

profile of v3, /device:TPU:0, one launch (start us, length us, event | category | flops | bytes accessed | tf_op | source)
XLA Modules:
  0.0 86.1 jit_solution(15715504565412683462)
XLA Ops:
  0.0 1.2 %copy-done = bf16[1,8,128,512]{3,2,1,0:T(8,128)(2,1)S(1)} copy-done((bf16[1,8,128,512]{3,2,1,0:T(8,128)(2,1)S(1)}, bf16[1,8,128,512]{3,2,1,0:T(8,128)(2,1)}, u32[]{:S(2)}) %copy-start) | copy-done | bytes 1048600
  1.2 1.0 %copy-done.2 = bf16[1,512,512]{2,1,0:T(8,128)(2,1)S(1)} copy-done((bf16[1,512,512]{2,1,0:T(8,128)(2,1)S(1)}, bf16[1,512,512]{2,1,0:T(8,128)(2,1)}, u32[]{:S(2)}) %copy-start.2) | copy-done | bytes 524312
  2.3 0.5 solve.2.give_ref
  2.8 0.5 collective-permute-start
  3.3 0.5 solve.3.rest_ref
  3.7 0.1 collective-permute-start.1
  3.9 0.9 %collective-permute-done.got_ref = bf16[512,512]{1,0:T(8,128)(2,1)S(1)} collective-permute-done((bf16[512,512]{1,0:T(8,128)(2,1)S(1)}, bf16[512,512]{1,0:T(8,128)(2,1)S(1)}, u32[]{:S(2)}, u32[]{:S(2)}) %collective-permute-start) | collective-permute-done | bytes 524320 | tf_op jit(solution)/shard_map/ppermute | solution.py:91
  4.8 0.1 join.1
  5.0 3.0 %collective-permute-start.4 = (bf16[256,1024]{1,0:T(8,128)(2,1)S(1)}, bf16[256,1024]{1,0:T(8,128)(2,1)S(1)}, u32[]{:S(2)}, u32[]{:S(2)}) collective-permute-start(bf16[256,1024]{1,0:T(8,128)(2,1)S(1)} %get-tuple-element.33), channel_id=1, source_target_pairs={{0,8},{8,0},{16,24},{24,16},{1,9},{9,1},{17,25},{25,17},{2,10},{10... | collective-permute-start | bytes 1572872 | tf_op jit(solution)/shard_map/ppermute | solution.py:87
  8.0 0.8 pick_own.1.refs_0_
  8.8 0.7 collective-permute-start.2
  9.6 4.4 %collective-permute-start.5 = (bf16[256,1024]{1,0:T(8,128)(2,1)S(1)}, bf16[256,1024]{1,0:T(8,128)(2,1)S(1)}, u32[]{:S(2)}, u32[]{:S(2)}) collective-permute-start(bf16[256,1024]{1,0:T(8,128)(2,1)S(1)} %get-tuple-element.34), channel_id=1, source_target_pairs={{0,8},{8,0},{16,24},{24,16},{1,9},{9,1},{17,25},{25,17},{2,10},{10... | collective-permute-start | bytes 1572872 | tf_op jit(solution)/shard_map/ppermute | solution.py:87
  14.0 6.7 %collective-permute-done.4.refs_0_ = bf16[256,1024]{1,0:T(8,128)(2,1)S(1)} collective-permute-done((bf16[256,1024]{1,0:T(8,128)(2,1)S(1)}, bf16[256,1024]{1,0:T(8,128)(2,1)S(1)}, u32[]{:S(2)}, u32[]{:S(2)}) %collective-permute-start.4) | collective-permute-done | bytes 524320 | tf_op jit(solution)/shard_map/ppermute | solution.py:87
  20.7 10.7 %collective-permute-done.5.refs_1_ = bf16[256,1024]{1,0:T(8,128)(2,1)S(1)} collective-permute-done((bf16[256,1024]{1,0:T(8,128)(2,1)S(1)}, bf16[256,1024]{1,0:T(8,128)(2,1)S(1)}, u32[]{:S(2)}, u32[]{:S(2)}) %collective-permute-start.5) | collective-permute-done | bytes 524320 | tf_op jit(solution)/shard_map/ppermute | solution.py:87
  31.4 0.7 collective-permute-start.8
  32.1 1.3 %products.4 = (f32[512,512]{1,0:T(8,128)S(1)}, bf16[512,512]{1,0:T(8,128)(2,1)S(1)}) custom-call(bf16[1024,1024]{1,0:T(8,128)(2,1)S(1)} %pick_own.1.refs_0_, bf16[512,1024]{1,0:T(8,128)(2,1)S(1)} %collective-permute-done.2.refs_1_), custom_call_target="tpu_custom_call" | custom-call | flops 1 | bytes 1 | tf_op jit(solution)/shard_map/products/pallas_call | solution.py:114
  33.4 1.7 %collective-permute-start.3 = (bf16[512,512]{1,0:T(8,128)(2,1)S(1)}, bf16[512,512]{1,0:T(8,128)(2,1)S(1)}, u32[]{:S(2)}, u32[]{:S(2)}) collective-permute-start(bf16[512,512]{1,0:T(8,128)(2,1)S(1)} %get-tuple-element.32), channel_id=1, source_target_pairs={{0,2},{1,5},{2,0},{3,7},{4,6},{5,1},{6,4},{7,3},{8,10},{9,13},{10,... | collective-permute-start | bytes 1572872 | tf_op jit(solution)/shard_map/ppermute | solution.py:95
  35.2 0.9 %pick_pair.1.refs_0_.refs_1_ = bf16[1024,1024]{1,0:T(8,128)(2,1)S(1)} custom-call(s32[8]{0:T(128)S(1)} %copy-done.3, bf16[256,1024]{1,0:T(8,128)(2,1)S(1)} %collective-permute-done.4.refs_0_, bf16[256,1024]{1,0:T(8,128)(2,1)S(1)} %collective-permute-done.5.refs_1_, bf16[256,1024]{1,0:T(8,128)(2,1)S(1)} %collective-permute-done.6.refs_2_, ...), custom_call_target="tpu_custom_call" | custom-call | flops 1 | bytes 1 | tf_op jit(solution)/shard_map/pick_pair/pallas_call | solution.py:114
  36.1 1.3 %products.5 = (f32[512,512]{1,0:T(8,128)S(1)}, bf16[512,512]{1,0:T(8,128)(2,1)S(1)}) custom-call(bf16[1024,1024]{1,0:T(8,128)(2,1)S(1)} %pick_pair.1.refs_0_.refs_1_, bf16[512,1024]{1,0:T(8,128)(2,1)S(1)} %collective-permute-done.2.refs_1_), custom_call_target="tpu_custom_call" | custom-call | flops 1 | bytes 1 | tf_op jit(solution)/shard_map/products/pallas_call | solution.py:114
  37.4 0.4 collective-permute-start.10
  37.8 0.7 collective-permute-start.13
  38.5 1.3 %products.6 = (f32[1024,256]{1,0:T(8,128)S(1)}, bf16[1024,256]{1,0:T(8,128)(2,1)S(1)}) custom-call(bf16[1024,1024]{1,0:T(8,128)(2,1)S(1)} %pick_own.1.refs_0_, bf16[1024,1024]{1,0:T(8,128)(2,1)S(1)} %pick_pair.1.refs_0_.refs_1_, bf16[256,1024]{1,0:T(8,128)(2,1)S(1)} %collective-permute-done.8.refs_2_), custom_call_target="tpu_custom_call" | custom-call | flops 1 | bytes 1 | tf_op jit(solution)/shard_map/products/pallas_call | solution.py:114
  39.8 2.9 %collective-permute-done.3 = bf16[512,512]{1,0:T(8,128)(2,1)S(1)} collective-permute-done((bf16[512,512]{1,0:T(8,128)(2,1)S(1)}, bf16[512,512]{1,0:T(8,128)(2,1)S(1)}, u32[]{:S(2)}, u32[]{:S(2)}) %collective-permute-start.3) | collective-permute-done | bytes 524320 | tf_op jit(solution)/shard_map/ppermute | solution.py:95
  42.7 0.2 fusion.2
  43.0 1.7 %collective-permute-start.9 = (bf16[256,512]{1,0:T(8,128)(2,1)S(1)}, bf16[256,512]{1,0:T(8,128)(2,1)S(1)}, u32[]{:S(2)}, u32[]{:S(2)}) collective-permute-start(bf16[256,512]{1,0:T(8,128)(2,1)S(1)} %slice.120), channel_id=1, source_target_pairs={{0,4},{1,3},{2,6},{3,1},{4,0},{5,7},{6,2},{7,5},{8,12},{9,11},{10,... | collective-permute-start | bytes 786440 | tf_op jit(solution)/shard_map/ppermute | solution.py:95
  44.7 1.5 %collective-permute-start.15 = (bf16[1024,256]{1,0:T(8,128)(2,1)S(1)}, bf16[1024,256]{1,0:T(8,128)(2,1)S(1)}, u32[]{:S(2)}, u32[]{:S(2)}) collective-permute-start(bf16[1024,256]{1,0:T(8,128)(2,1)S(1)} %get-tuple-element.47), channel_id=1, source_target_pairs={{0,2},{1,5},{2,0},{3,7},{4,6},{5,1},{6,4},{7,3},{8,10},{9,13},{10,... | collective-permute-start | bytes 1572872 | tf_op jit(solution)/shard_map/ppermute | solution.py:95
  46.2 4.9 %collective-permute-done.10 = bf16[512,512]{1,0:T(8,128)(2,1)S(1)} collective-permute-done((bf16[512,512]{1,0:T(8,128)(2,1)S(1)}, bf16[512,512]{1,0:T(8,128)(2,1)S(1)}, u32[]{:S(2)}, u32[]{:S(2)}) %collective-permute-start.10) | collective-permute-done | bytes 524320 | tf_op jit(solution)/shard_map/ppermute | solution.py:95
  51.1 0.2 add_convert_fusion
  51.3 3.3 %collective-permute-start.12 = (bf16[256,512]{1,0:T(8,128)(2,1)S(1)}, bf16[256,512]{1,0:T(8,128)(2,1)S(1)}, u32[]{:S(2)}, u32[]{:S(2)}) collective-permute-start(bf16[256,512]{1,0:T(8,128)(2,1)S(1)} %get-tuple-element.63), channel_id=1, source_target_pairs={{0,12},{1,11},{2,14},{3,9},{4,8},{5,15},{6,10},{7,13},{8,4},{9,3},... | collective-permute-start | bytes 786440 | tf_op jit(solution)/shard_map/ppermute | solution.py:101
  54.7 0.1 collective-permute-start.11
  54.8 1.3 %products.7 = (f32[1024,256]{1,0:T(8,128)S(1)}, bf16[1024,256]{1,0:T(8,128)(2,1)S(1)}) custom-call(bf16[1024,1024]{1,0:T(8,128)(2,1)S(1)} %pick_own.1.refs_0_, bf16[1024,1024]{1,0:T(8,128)(2,1)S(1)} %pick_pair.1.refs_0_.refs_1_, bf16[256,1024]{1,0:T(8,128)(2,1)S(1)} %collective-permute-done.13.refs_2_), custom_call_target="tpu_custom_call" | custom-call | flops 1 | bytes 1 | tf_op jit(solution)/shard_map/products/pallas_call | solution.py:114
  56.1 1.3 %collective-permute-start.20 = (bf16[1024,256]{1,0:T(8,128)(2,1)S(1)}, bf16[1024,256]{1,0:T(8,128)(2,1)S(1)}, u32[]{:S(2)}, u32[]{:S(2)}) collective-permute-start(bf16[1024,256]{1,0:T(8,128)(2,1)S(1)} %get-tuple-element.49), channel_id=1, source_target_pairs={{0,2},{1,5},{2,0},{3,7},{4,6},{5,1},{6,4},{7,3},{8,10},{9,13},{10,... | collective-permute-start | bytes 1572872 | tf_op jit(solution)/shard_map/ppermute | solution.py:95
  57.4 4.4 %collective-permute-done.12.refs_3_ = bf16[256,512]{1,0:T(8,128)(2,1)S(1)} collective-permute-done((bf16[256,512]{1,0:T(8,128)(2,1)S(1)}, bf16[256,512]{1,0:T(8,128)(2,1)S(1)}, u32[]{:S(2)}, u32[]{:S(2)}) %collective-permute-start.12) | collective-permute-done | bytes 262176 | tf_op jit(solution)/shard_map/ppermute | solution.py:101
  61.9 3.7 %collective-permute-done.11.refs_2_ = bf16[256,512]{1,0:T(8,128)(2,1)S(1)} collective-permute-done((bf16[256,512]{1,0:T(8,128)(2,1)S(1)}, bf16[256,512]{1,0:T(8,128)(2,1)S(1)}, u32[]{:S(2)}, u32[]{:S(2)}) %collective-permute-start.11) | collective-permute-done | bytes 262176 | tf_op jit(solution)/shard_map/ppermute | solution.py:87
  65.7 0.1 fusion.1
  65.9 2.7 %collective-permute-start.18 = (bf16[256,256]{1,0:T(8,128)(2,1)S(1)}, bf16[256,256]{1,0:T(8,128)(2,1)S(1)}, u32[]{:S(2)}, u32[]{:S(2)}) collective-permute-start(bf16[256,256]{1,0:T(8,128)(2,1)S(1)} %get-tuple-element.60), channel_id=1, source_target_pairs={{0,12},{1,11},{2,14},{3,9},{4,8},{5,15},{6,10},{7,13},{8,4},{9,3},... | collective-permute-start | bytes 393224 | tf_op jit(solution)/shard_map/ppermute | solution.py:101
  68.6 0.9 %collective-permute-start.16 = (bf16[256,256]{1,0:T(8,128)(2,1)S(1)}, bf16[256,256]{1,0:T(8,128)(2,1)S(1)}, u32[]{:S(2)}, u32[]{:S(2)}) collective-permute-start(bf16[256,256]{1,0:T(8,128)(2,1)S(1)} %get-tuple-element.62), channel_id=1, source_target_pairs={{0,4},{1,3},{2,6},{3,1},{4,0},{5,7},{6,2},{7,5},{8,12},{9,11},{10,... | collective-permute-start | bytes 393224 | tf_op jit(solution)/shard_map/ppermute | solution.py:95
  69.4 2.8 %collective-permute-done.18.refs_8_ = bf16[256,256]{1,0:T(8,128)(2,1)S(1)} collective-permute-done((bf16[256,256]{1,0:T(8,128)(2,1)S(1)}, bf16[256,256]{1,0:T(8,128)(2,1)S(1)}, u32[]{:S(2)}, u32[]{:S(2)}) %collective-permute-start.18) | collective-permute-done | bytes 131104 | tf_op jit(solution)/shard_map/ppermute | solution.py:101
  72.2 1.3 %collective-permute-done.17.refs_7_ = bf16[256,256]{1,0:T(8,128)(2,1)S(1)} collective-permute-done((bf16[256,256]{1,0:T(8,128)(2,1)S(1)}, bf16[256,256]{1,0:T(8,128)(2,1)S(1)}, u32[]{:S(2)}, u32[]{:S(2)}) %collective-permute-start.17) | collective-permute-done | bytes 131104 | tf_op jit(solution)/shard_map/ppermute | solution.py:87
  73.5 0.1 collective-permute-done.16.refs_6_
  73.6 0.1 fusion
  73.8 3.5 %collective-permute-start.23 = (bf16[256,256]{1,0:T(8,128)(2,1)S(1)}, bf16[256,256]{1,0:T(8,128)(2,1)S(1)}, u32[]{:S(2)}, u32[]{:S(2)}) collective-permute-start(bf16[256,256]{1,0:T(8,128)(2,1)S(1)} %get-tuple-element.57), channel_id=1, source_target_pairs={{0,12},{1,11},{2,14},{3,9},{4,8},{5,15},{6,10},{7,13},{8,4},{9,3},... | collective-permute-start | bytes 393224 | tf_op jit(solution)/shard_map/ppermute | solution.py:101
  77.4 0.6 collective-permute-start.21
  78.0 2.4 %collective-permute-done.23.refs_13_ = bf16[256,256]{1,0:T(8,128)(2,1)S(1)} collective-permute-done((bf16[256,256]{1,0:T(8,128)(2,1)S(1)}, bf16[256,256]{1,0:T(8,128)(2,1)S(1)}, u32[]{:S(2)}, u32[]{:S(2)}) %collective-permute-start.23) | collective-permute-done | bytes 131104 | tf_op jit(solution)/shard_map/ppermute | solution.py:101
  80.5 1.9 %collective-permute-done.22.refs_12_ = bf16[256,256]{1,0:T(8,128)(2,1)S(1)} collective-permute-done((bf16[256,256]{1,0:T(8,128)(2,1)S(1)}, bf16[256,256]{1,0:T(8,128)(2,1)S(1)}, u32[]{:S(2)}, u32[]{:S(2)}) %collective-permute-start.22) | collective-permute-done | bytes 131104 | tf_op jit(solution)/shard_map/ppermute | solution.py:87
  82.4 0.1 collective-permute-start.24
  82.6 1.4 %collective-permute-done.24.refs_14_ = bf16[512,256]{1,0:T(8,128)(2,1)S(1)} collective-permute-done((bf16[512,256]{1,0:T(8,128)(2,1)S(1)}, bf16[512,256]{1,0:T(8,128)(2,1)S(1)}, u32[]{:S(2)}, u32[]{:S(2)}) %collective-permute-start.24) | collective-permute-done | bytes 262176 | tf_op jit(solution)/shard_map/ppermute | solution.py:91
  84.0 2.1 %finish.1 = f32[128,4096]{1,0:T(8,128)} custom-call(f32[128,4096]{1,0:T(8,128)S(1)} %bitcast.6, f32[256,512]{1,0:T(8,128)S(1)} %slice.119.refs_0_, bf16[256,512]{1,0:T(8,128)(2,1)S(1)} %collective-permute-done.9.refs_1_, bf16[256,512]{1,0:T(8,128)(2,1)S(1)} %collective-permute-done.11.refs_2_, bf16[256,512]{1,0:T(8,128)(2,1)S(1)} %collective-permute-done.12.refs_3_, ...), custom_call_target="tpu_custom_call" | custom-call | flops 1 | bytes 1 | tf_op jit(solution)/shard_map/finish/pallas_call | solution.py:114
  (46 shorter events, 0.4 us)
Async XLA Ops:
  0.0 1.2 %copy-start = (bf16[1,8,128,512]{3,2,1,0:T(8,128)(2,1)S(1)}, bf16[1,8,128,512]{3,2,1,0:T(8,128)(2,1)}, u32[]{:S(2)}) copy-start(bf16[1,8,128,512]{3,2,1,0:T(8,128)(2,1)} %param.5) | copy-start | bytes 3145732
  1.2 1.0 %copy-start.2 = (bf16[1,512,512]{2,1,0:T(8,128)(2,1)S(1)}, bf16[1,512,512]{2,1,0:T(8,128)(2,1)}, u32[]{:S(2)}) copy-start(bf16[1,512,512]{2,1,0:T(8,128)(2,1)} %param.6) | copy-start | bytes 1572868
  2.7 5.2 %copy-start.3 = (s32[8]{0:T(128)S(1)}, s32[8]{0:T(128)}, u32[]{:S(2)}) copy-start(s32[8]{0:T(128)} %order_ref.3) | copy-start | bytes 100
  2.8 2.1 %collective-permute-start = (bf16[512,512]{1,0:T(8,128)(2,1)S(1)}, bf16[512,512]{1,0:T(8,128)(2,1)S(1)}, u32[]{:S(2)}, u32[]{:S(2)}) collective-permute-start(bf16[512,512]{1,0:T(8,128)(2,1)S(1)} %solve.2.give_ref), channel_id=1, source_target_pairs={{0,1},{1,0},{2,3},{3,2},{4,5},{5,4},{6,7},{7,6},{8,9},{9,8},{10,11... | collective-permute-start | bytes 1572872 | tf_op jit(solution)/shard_map/ppermute | solution.py:91
  3.7 4.2 %collective-permute-start.1 = (bf16[512,512]{1,0:T(8,128)(2,1)S(1)}, bf16[512,512]{1,0:T(8,128)(2,1)S(1)}, u32[]{:S(2)}, u32[]{:S(2)}) collective-permute-start(bf16[512,512]{1,0:T(8,128)(2,1)S(1)} %solve.3.rest_ref), channel_id=1, source_target_pairs={{0,1},{1,0},{2,3},{3,2},{4,5},{5,4},{6,7},{7,6},{8,9},{9,8},{10,11... | collective-permute-start | bytes 1572872 | tf_op jit(solution)/shard_map/ppermute | solution.py:91
  5.0 15.7 %collective-permute-start.4 = (bf16[256,1024]{1,0:T(8,128)(2,1)S(1)}, bf16[256,1024]{1,0:T(8,128)(2,1)S(1)}, u32[]{:S(2)}, u32[]{:S(2)}) collective-permute-start(bf16[256,1024]{1,0:T(8,128)(2,1)S(1)} %get-tuple-element.33), channel_id=1, source_target_pairs={{0,8},{8,0},{16,24},{24,16},{1,9},{9,1},{17,25},{25,17},{2,10},{10... | collective-permute-start | bytes 1572872 | tf_op jit(solution)/shard_map/ppermute | solution.py:87
  8.8 23.3 %collective-permute-start.2 = (bf16[512,1024]{1,0:T(8,128)(2,1)S(1)}, bf16[512,1024]{1,0:T(8,128)(2,1)S(1)}, u32[]{:S(2)}, u32[]{:S(2)}) collective-permute-start(bf16[512,1024]{1,0:T(8,128)(2,1)S(1)} %get-tuple-element.30), channel_id=1, source_target_pairs={{0,0},{8,16},{16,8},{24,24},{1,1},{9,17},{17,9},{25,25},{2,2},{10,... | collective-permute-start | bytes 3145736 | tf_op jit(solution)/shard_map/ppermute | solution.py:87
  9.6 21.9 %collective-permute-start.5 = (bf16[256,1024]{1,0:T(8,128)(2,1)S(1)}, bf16[256,1024]{1,0:T(8,128)(2,1)S(1)}, u32[]{:S(2)}, u32[]{:S(2)}) collective-permute-start(bf16[256,1024]{1,0:T(8,128)(2,1)S(1)} %get-tuple-element.34), channel_id=1, source_target_pairs={{0,8},{8,0},{16,24},{24,16},{1,9},{9,1},{17,25},{25,17},{2,10},{10... | collective-permute-start | bytes 1572872 | tf_op jit(solution)/shard_map/ppermute | solution.py:87
  20.7 10.8 %collective-permute-start.6 = (bf16[256,1024]{1,0:T(8,128)(2,1)S(1)}, bf16[256,1024]{1,0:T(8,128)(2,1)S(1)}, u32[]{:S(2)}, u32[]{:S(2)}) collective-permute-start(bf16[256,1024]{1,0:T(8,128)(2,1)S(1)} %collective-permute-done.4.refs_0_), channel_id=1, source_target_pairs={{0,1},{1,0},{2,3},{3,2},{4,5},{5,4},{6,7},{7,6},{8,9},{9,8},{10,11... | collective-permute-start | bytes 1572872 | tf_op jit(solution)/shard_map/ppermute | solution.py:91
  31.4 3.7 %collective-permute-start.7 = (bf16[256,1024]{1,0:T(8,128)(2,1)S(1)}, bf16[256,1024]{1,0:T(8,128)(2,1)S(1)}, u32[]{:S(2)}, u32[]{:S(2)}) collective-permute-start(bf16[256,1024]{1,0:T(8,128)(2,1)S(1)} %collective-permute-done.5.refs_1_), channel_id=1, source_target_pairs={{0,1},{1,0},{2,3},{3,2},{4,5},{5,4},{6,7},{7,6},{8,9},{9,8},{10,11... | collective-permute-start | bytes 1572872 | tf_op jit(solution)/shard_map/ppermute | solution.py:91
  31.4 7.1 %collective-permute-start.8 = (bf16[256,1024]{1,0:T(8,128)(2,1)S(1)}, bf16[256,1024]{1,0:T(8,128)(2,1)S(1)}, u32[]{:S(2)}, u32[]{:S(2)}) collective-permute-start(bf16[256,1024]{1,0:T(8,128)(2,1)S(1)} %collective-permute-done.4.refs_0_), channel_id=1, source_target_pairs={{0,0},{8,16},{16,8},{24,24},{1,1},{9,17},{17,9},{25,25},{2,2},{10,... | collective-permute-start | bytes 1572872 | tf_op jit(solution)/shard_map/ppermute | solution.py:87
  33.4 9.2 %collective-permute-start.3 = (bf16[512,512]{1,0:T(8,128)(2,1)S(1)}, bf16[512,512]{1,0:T(8,128)(2,1)S(1)}, u32[]{:S(2)}, u32[]{:S(2)}) collective-permute-start(bf16[512,512]{1,0:T(8,128)(2,1)S(1)} %get-tuple-element.32), channel_id=1, source_target_pairs={{0,2},{1,5},{2,0},{3,7},{4,6},{5,1},{6,4},{7,3},{8,10},{9,13},{10,... | collective-permute-start | bytes 1572872 | tf_op jit(solution)/shard_map/ppermute | solution.py:95
  37.4 13.7 %collective-permute-start.10 = (bf16[512,512]{1,0:T(8,128)(2,1)S(1)}, bf16[512,512]{1,0:T(8,128)(2,1)S(1)}, u32[]{:S(2)}, u32[]{:S(2)}) collective-permute-start(bf16[512,512]{1,0:T(8,128)(2,1)S(1)} %get-tuple-element.42), channel_id=1, source_target_pairs={{0,2},{1,5},{2,0},{3,7},{4,6},{5,1},{6,4},{7,3},{8,10},{9,13},{10,... | collective-permute-start | bytes 1572872 | tf_op jit(solution)/shard_map/ppermute | solution.py:95
  37.8 17.0 %collective-permute-start.13 = (bf16[256,1024]{1,0:T(8,128)(2,1)S(1)}, bf16[256,1024]{1,0:T(8,128)(2,1)S(1)}, u32[]{:S(2)}, u32[]{:S(2)}) collective-permute-start(bf16[256,1024]{1,0:T(8,128)(2,1)S(1)} %collective-permute-done.5.refs_1_), channel_id=1, source_target_pairs={{0,0},{8,16},{16,8},{24,24},{1,1},{9,17},{17,9},{25,25},{2,2},{10,... | collective-permute-start | bytes 1572872 | tf_op jit(solution)/shard_map/ppermute | solution.py:87
  43.0 11.9 %collective-permute-start.9 = (bf16[256,512]{1,0:T(8,128)(2,1)S(1)}, bf16[256,512]{1,0:T(8,128)(2,1)S(1)}, u32[]{:S(2)}, u32[]{:S(2)}) collective-permute-start(bf16[256,512]{1,0:T(8,128)(2,1)S(1)} %slice.120), channel_id=1, source_target_pairs={{0,4},{1,3},{2,6},{3,1},{4,0},{5,7},{6,2},{7,5},{8,12},{9,11},{10,... | collective-permute-start | bytes 786440 | tf_op jit(solution)/shard_map/ppermute | solution.py:95
  44.7 21.0 %collective-permute-start.15 = (bf16[1024,256]{1,0:T(8,128)(2,1)S(1)}, bf16[1024,256]{1,0:T(8,128)(2,1)S(1)}, u32[]{:S(2)}, u32[]{:S(2)}) collective-permute-start(bf16[1024,256]{1,0:T(8,128)(2,1)S(1)} %get-tuple-element.47), channel_id=1, source_target_pairs={{0,2},{1,5},{2,0},{3,7},{4,6},{5,1},{6,4},{7,3},{8,10},{9,13},{10,... | collective-permute-start | bytes 1572872 | tf_op jit(solution)/shard_map/ppermute | solution.py:95
  51.3 10.6 %collective-permute-start.12 = (bf16[256,512]{1,0:T(8,128)(2,1)S(1)}, bf16[256,512]{1,0:T(8,128)(2,1)S(1)}, u32[]{:S(2)}, u32[]{:S(2)}) collective-permute-start(bf16[256,512]{1,0:T(8,128)(2,1)S(1)} %get-tuple-element.63), channel_id=1, source_target_pairs={{0,12},{1,11},{2,14},{3,9},{4,8},{5,15},{6,10},{7,13},{8,4},{9,3},... | collective-permute-start | bytes 786440 | tf_op jit(solution)/shard_map/ppermute | solution.py:101
  54.7 11.0 %collective-permute-start.11 = (bf16[256,512]{1,0:T(8,128)(2,1)S(1)}, bf16[256,512]{1,0:T(8,128)(2,1)S(1)}, u32[]{:S(2)}, u32[]{:S(2)}) collective-permute-start(bf16[256,512]{1,0:T(8,128)(2,1)S(1)} %get-tuple-element.64), channel_id=1, source_target_pairs={{0,8},{8,0},{16,24},{24,16},{1,9},{9,1},{17,25},{25,17},{2,10},{10... | collective-permute-start | bytes 786440 | tf_op jit(solution)/shard_map/ppermute | solution.py:87
  56.1 17.5 %collective-permute-start.20 = (bf16[1024,256]{1,0:T(8,128)(2,1)S(1)}, bf16[1024,256]{1,0:T(8,128)(2,1)S(1)}, u32[]{:S(2)}, u32[]{:S(2)}) collective-permute-start(bf16[1024,256]{1,0:T(8,128)(2,1)S(1)} %get-tuple-element.49), channel_id=1, source_target_pairs={{0,2},{1,5},{2,0},{3,7},{4,6},{5,1},{6,4},{7,3},{8,10},{9,13},{10,... | collective-permute-start | bytes 1572872 | tf_op jit(solution)/shard_map/ppermute | solution.py:95
  65.9 6.3 %collective-permute-start.18 = (bf16[256,256]{1,0:T(8,128)(2,1)S(1)}, bf16[256,256]{1,0:T(8,128)(2,1)S(1)}, u32[]{:S(2)}, u32[]{:S(2)}) collective-permute-start(bf16[256,256]{1,0:T(8,128)(2,1)S(1)} %get-tuple-element.60), channel_id=1, source_target_pairs={{0,12},{1,11},{2,14},{3,9},{4,8},{5,15},{6,10},{7,13},{8,4},{9,3},... | collective-permute-start | bytes 393224 | tf_op jit(solution)/shard_map/ppermute | solution.py:101
  68.5 5.0 %collective-permute-start.17 = (bf16[256,256]{1,0:T(8,128)(2,1)S(1)}, bf16[256,256]{1,0:T(8,128)(2,1)S(1)}, u32[]{:S(2)}, u32[]{:S(2)}) collective-permute-start(bf16[256,256]{1,0:T(8,128)(2,1)S(1)} %get-tuple-element.61), channel_id=1, source_target_pairs={{0,8},{8,0},{16,24},{24,16},{1,9},{9,1},{17,25},{25,17},{2,10},{10... | collective-permute-start | bytes 393224 | tf_op jit(solution)/shard_map/ppermute | solution.py:87
  68.6 5.1 %collective-permute-start.16 = (bf16[256,256]{1,0:T(8,128)(2,1)S(1)}, bf16[256,256]{1,0:T(8,128)(2,1)S(1)}, u32[]{:S(2)}, u32[]{:S(2)}) collective-permute-start(bf16[256,256]{1,0:T(8,128)(2,1)S(1)} %get-tuple-element.62), channel_id=1, source_target_pairs={{0,4},{1,3},{2,6},{3,1},{4,0},{5,7},{6,2},{7,5},{8,12},{9,11},{10,... | collective-permute-start | bytes 393224 | tf_op jit(solution)/shard_map/ppermute | solution.py:95
  69.4 13.1 %collective-permute-start.14 = (bf16[512,512]{1,0:T(8,128)(2,1)S(1)}, bf16[512,512]{1,0:T(8,128)(2,1)S(1)}, u32[]{:S(2)}, u32[]{:S(2)}) collective-permute-start(bf16[512,512]{1,0:T(8,128)(2,1)S(1)} %pad_maximum_fusion), channel_id=1, source_target_pairs={{0,1},{1,0},{2,3},{3,2},{4,5},{5,4},{6,7},{7,6},{8,9},{9,8},{10,11... | collective-permute-start | bytes 1572872 | tf_op jit(solution)/shard_map/ppermute | solution.py:91
  73.8 10.2 %copy-start.1 = (f32[1,128,4096]{2,1,0:T(8,128)S(1)}, f32[1,128,4096]{2,1,0:T(8,128)}, u32[]{:S(2)}) copy-start(f32[1,128,4096]{2,1,0:T(8,128)} %param.8) | copy-start | bytes 6291460
  73.8 6.6 %collective-permute-start.23 = (bf16[256,256]{1,0:T(8,128)(2,1)S(1)}, bf16[256,256]{1,0:T(8,128)(2,1)S(1)}, u32[]{:S(2)}, u32[]{:S(2)}) collective-permute-start(bf16[256,256]{1,0:T(8,128)(2,1)S(1)} %get-tuple-element.57), channel_id=1, source_target_pairs={{0,12},{1,11},{2,14},{3,9},{4,8},{5,15},{6,10},{7,13},{8,4},{9,3},... | collective-permute-start | bytes 393224 | tf_op jit(solution)/shard_map/ppermute | solution.py:101
  77.4 5.0 %collective-permute-start.22 = (bf16[256,256]{1,0:T(8,128)(2,1)S(1)}, bf16[256,256]{1,0:T(8,128)(2,1)S(1)}, u32[]{:S(2)}, u32[]{:S(2)}) collective-permute-start(bf16[256,256]{1,0:T(8,128)(2,1)S(1)} %get-tuple-element.58), channel_id=1, source_target_pairs={{0,8},{8,0},{16,24},{24,16},{1,9},{9,1},{17,25},{25,17},{2,10},{10... | collective-permute-start | bytes 393224 | tf_op jit(solution)/shard_map/ppermute | solution.py:87
  77.4 5.0 %collective-permute-start.21 = (bf16[256,256]{1,0:T(8,128)(2,1)S(1)}, bf16[256,256]{1,0:T(8,128)(2,1)S(1)}, u32[]{:S(2)}, u32[]{:S(2)}) collective-permute-start(bf16[256,256]{1,0:T(8,128)(2,1)S(1)} %get-tuple-element.59), channel_id=1, source_target_pairs={{0,4},{1,3},{2,6},{3,1},{4,0},{5,7},{6,2},{7,5},{8,12},{9,11},{10,... | collective-permute-start | bytes 393224 | tf_op jit(solution)/shard_map/ppermute | solution.py:95
  78.0 4.5 %collective-permute-start.19 = (bf16[512,256]{1,0:T(8,128)(2,1)S(1)}, bf16[512,256]{1,0:T(8,128)(2,1)S(1)}, u32[]{:S(2)}, u32[]{:S(2)}) collective-permute-start(bf16[512,256]{1,0:T(8,128)(2,1)S(1)} %pad_maximum_fusion.1), channel_id=1, source_target_pairs={{0,1},{1,0},{2,3},{3,2},{4,5},{5,4},{6,7},{7,6},{8,9},{9,8},{10,11... | collective-permute-start | bytes 786440 | tf_op jit(solution)/shard_map/ppermute | solution.py:91
  82.4 1.6 %collective-permute-start.24 = (bf16[512,256]{1,0:T(8,128)(2,1)S(1)}, bf16[512,256]{1,0:T(8,128)(2,1)S(1)}, u32[]{:S(2)}, u32[]{:S(2)}) collective-permute-start(bf16[512,256]{1,0:T(8,128)(2,1)S(1)} %pad_maximum_fusion.2), channel_id=1, source_target_pairs={{0,1},{1,0},{2,3},{3,2},{4,5},{5,4},{6,7},{7,6},{8,9},{9,8},{10,11... | collective-permute-start | bytes 786440 | tf_op jit(solution)/shard_map/ppermute | solution.py:91

commit v4 on v3

--- a/solution.py
+++ b/solution.py
@@ -287,7 +287,7 @@
     got2 = hop_swap(send, FIRST_HOP)
     own1 = own_ways(keep_own + after(got_own, keep2).astype(F32))
     *pair1, sent1 = pair_ways(keep_pair + after(got_pair, own1[0]).astype(F32))
-    keep3, send = products([a_own, a_pair], after(second[1], sent1))
+    keep3, send = products([a_own, a_pair], after(second[1], keep2))
     got3 = hop_swap(send, FIRST_HOP)
     terms1 = (*own1, pair1[0], after(pair1[1], keep3))
     packed1 = pack(terms1, height)

time: 86.3 us -> 85.8 us (level)
    ppermute x3, starting transfers between devices: 9.55 us -> 8.34 us  [both_swap(): return lax.ppermute(value, ('row', 'col'), pairs)]
    ppermute x8, waiting for transfers between devices: 24.4 us -> 23.5 us  [row_swap(): return lax.ppermute(value, 'row', list(enumerate(partner)))]
  transfers between devices with their start and end apart: 25 -> 25, of which waited for: 13 -> 14; matrix products, arithmetic and copies ran while one was open for 1% -> 1% of each run, Pallas kernels for 9% -> 9%
where the time goes in v4:
time: 85.8 us; the launch traced here: 85.6 us
  waiting for transfers between devices  44.5 us (52%)
  starting transfers between devices  27.5 us (32%)
  Pallas kernels  10.1 us (12%)
  local copies, waits for them, and re-layouts  2.54 us (3%)
    ppermute x8, waiting for transfers between devices, row_swap(): return lax.ppermute(value, 'row', list(enumerate(partner)))  23.5 us
    ppermute x3, waiting for transfers between devices, both_swap(): return lax.ppermute(value, ('row', 'col'), pairs)  10.4 us
    pallas_call x10, Pallas kernels, local_call(): pl.pallas_call(kernel, in_specs=[pl.BlockSpec(memory_space=pltpu.SMEM)] *...  10.1 us
    ppermute x8, starting transfers between devices, row_swap(): return lax.ppermute(value, 'row', list(enumerate(partner)))  9.94 us
    ppermute x7, starting transfers between devices, hop_swap(): lax.ppermute(value, 'col', [(i, i ^ hops[i & CORE]) for i in range(lax.ax...  8.49 us
    ppermute x3, starting transfers between devices, both_swap(): return lax.ppermute(value, ('row', 'col'), pairs)  8.34 us
    ppermute x7, waiting for transfers between devices, hop_swap(): lax.ppermute(value, 'col', [(i, i ^ hops[i & CORE]) for i in range(lax.ax...  8.21 us
    ppermute x7, waiting for transfers between devices, core_swap(): lax.ppermute(value, 'col', [(i, i ^ CORE) for i in range(lax.axis_size('c...  2.4 us
  transfers between devices with their start and end apart: 25, of which 14 were waited for; matrix products, arithmetic and copies ran while one was open for 1% of the time, Pallas kernels for 9%

profile of v4, /device:TPU:0, one launch (start us, length us, event | category | flops | bytes accessed | tf_op | source)
XLA Modules:
  0.0 85.6 jit_solution(8126745082549317062)
XLA Ops:
  0.0 1.2 %copy-done = bf16[1,8,128,512]{3,2,1,0:T(8,128)(2,1)S(1)} copy-done((bf16[1,8,128,512]{3,2,1,0:T(8,128)(2,1)S(1)}, bf16[1,8,128,512]{3,2,1,0:T(8,128)(2,1)}, u32[]{:S(2)}) %copy-start) | copy-done | bytes 1048600
  1.2 1.0 %copy-done.2 = bf16[1,512,512]{2,1,0:T(8,128)(2,1)S(1)} copy-done((bf16[1,512,512]{2,1,0:T(8,128)(2,1)S(1)}, bf16[1,512,512]{2,1,0:T(8,128)(2,1)}, u32[]{:S(2)}) %copy-start.2) | copy-done | bytes 524312
  2.3 0.5 solve.2.give_ref
  2.8 0.5 collective-permute-start
  3.3 0.5 solve.3.rest_ref
  3.7 0.1 collective-permute-start.1
  3.9 0.9 %collective-permute-done.got_ref = bf16[512,512]{1,0:T(8,128)(2,1)S(1)} collective-permute-done((bf16[512,512]{1,0:T(8,128)(2,1)S(1)}, bf16[512,512]{1,0:T(8,128)(2,1)S(1)}, u32[]{:S(2)}, u32[]{:S(2)}) %collective-permute-start) | collective-permute-done | bytes 524320 | tf_op jit(solution)/shard_map/ppermute | solution.py:91
  4.8 0.1 join.1
  5.0 3.0 %collective-permute-start.4 = (bf16[256,1024]{1,0:T(8,128)(2,1)S(1)}, bf16[256,1024]{1,0:T(8,128)(2,1)S(1)}, u32[]{:S(2)}, u32[]{:S(2)}) collective-permute-start(bf16[256,1024]{1,0:T(8,128)(2,1)S(1)} %get-tuple-element.33), channel_id=1, source_target_pairs={{0,8},{8,0},{16,24},{24,16},{1,9},{9,1},{17,25},{25,17},{2,10},{10... | collective-permute-start | bytes 1572872 | tf_op jit(solution)/shard_map/ppermute | solution.py:87
  8.0 0.8 pick_own.1.refs_0_
  8.8 0.7 collective-permute-start.2
  9.6 4.4 %collective-permute-start.5 = (bf16[256,1024]{1,0:T(8,128)(2,1)S(1)}, bf16[256,1024]{1,0:T(8,128)(2,1)S(1)}, u32[]{:S(2)}, u32[]{:S(2)}) collective-permute-start(bf16[256,1024]{1,0:T(8,128)(2,1)S(1)} %get-tuple-element.34), channel_id=1, source_target_pairs={{0,8},{8,0},{16,24},{24,16},{1,9},{9,1},{17,25},{25,17},{2,10},{10... | collective-permute-start | bytes 1572872 | tf_op jit(solution)/shard_map/ppermute | solution.py:87
  14.0 6.7 %collective-permute-done.4.refs_0_ = bf16[256,1024]{1,0:T(8,128)(2,1)S(1)} collective-permute-done((bf16[256,1024]{1,0:T(8,128)(2,1)S(1)}, bf16[256,1024]{1,0:T(8,128)(2,1)S(1)}, u32[]{:S(2)}, u32[]{:S(2)}) %collective-permute-start.4) | collective-permute-done | bytes 524320 | tf_op jit(solution)/shard_map/ppermute | solution.py:87
  20.7 10.7 %collective-permute-done.5.refs_1_ = bf16[256,1024]{1,0:T(8,128)(2,1)S(1)} collective-permute-done((bf16[256,1024]{1,0:T(8,128)(2,1)S(1)}, bf16[256,1024]{1,0:T(8,128)(2,1)S(1)}, u32[]{:S(2)}, u32[]{:S(2)}) %collective-permute-start.5) | collective-permute-done | bytes 524320 | tf_op jit(solution)/shard_map/ppermute | solution.py:87
  31.4 0.7 collective-permute-start.8
  32.1 1.3 %products.4 = (f32[512,512]{1,0:T(8,128)S(1)}, bf16[512,512]{1,0:T(8,128)(2,1)S(1)}) custom-call(bf16[1024,1024]{1,0:T(8,128)(2,1)S(1)} %pick_own.1.refs_0_, bf16[512,1024]{1,0:T(8,128)(2,1)S(1)} %collective-permute-done.2.refs_1_), custom_call_target="tpu_custom_call" | custom-call | flops 1 | bytes 1 | tf_op jit(solution)/shard_map/products/pallas_call | solution.py:114
  33.4 1.7 %collective-permute-start.3 = (bf16[512,512]{1,0:T(8,128)(2,1)S(1)}, bf16[512,512]{1,0:T(8,128)(2,1)S(1)}, u32[]{:S(2)}, u32[]{:S(2)}) collective-permute-start(bf16[512,512]{1,0:T(8,128)(2,1)S(1)} %get-tuple-element.32), channel_id=1, source_target_pairs={{0,2},{1,5},{2,0},{3,7},{4,6},{5,1},{6,4},{7,3},{8,10},{9,13},{10,... | collective-permute-start | bytes 1572872 | tf_op jit(solution)/shard_map/ppermute | solution.py:95
  35.2 0.9 %pick_pair.1.refs_0_.refs_1_ = bf16[1024,1024]{1,0:T(8,128)(2,1)S(1)} custom-call(s32[8]{0:T(128)S(1)} %copy-done.3, bf16[256,1024]{1,0:T(8,128)(2,1)S(1)} %collective-permute-done.4.refs_0_, bf16[256,1024]{1,0:T(8,128)(2,1)S(1)} %collective-permute-done.5.refs_1_, bf16[256,1024]{1,0:T(8,128)(2,1)S(1)} %collective-permute-done.6.refs_2_, ...), custom_call_target="tpu_custom_call" | custom-call | flops 1 | bytes 1 | tf_op jit(solution)/shard_map/pick_pair/pallas_call | solution.py:114
  36.1 1.3 %products.5 = (f32[512,512]{1,0:T(8,128)S(1)}, bf16[512,512]{1,0:T(8,128)(2,1)S(1)}) custom-call(bf16[1024,1024]{1,0:T(8,128)(2,1)S(1)} %pick_pair.1.refs_0_.refs_1_, bf16[512,1024]{1,0:T(8,128)(2,1)S(1)} %collective-permute-done.2.refs_1_), custom_call_target="tpu_custom_call" | custom-call | flops 1 | bytes 1 | tf_op jit(solution)/shard_map/products/pallas_call | solution.py:114
  37.4 0.4 collective-permute-start.10
  37.8 0.7 collective-permute-start.13
  38.5 1.3 %products.6 = (f32[1024,256]{1,0:T(8,128)S(1)}, bf16[1024,256]{1,0:T(8,128)(2,1)S(1)}) custom-call(bf16[1024,1024]{1,0:T(8,128)(2,1)S(1)} %pick_own.1.refs_0_, bf16[1024,1024]{1,0:T(8,128)(2,1)S(1)} %pick_pair.1.refs_0_.refs_1_, bf16[256,1024]{1,0:T(8,128)(2,1)S(1)} %collective-permute-done.8.refs_2_), custom_call_target="tpu_custom_call" | custom-call | flops 1 | bytes 1 | tf_op jit(solution)/shard_map/products/pallas_call | solution.py:114
  39.8 2.9 %collective-permute-done.3 = bf16[512,512]{1,0:T(8,128)(2,1)S(1)} collective-permute-done((bf16[512,512]{1,0:T(8,128)(2,1)S(1)}, bf16[512,512]{1,0:T(8,128)(2,1)S(1)}, u32[]{:S(2)}, u32[]{:S(2)}) %collective-permute-start.3) | collective-permute-done | bytes 524320 | tf_op jit(solution)/shard_map/ppermute | solution.py:95
  42.7 0.2 fusion.2
  43.0 1.7 %collective-permute-start.9 = (bf16[256,512]{1,0:T(8,128)(2,1)S(1)}, bf16[256,512]{1,0:T(8,128)(2,1)S(1)}, u32[]{:S(2)}, u32[]{:S(2)}) collective-permute-start(bf16[256,512]{1,0:T(8,128)(2,1)S(1)} %slice.120), channel_id=1, source_target_pairs={{0,4},{1,3},{2,6},{3,1},{4,0},{5,7},{6,2},{7,5},{8,12},{9,11},{10,... | collective-permute-start | bytes 786440 | tf_op jit(solution)/shard_map/ppermute | solution.py:95
  44.7 1.5 %collective-permute-start.15 = (bf16[1024,256]{1,0:T(8,128)(2,1)S(1)}, bf16[1024,256]{1,0:T(8,128)(2,1)S(1)}, u32[]{:S(2)}, u32[]{:S(2)}) collective-permute-start(bf16[1024,256]{1,0:T(8,128)(2,1)S(1)} %get-tuple-element.47), channel_id=1, source_target_pairs={{0,2},{1,5},{2,0},{3,7},{4,6},{5,1},{6,4},{7,3},{8,10},{9,13},{10,... | collective-permute-start | bytes 1572872 | tf_op jit(solution)/shard_map/ppermute | solution.py:95
  46.2 4.9 %collective-permute-done.10 = bf16[512,512]{1,0:T(8,128)(2,1)S(1)} collective-permute-done((bf16[512,512]{1,0:T(8,128)(2,1)S(1)}, bf16[512,512]{1,0:T(8,128)(2,1)S(1)}, u32[]{:S(2)}, u32[]{:S(2)}) %collective-permute-start.10) | collective-permute-done | bytes 524320 | tf_op jit(solution)/shard_map/ppermute | solution.py:95
  51.1 0.2 add_convert_fusion
  51.3 3.3 %collective-permute-start.12 = (bf16[256,512]{1,0:T(8,128)(2,1)S(1)}, bf16[256,512]{1,0:T(8,128)(2,1)S(1)}, u32[]{:S(2)}, u32[]{:S(2)}) collective-permute-start(bf16[256,512]{1,0:T(8,128)(2,1)S(1)} %get-tuple-element.63), channel_id=1, source_target_pairs={{0,12},{1,11},{2,14},{3,9},{4,8},{5,15},{6,10},{7,13},{8,4},{9,3},... | collective-permute-start | bytes 786440 | tf_op jit(solution)/shard_map/ppermute | solution.py:101
  54.7 0.1 collective-permute-start.11
  54.8 1.3 %products.7 = (f32[1024,256]{1,0:T(8,128)S(1)}, bf16[1024,256]{1,0:T(8,128)(2,1)S(1)}) custom-call(bf16[1024,1024]{1,0:T(8,128)(2,1)S(1)} %pick_own.1.refs_0_, bf16[1024,1024]{1,0:T(8,128)(2,1)S(1)} %pick_pair.1.refs_0_.refs_1_, bf16[256,1024]{1,0:T(8,128)(2,1)S(1)} %collective-permute-done.13.refs_2_), custom_call_target="tpu_custom_call" | custom-call | flops 1 | bytes 1 | tf_op jit(solution)/shard_map/products/pallas_call | solution.py:114
  56.1 1.3 %collective-permute-start.20 = (bf16[1024,256]{1,0:T(8,128)(2,1)S(1)}, bf16[1024,256]{1,0:T(8,128)(2,1)S(1)}, u32[]{:S(2)}, u32[]{:S(2)}) collective-permute-start(bf16[1024,256]{1,0:T(8,128)(2,1)S(1)} %get-tuple-element.49), channel_id=1, source_target_pairs={{0,2},{1,5},{2,0},{3,7},{4,6},{5,1},{6,4},{7,3},{8,10},{9,13},{10,... | collective-permute-start | bytes 1572872 | tf_op jit(solution)/shard_map/ppermute | solution.py:95
  57.4 4.5 %collective-permute-done.12.refs_3_ = bf16[256,512]{1,0:T(8,128)(2,1)S(1)} collective-permute-done((bf16[256,512]{1,0:T(8,128)(2,1)S(1)}, bf16[256,512]{1,0:T(8,128)(2,1)S(1)}, u32[]{:S(2)}, u32[]{:S(2)}) %collective-permute-start.12) | collective-permute-done | bytes 262176 | tf_op jit(solution)/shard_map/ppermute | solution.py:101
  61.9 3.7 %collective-permute-done.11.refs_2_ = bf16[256,512]{1,0:T(8,128)(2,1)S(1)} collective-permute-done((bf16[256,512]{1,0:T(8,128)(2,1)S(1)}, bf16[256,512]{1,0:T(8,128)(2,1)S(1)}, u32[]{:S(2)}, u32[]{:S(2)}) %collective-permute-start.11) | collective-permute-done | bytes 262176 | tf_op jit(solution)/shard_map/ppermute | solution.py:87
  65.7 0.1 fusion.1
  65.9 2.7 %collective-permute-start.18 = (bf16[256,256]{1,0:T(8,128)(2,1)S(1)}, bf16[256,256]{1,0:T(8,128)(2,1)S(1)}, u32[]{:S(2)}, u32[]{:S(2)}) collective-permute-start(bf16[256,256]{1,0:T(8,128)(2,1)S(1)} %get-tuple-element.60), channel_id=1, source_target_pairs={{0,12},{1,11},{2,14},{3,9},{4,8},{5,15},{6,10},{7,13},{8,4},{9,3},... | collective-permute-start | bytes 393224 | tf_op jit(solution)/shard_map/ppermute | solution.py:101
  68.6 0.9 %collective-permute-start.16 = (bf16[256,256]{1,0:T(8,128)(2,1)S(1)}, bf16[256,256]{1,0:T(8,128)(2,1)S(1)}, u32[]{:S(2)}, u32[]{:S(2)}) collective-permute-start(bf16[256,256]{1,0:T(8,128)(2,1)S(1)} %get-tuple-element.62), channel_id=1, source_target_pairs={{0,4},{1,3},{2,6},{3,1},{4,0},{5,7},{6,2},{7,5},{8,12},{9,11},{10,... | collective-permute-start | bytes 393224 | tf_op jit(solution)/shard_map/ppermute | solution.py:95
  69.4 2.8 %collective-permute-done.18.refs_8_ = bf16[256,256]{1,0:T(8,128)(2,1)S(1)} collective-permute-done((bf16[256,256]{1,0:T(8,128)(2,1)S(1)}, bf16[256,256]{1,0:T(8,128)(2,1)S(1)}, u32[]{:S(2)}, u32[]{:S(2)}) %collective-permute-start.18) | collective-permute-done | bytes 131104 | tf_op jit(solution)/shard_map/ppermute | solution.py:101
  72.2 1.3 %collective-permute-done.17.refs_7_ = bf16[256,256]{1,0:T(8,128)(2,1)S(1)} collective-permute-done((bf16[256,256]{1,0:T(8,128)(2,1)S(1)}, bf16[256,256]{1,0:T(8,128)(2,1)S(1)}, u32[]{:S(2)}, u32[]{:S(2)}) %collective-permute-start.17) | collective-permute-done | bytes 131104 | tf_op jit(solution)/shard_map/ppermute | solution.py:87
  73.6 0.1 fusion
  73.8 2.3 %collective-permute-start.23 = (bf16[256,256]{1,0:T(8,128)(2,1)S(1)}, bf16[256,256]{1,0:T(8,128)(2,1)S(1)}, u32[]{:S(2)}, u32[]{:S(2)}) collective-permute-start(bf16[256,256]{1,0:T(8,128)(2,1)S(1)} %get-tuple-element.57), channel_id=1, source_target_pairs={{0,12},{1,11},{2,14},{3,9},{4,8},{5,15},{6,10},{7,13},{8,4},{9,3},... | collective-permute-start | bytes 393224 | tf_op jit(solution)/shard_map/ppermute | solution.py:101
  76.2 0.3 collective-permute-start.22
  76.5 0.9 %collective-permute-start.21 = (bf16[256,256]{1,0:T(8,128)(2,1)S(1)}, bf16[256,256]{1,0:T(8,128)(2,1)S(1)}, u32[]{:S(2)}, u32[]{:S(2)}) collective-permute-start(bf16[256,256]{1,0:T(8,128)(2,1)S(1)} %get-tuple-element.59), channel_id=1, source_target_pairs={{0,4},{1,3},{2,6},{3,1},{4,0},{5,7},{6,2},{7,5},{8,12},{9,11},{10,... | collective-permute-start | bytes 393224 | tf_op jit(solution)/shard_map/ppermute | solution.py:95
  77.4 3.1 %collective-permute-done.23.refs_13_ = bf16[256,256]{1,0:T(8,128)(2,1)S(1)} collective-permute-done((bf16[256,256]{1,0:T(8,128)(2,1)S(1)}, bf16[256,256]{1,0:T(8,128)(2,1)S(1)}, u32[]{:S(2)}, u32[]{:S(2)}) %collective-permute-start.23) | collective-permute-done | bytes 131104 | tf_op jit(solution)/shard_map/ppermute | solution.py:101
  80.5 1.0 %collective-permute-done.22.refs_12_ = bf16[256,256]{1,0:T(8,128)(2,1)S(1)} collective-permute-done((bf16[256,256]{1,0:T(8,128)(2,1)S(1)}, bf16[256,256]{1,0:T(8,128)(2,1)S(1)}, u32[]{:S(2)}, u32[]{:S(2)}) %collective-permute-start.22) | collective-permute-done | bytes 131104 | tf_op jit(solution)/shard_map/ppermute | solution.py:87
  81.5 0.4 collective-permute-done.21.refs_11_
  82.1 1.4 %collective-permute-done.24.refs_14_ = bf16[512,256]{1,0:T(8,128)(2,1)S(1)} collective-permute-done((bf16[512,256]{1,0:T(8,128)(2,1)S(1)}, bf16[512,256]{1,0:T(8,128)(2,1)S(1)}, u32[]{:S(2)}, u32[]{:S(2)}) %collective-permute-start.24) | collective-permute-done | bytes 262176 | tf_op jit(solution)/shard_map/ppermute | solution.py:91
  83.5 2.1 %finish.1 = f32[128,4096]{1,0:T(8,128)} custom-call(f32[128,4096]{1,0:T(8,128)S(1)} %bitcast.6, f32[256,512]{1,0:T(8,128)S(1)} %slice.119.refs_0_, bf16[256,512]{1,0:T(8,128)(2,1)S(1)} %collective-permute-done.9.refs_1_, bf16[256,512]{1,0:T(8,128)(2,1)S(1)} %collective-permute-done.11.refs_2_, bf16[256,512]{1,0:T(8,128)(2,1)S(1)} %collective-permute-done.12.refs_3_, ...), custom_call_target="tpu_custom_call" | custom-call | flops 1 | bytes 1 | tf_op jit(solution)/shard_map/finish/pallas_call | solution.py:114
  (46 shorter events, 0.6 us)
Async XLA Ops:
  0.0 1.2 %copy-start = (bf16[1,8,128,512]{3,2,1,0:T(8,128)(2,1)S(1)}, bf16[1,8,128,512]{3,2,1,0:T(8,128)(2,1)}, u32[]{:S(2)}) copy-start(bf16[1,8,128,512]{3,2,1,0:T(8,128)(2,1)} %param.5) | copy-start | bytes 3145732
  1.2 1.0 %copy-start.2 = (bf16[1,512,512]{2,1,0:T(8,128)(2,1)S(1)}, bf16[1,512,512]{2,1,0:T(8,128)(2,1)}, u32[]{:S(2)}) copy-start(bf16[1,512,512]{2,1,0:T(8,128)(2,1)} %param.6) | copy-start | bytes 1572868
  2.7 5.2 %copy-start.3 = (s32[8]{0:T(128)S(1)}, s32[8]{0:T(128)}, u32[]{:S(2)}) copy-start(s32[8]{0:T(128)} %order_ref.3) | copy-start | bytes 100
  2.8 2.1 %collective-permute-start = (bf16[512,512]{1,0:T(8,128)(2,1)S(1)}, bf16[512,512]{1,0:T(8,128)(2,1)S(1)}, u32[]{:S(2)}, u32[]{:S(2)}) collective-permute-start(bf16[512,512]{1,0:T(8,128)(2,1)S(1)} %solve.2.give_ref), channel_id=1, source_target_pairs={{0,1},{1,0},{2,3},{3,2},{4,5},{5,4},{6,7},{7,6},{8,9},{9,8},{10,11... | collective-permute-start | bytes 1572872 | tf_op jit(solution)/shard_map/ppermute | solution.py:91
  3.7 4.2 %collective-permute-start.1 = (bf16[512,512]{1,0:T(8,128)(2,1)S(1)}, bf16[512,512]{1,0:T(8,128)(2,1)S(1)}, u32[]{:S(2)}, u32[]{:S(2)}) collective-permute-start(bf16[512,512]{1,0:T(8,128)(2,1)S(1)} %solve.3.rest_ref), channel_id=1, source_target_pairs={{0,1},{1,0},{2,3},{3,2},{4,5},{5,4},{6,7},{7,6},{8,9},{9,8},{10,11... | collective-permute-start | bytes 1572872 | tf_op jit(solution)/shard_map/ppermute | solution.py:91
  5.0 15.7 %collective-permute-start.4 = (bf16[256,1024]{1,0:T(8,128)(2,1)S(1)}, bf16[256,1024]{1,0:T(8,128)(2,1)S(1)}, u32[]{:S(2)}, u32[]{:S(2)}) collective-permute-start(bf16[256,1024]{1,0:T(8,128)(2,1)S(1)} %get-tuple-element.33), channel_id=1, source_target_pairs={{0,8},{8,0},{16,24},{24,16},{1,9},{9,1},{17,25},{25,17},{2,10},{10... | collective-permute-start | bytes 1572872 | tf_op jit(solution)/shard_map/ppermute | solution.py:87
  8.8 23.3 %collective-permute-start.2 = (bf16[512,1024]{1,0:T(8,128)(2,1)S(1)}, bf16[512,1024]{1,0:T(8,128)(2,1)S(1)}, u32[]{:S(2)}, u32[]{:S(2)}) collective-permute-start(bf16[512,1024]{1,0:T(8,128)(2,1)S(1)} %get-tuple-element.30), channel_id=1, source_target_pairs={{0,0},{8,16},{16,8},{24,24},{1,1},{9,17},{17,9},{25,25},{2,2},{10,... | collective-permute-start | bytes 3145736 | tf_op jit(solution)/shard_map/ppermute | solution.py:87
  9.6 21.9 %collective-permute-start.5 = (bf16[256,1024]{1,0:T(8,128)(2,1)S(1)}, bf16[256,1024]{1,0:T(8,128)(2,1)S(1)}, u32[]{:S(2)}, u32[]{:S(2)}) collective-permute-start(bf16[256,1024]{1,0:T(8,128)(2,1)S(1)} %get-tuple-element.34), channel_id=1, source_target_pairs={{0,8},{8,0},{16,24},{24,16},{1,9},{9,1},{17,25},{25,17},{2,10},{10... | collective-permute-start | bytes 1572872 | tf_op jit(solution)/shard_map/ppermute | solution.py:87
  20.7 10.8 %collective-permute-start.6 = (bf16[256,1024]{1,0:T(8,128)(2,1)S(1)}, bf16[256,1024]{1,0:T(8,128)(2,1)S(1)}, u32[]{:S(2)}, u32[]{:S(2)}) collective-permute-start(bf16[256,1024]{1,0:T(8,128)(2,1)S(1)} %collective-permute-done.4.refs_0_), channel_id=1, source_target_pairs={{0,1},{1,0},{2,3},{3,2},{4,5},{5,4},{6,7},{7,6},{8,9},{9,8},{10,11... | collective-permute-start | bytes 1572872 | tf_op jit(solution)/shard_map/ppermute | solution.py:91
  31.4 3.7 %collective-permute-start.7 = (bf16[256,1024]{1,0:T(8,128)(2,1)S(1)}, bf16[256,1024]{1,0:T(8,128)(2,1)S(1)}, u32[]{:S(2)}, u32[]{:S(2)}) collective-permute-start(bf16[256,1024]{1,0:T(8,128)(2,1)S(1)} %collective-permute-done.5.refs_1_), channel_id=1, source_target_pairs={{0,1},{1,0},{2,3},{3,2},{4,5},{5,4},{6,7},{7,6},{8,9},{9,8},{10,11... | collective-permute-start | bytes 1572872 | tf_op jit(solution)/shard_map/ppermute | solution.py:91
  31.4 7.1 %collective-permute-start.8 = (bf16[256,1024]{1,0:T(8,128)(2,1)S(1)}, bf16[256,1024]{1,0:T(8,128)(2,1)S(1)}, u32[]{:S(2)}, u32[]{:S(2)}) collective-permute-start(bf16[256,1024]{1,0:T(8,128)(2,1)S(1)} %collective-permute-done.4.refs_0_), channel_id=1, source_target_pairs={{0,0},{8,16},{16,8},{24,24},{1,1},{9,17},{17,9},{25,25},{2,2},{10,... | collective-permute-start | bytes 1572872 | tf_op jit(solution)/shard_map/ppermute | solution.py:87
  33.4 9.2 %collective-permute-start.3 = (bf16[512,512]{1,0:T(8,128)(2,1)S(1)}, bf16[512,512]{1,0:T(8,128)(2,1)S(1)}, u32[]{:S(2)}, u32[]{:S(2)}) collective-permute-start(bf16[512,512]{1,0:T(8,128)(2,1)S(1)} %get-tuple-element.32), channel_id=1, source_target_pairs={{0,2},{1,5},{2,0},{3,7},{4,6},{5,1},{6,4},{7,3},{8,10},{9,13},{10,... | collective-permute-start | bytes 1572872 | tf_op jit(solution)/shard_map/ppermute | solution.py:95
  37.4 13.7 %collective-permute-start.10 = (bf16[512,512]{1,0:T(8,128)(2,1)S(1)}, bf16[512,512]{1,0:T(8,128)(2,1)S(1)}, u32[]{:S(2)}, u32[]{:S(2)}) collective-permute-start(bf16[512,512]{1,0:T(8,128)(2,1)S(1)} %get-tuple-element.42), channel_id=1, source_target_pairs={{0,2},{1,5},{2,0},{3,7},{4,6},{5,1},{6,4},{7,3},{8,10},{9,13},{10,... | collective-permute-start | bytes 1572872 | tf_op jit(solution)/shard_map/ppermute | solution.py:95
  37.8 17.0 %collective-permute-start.13 = (bf16[256,1024]{1,0:T(8,128)(2,1)S(1)}, bf16[256,1024]{1,0:T(8,128)(2,1)S(1)}, u32[]{:S(2)}, u32[]{:S(2)}) collective-permute-start(bf16[256,1024]{1,0:T(8,128)(2,1)S(1)} %collective-permute-done.5.refs_1_), channel_id=1, source_target_pairs={{0,0},{8,16},{16,8},{24,24},{1,1},{9,17},{17,9},{25,25},{2,2},{10,... | collective-permute-start | bytes 1572872 | tf_op jit(solution)/shard_map/ppermute | solution.py:87
  43.0 14.4 %collective-permute-start.9 = (bf16[256,512]{1,0:T(8,128)(2,1)S(1)}, bf16[256,512]{1,0:T(8,128)(2,1)S(1)}, u32[]{:S(2)}, u32[]{:S(2)}) collective-permute-start(bf16[256,512]{1,0:T(8,128)(2,1)S(1)} %slice.120), channel_id=1, source_target_pairs={{0,4},{1,3},{2,6},{3,1},{4,0},{5,7},{6,2},{7,5},{8,12},{9,11},{10,... | collective-permute-start | bytes 786440 | tf_op jit(solution)/shard_map/ppermute | solution.py:95
  44.7 21.0 %collective-permute-start.15 = (bf16[1024,256]{1,0:T(8,128)(2,1)S(1)}, bf16[1024,256]{1,0:T(8,128)(2,1)S(1)}, u32[]{:S(2)}, u32[]{:S(2)}) collective-permute-start(bf16[1024,256]{1,0:T(8,128)(2,1)S(1)} %get-tuple-element.47), channel_id=1, source_target_pairs={{0,2},{1,5},{2,0},{3,7},{4,6},{5,1},{6,4},{7,3},{8,10},{9,13},{10,... | collective-permute-start | bytes 1572872 | tf_op jit(solution)/shard_map/ppermute | solution.py:95
  51.3 10.6 %collective-permute-start.12 = (bf16[256,512]{1,0:T(8,128)(2,1)S(1)}, bf16[256,512]{1,0:T(8,128)(2,1)S(1)}, u32[]{:S(2)}, u32[]{:S(2)}) collective-permute-start(bf16[256,512]{1,0:T(8,128)(2,1)S(1)} %get-tuple-element.63), channel_id=1, source_target_pairs={{0,12},{1,11},{2,14},{3,9},{4,8},{5,15},{6,10},{7,13},{8,4},{9,3},... | collective-permute-start | bytes 786440 | tf_op jit(solution)/shard_map/ppermute | solution.py:101
  54.7 11.0 %collective-permute-start.11 = (bf16[256,512]{1,0:T(8,128)(2,1)S(1)}, bf16[256,512]{1,0:T(8,128)(2,1)S(1)}, u32[]{:S(2)}, u32[]{:S(2)}) collective-permute-start(bf16[256,512]{1,0:T(8,128)(2,1)S(1)} %get-tuple-element.64), channel_id=1, source_target_pairs={{0,8},{8,0},{16,24},{24,16},{1,9},{9,1},{17,25},{25,17},{2,10},{10... | collective-permute-start | bytes 786440 | tf_op jit(solution)/shard_map/ppermute | solution.py:87
  56.1 17.5 %collective-permute-start.20 = (bf16[1024,256]{1,0:T(8,128)(2,1)S(1)}, bf16[1024,256]{1,0:T(8,128)(2,1)S(1)}, u32[]{:S(2)}, u32[]{:S(2)}) collective-permute-start(bf16[1024,256]{1,0:T(8,128)(2,1)S(1)} %get-tuple-element.49), channel_id=1, source_target_pairs={{0,2},{1,5},{2,0},{3,7},{4,6},{5,1},{6,4},{7,3},{8,10},{9,13},{10,... | collective-permute-start | bytes 1572872 | tf_op jit(solution)/shard_map/ppermute | solution.py:95
  65.9 6.3 %collective-permute-start.18 = (bf16[256,256]{1,0:T(8,128)(2,1)S(1)}, bf16[256,256]{1,0:T(8,128)(2,1)S(1)}, u32[]{:S(2)}, u32[]{:S(2)}) collective-permute-start(bf16[256,256]{1,0:T(8,128)(2,1)S(1)} %get-tuple-element.60), channel_id=1, source_target_pairs={{0,12},{1,11},{2,14},{3,9},{4,8},{5,15},{6,10},{7,13},{8,4},{9,3},... | collective-permute-start | bytes 393224 | tf_op jit(solution)/shard_map/ppermute | solution.py:101
  68.5 5.0 %collective-permute-start.17 = (bf16[256,256]{1,0:T(8,128)(2,1)S(1)}, bf16[256,256]{1,0:T(8,128)(2,1)S(1)}, u32[]{:S(2)}, u32[]{:S(2)}) collective-permute-start(bf16[256,256]{1,0:T(8,128)(2,1)S(1)} %get-tuple-element.61), channel_id=1, source_target_pairs={{0,8},{8,0},{16,24},{24,16},{1,9},{9,1},{17,25},{25,17},{2,10},{10... | collective-permute-start | bytes 393224 | tf_op jit(solution)/shard_map/ppermute | solution.py:87
  68.6 5.1 %collective-permute-start.16 = (bf16[256,256]{1,0:T(8,128)(2,1)S(1)}, bf16[256,256]{1,0:T(8,128)(2,1)S(1)}, u32[]{:S(2)}, u32[]{:S(2)}) collective-permute-start(bf16[256,256]{1,0:T(8,128)(2,1)S(1)} %get-tuple-element.62), channel_id=1, source_target_pairs={{0,4},{1,3},{2,6},{3,1},{4,0},{5,7},{6,2},{7,5},{8,12},{9,11},{10,... | collective-permute-start | bytes 393224 | tf_op jit(solution)/shard_map/ppermute | solution.py:95
  69.4 12.6 %collective-permute-start.14 = (bf16[512,512]{1,0:T(8,128)(2,1)S(1)}, bf16[512,512]{1,0:T(8,128)(2,1)S(1)}, u32[]{:S(2)}, u32[]{:S(2)}) collective-permute-start(bf16[512,512]{1,0:T(8,128)(2,1)S(1)} %pad_maximum_fusion), channel_id=1, source_target_pairs={{0,1},{1,0},{2,3},{3,2},{4,5},{5,4},{6,7},{7,6},{8,9},{9,8},{10,11... | collective-permute-start | bytes 1572872 | tf_op jit(solution)/shard_map/ppermute | solution.py:91
  73.8 9.7 %copy-start.1 = (f32[1,128,4096]{2,1,0:T(8,128)S(1)}, f32[1,128,4096]{2,1,0:T(8,128)}, u32[]{:S(2)}) copy-start(f32[1,128,4096]{2,1,0:T(8,128)} %param.8) | copy-start | bytes 6291460
  73.8 6.7 %collective-permute-start.23 = (bf16[256,256]{1,0:T(8,128)(2,1)S(1)}, bf16[256,256]{1,0:T(8,128)(2,1)S(1)}, u32[]{:S(2)}, u32[]{:S(2)}) collective-permute-start(bf16[256,256]{1,0:T(8,128)(2,1)S(1)} %get-tuple-element.57), channel_id=1, source_target_pairs={{0,12},{1,11},{2,14},{3,9},{4,8},{5,15},{6,10},{7,13},{8,4},{9,3},... | collective-permute-start | bytes 393224 | tf_op jit(solution)/shard_map/ppermute | solution.py:101
  76.2 5.4 %collective-permute-start.22 = (bf16[256,256]{1,0:T(8,128)(2,1)S(1)}, bf16[256,256]{1,0:T(8,128)(2,1)S(1)}, u32[]{:S(2)}, u32[]{:S(2)}) collective-permute-start(bf16[256,256]{1,0:T(8,128)(2,1)S(1)} %get-tuple-element.58), channel_id=1, source_target_pairs={{0,8},{8,0},{16,24},{24,16},{1,9},{9,1},{17,25},{25,17},{2,10},{10... | collective-permute-start | bytes 393224 | tf_op jit(solution)/shard_map/ppermute | solution.py:87
  76.5 5.4 %collective-permute-start.21 = (bf16[256,256]{1,0:T(8,128)(2,1)S(1)}, bf16[256,256]{1,0:T(8,128)(2,1)S(1)}, u32[]{:S(2)}, u32[]{:S(2)}) collective-permute-start(bf16[256,256]{1,0:T(8,128)(2,1)S(1)} %get-tuple-element.59), channel_id=1, source_target_pairs={{0,4},{1,3},{2,6},{3,1},{4,0},{5,7},{6,2},{7,5},{8,12},{9,11},{10,... | collective-permute-start | bytes 393224 | tf_op jit(solution)/shard_map/ppermute | solution.py:95
  77.4 4.7 %collective-permute-start.19 = (bf16[512,256]{1,0:T(8,128)(2,1)S(1)}, bf16[512,256]{1,0:T(8,128)(2,1)S(1)}, u32[]{:S(2)}, u32[]{:S(2)}) collective-permute-start(bf16[512,256]{1,0:T(8,128)(2,1)S(1)} %pad_maximum_fusion.1), channel_id=1, source_target_pairs={{0,1},{1,0},{2,3},{3,2},{4,5},{5,4},{6,7},{7,6},{8,9},{9,8},{10,11... | collective-permute-start | bytes 786440 | tf_op jit(solution)/shard_map/ppermute | solution.py:91
  81.9 1.6 %collective-permute-start.24 = (bf16[512,256]{1,0:T(8,128)(2,1)S(1)}, bf16[512,256]{1,0:T(8,128)(2,1)S(1)}, u32[]{:S(2)}, u32[]{:S(2)}) collective-permute-start(bf16[512,256]{1,0:T(8,128)(2,1)S(1)} %pad_maximum_fusion.2), channel_id=1, source_target_pairs={{0,1},{1,0},{2,3},{3,2},{4,5},{5,4},{6,7},{7,6},{8,9},{9,8},{10,11... | collective-permute-start | bytes 786440 | tf_op jit(solution)/shard_map/ppermute | solution.py:91

commit v5 on v4

--- a/solution.py
+++ b/solution.py
@@ -228,6 +228,8 @@
     half = out_ref.shape[1] // 2
     base = jnp.bitwise_or((row & 1) * 2, row >> 1)
     position = 0
+    tile = out_ref.shape[0]
+    rows = aligned(pl.program_id(0), tile)
     for which, first, count, terms in plan:
         mine = refs[position : position + terms]
         other = refs[position + terms]
@@ -237,11 +239,14 @@
             for block in range(count):
                 source = pl.ds(block * height, height)
                 for side in range(2):
-                    tiles = [other[pl.ds(k * height, height), source] if side else mine[k][:height, source] for k in wanted]
+                    if side:
+                        tiles = [other[aligned(k * (height // tile) + pl.program_id(0), tile), source] for k in wanted]
+                    else:
+                        tiles = [mine[k][rows, source] for k in wanted]
                     total = sum(tile.astype(F32) for tile in tiles)
                     place = (1 - core if side else core) * half + (first + block) * width + at * height
                     place = pl.ds(pl.multiple_of(place, height), height)
-                    out_ref[:, place] = anc_ref[:, place] - total
+                    out_ref[:, place] = anc_ref[rows, place] - total
 
 
 def paired_body(panel_blocks, factor_inverse, target_rows, owner_order, ancestor_rows):
@@ -306,12 +311,18 @@
     other3 = core_swap(packed3)
     blocks = [count // height for count in pieces]
     plan = ((0, 0, half // height, len(terms1)), (1, 0, blocks[0], len(terms2)), (1, blocks[0], blocks[1], len(terms3)))
-    (result,) = local_call(
+    operands = [ancestor_rows[0], *terms1, other1, *terms2, other2, *terms3, other3]
+    columns = ancestor_rows.shape[2]
+    result = pl.pallas_call(
         functools.partial(finish_kernel, height, plan),
-        [ancestor_rows[0], *terms1, other1, *terms2, other2, *terms3, other3],
-        [(ancestor_rows.shape[1:], F32)],
-        "finish",
-    )
+        grid=(2,),
+        in_specs=[pl.BlockSpec(memory_space=pltpu.VMEM)] * len(operands),
+        out_specs=pl.BlockSpec((height // 2, columns), lambda i: (i, 0)),
+        out_shape=jax.ShapeDtypeStruct((height, columns), F32),
+        cost_estimate=HINT,
+        compiler_params=pltpu.CompilerParams(vmem_limit_bytes=VMEM_LIMIT),
+        name="finish",
+    )(*operands)
     return result[None]
 
 

time: 85.8 us -> 85.4 us (level)
    pallas_call x10 -> x9, Pallas kernels: 10.1 us -> 8 us  [local_call(): pl.pallas_call(kernel, in_specs=[pl.BlockSpec(memory_space=pltpu.SMEM)] *...]
    pallas_call x0 -> x1, Pallas kernels: none -> 1.7 us  [paired_body(): pl.pallas_call(functools.partial(finish_kernel, height, plan), grid=(2,),...]
where the time goes in v5:
time: 85.4 us; the launch traced here: 85.2 us
  waiting for transfers between devices  44.5 us (52%)
  starting transfers between devices  27.5 us (32%)
  Pallas kernels  9.7 us (11%)
  local copies, waits for them, and re-layouts  2.54 us (3%)
    ppermute x8, waiting for transfers between devices, row_swap(): return lax.ppermute(value, 'row', list(enumerate(partner)))  23.5 us
    ppermute x3, waiting for transfers between devices, both_swap(): return lax.ppermute(value, ('row', 'col'), pairs)  10.4 us
    ppermute x8, starting transfers between devices, row_swap(): return lax.ppermute(value, 'row', list(enumerate(partner)))  9.94 us
    ppermute x7, starting transfers between devices, hop_swap(): lax.ppermute(value, 'col', [(i, i ^ hops[i & CORE]) for i in range(lax.ax...  8.49 us
    ppermute x3, starting transfers between devices, both_swap(): return lax.ppermute(value, ('row', 'col'), pairs)  8.34 us
    ppermute x7, waiting for transfers between devices, hop_swap(): lax.ppermute(value, 'col', [(i, i ^ hops[i & CORE]) for i in range(lax.ax...  8.21 us
    pallas_call x9, Pallas kernels, local_call(): pl.pallas_call(kernel, in_specs=[pl.BlockSpec(memory_space=pltpu.SMEM)] *...  8 us
    ppermute x7, waiting for transfers between devices, core_swap(): lax.ppermute(value, 'col', [(i, i ^ CORE) for i in range(lax.axis_size('c...  2.4 us
  transfers between devices with their start and end apart: 25, of which 14 were waited for; matrix products, arithmetic and copies ran while one was open for 1% of the time, Pallas kernels for 9%

profile of v5, /device:TPU:0, one launch (start us, length us, event | category | flops | bytes accessed | tf_op | source)
XLA Modules:
  0.0 85.2 jit_solution(8476201119214815561)
XLA Ops:
  0.0 1.2 %copy-done = bf16[1,8,128,512]{3,2,1,0:T(8,128)(2,1)S(1)} copy-done((bf16[1,8,128,512]{3,2,1,0:T(8,128)(2,1)S(1)}, bf16[1,8,128,512]{3,2,1,0:T(8,128)(2,1)}, u32[]{:S(2)}) %copy-start) | copy-done | bytes 1048600
  1.2 1.0 %copy-done.2 = bf16[1,512,512]{2,1,0:T(8,128)(2,1)S(1)} copy-done((bf16[1,512,512]{2,1,0:T(8,128)(2,1)S(1)}, bf16[1,512,512]{2,1,0:T(8,128)(2,1)}, u32[]{:S(2)}) %copy-start.2) | copy-done | bytes 524312
  2.3 0.5 solve.2.give_ref
  2.8 0.5 collective-permute-start
  3.3 0.5 solve.3.rest_ref
  3.7 0.1 collective-permute-start.1
  3.9 0.9 %collective-permute-done.got_ref = bf16[512,512]{1,0:T(8,128)(2,1)S(1)} collective-permute-done((bf16[512,512]{1,0:T(8,128)(2,1)S(1)}, bf16[512,512]{1,0:T(8,128)(2,1)S(1)}, u32[]{:S(2)}, u32[]{:S(2)}) %collective-permute-start) | collective-permute-done | bytes 524320 | tf_op jit(solution)/shard_map/ppermute | solution.py:91
  4.8 0.1 join.1
  5.0 3.0 %collective-permute-start.4 = (bf16[256,1024]{1,0:T(8,128)(2,1)S(1)}, bf16[256,1024]{1,0:T(8,128)(2,1)S(1)}, u32[]{:S(2)}, u32[]{:S(2)}) collective-permute-start(bf16[256,1024]{1,0:T(8,128)(2,1)S(1)} %get-tuple-element.33), channel_id=1, source_target_pairs={{0,8},{8,0},{16,24},{24,16},{1,9},{9,1},{17,25},{25,17},{2,10},{10... | collective-permute-start | bytes 1572872 | tf_op jit(solution)/shard_map/ppermute | solution.py:87
  8.0 0.8 pick_own.1.refs_0_
  8.8 0.7 collective-permute-start.2
  9.6 4.4 %collective-permute-start.5 = (bf16[256,1024]{1,0:T(8,128)(2,1)S(1)}, bf16[256,1024]{1,0:T(8,128)(2,1)S(1)}, u32[]{:S(2)}, u32[]{:S(2)}) collective-permute-start(bf16[256,1024]{1,0:T(8,128)(2,1)S(1)} %get-tuple-element.34), channel_id=1, source_target_pairs={{0,8},{8,0},{16,24},{24,16},{1,9},{9,1},{17,25},{25,17},{2,10},{10... | collective-permute-start | bytes 1572872 | tf_op jit(solution)/shard_map/ppermute | solution.py:87
  14.0 6.7 %collective-permute-done.4.refs_0_ = bf16[256,1024]{1,0:T(8,128)(2,1)S(1)} collective-permute-done((bf16[256,1024]{1,0:T(8,128)(2,1)S(1)}, bf16[256,1024]{1,0:T(8,128)(2,1)S(1)}, u32[]{:S(2)}, u32[]{:S(2)}) %collective-permute-start.4) | collective-permute-done | bytes 524320 | tf_op jit(solution)/shard_map/ppermute | solution.py:87
  20.7 10.7 %collective-permute-done.5.refs_1_ = bf16[256,1024]{1,0:T(8,128)(2,1)S(1)} collective-permute-done((bf16[256,1024]{1,0:T(8,128)(2,1)S(1)}, bf16[256,1024]{1,0:T(8,128)(2,1)S(1)}, u32[]{:S(2)}, u32[]{:S(2)}) %collective-permute-start.5) | collective-permute-done | bytes 524320 | tf_op jit(solution)/shard_map/ppermute | solution.py:87
  31.4 0.7 collective-permute-start.8
  32.1 1.3 %products.4 = (f32[512,512]{1,0:T(8,128)S(1)}, bf16[512,512]{1,0:T(8,128)(2,1)S(1)}) custom-call(bf16[1024,1024]{1,0:T(8,128)(2,1)S(1)} %pick_own.1.refs_0_, bf16[512,1024]{1,0:T(8,128)(2,1)S(1)} %collective-permute-done.2.refs_1_), custom_call_target="tpu_custom_call" | custom-call | flops 1 | bytes 1 | tf_op jit(solution)/shard_map/products/pallas_call | solution.py:114
  33.4 1.7 %collective-permute-start.3 = (bf16[512,512]{1,0:T(8,128)(2,1)S(1)}, bf16[512,512]{1,0:T(8,128)(2,1)S(1)}, u32[]{:S(2)}, u32[]{:S(2)}) collective-permute-start(bf16[512,512]{1,0:T(8,128)(2,1)S(1)} %get-tuple-element.32), channel_id=1, source_target_pairs={{0,2},{1,5},{2,0},{3,7},{4,6},{5,1},{6,4},{7,3},{8,10},{9,13},{10,... | collective-permute-start | bytes 1572872 | tf_op jit(solution)/shard_map/ppermute | solution.py:95
  35.2 0.9 %pick_pair.1.refs_0_.refs_1_ = bf16[1024,1024]{1,0:T(8,128)(2,1)S(1)} custom-call(s32[8]{0:T(128)S(1)} %copy-done.3, bf16[256,1024]{1,0:T(8,128)(2,1)S(1)} %collective-permute-done.4.refs_0_, bf16[256,1024]{1,0:T(8,128)(2,1)S(1)} %collective-permute-done.5.refs_1_, bf16[256,1024]{1,0:T(8,128)(2,1)S(1)} %collective-permute-done.6.refs_2_, ...), custom_call_target="tpu_custom_call" | custom-call | flops 1 | bytes 1 | tf_op jit(solution)/shard_map/pick_pair/pallas_call | solution.py:114
  36.1 1.3 %products.5 = (f32[512,512]{1,0:T(8,128)S(1)}, bf16[512,512]{1,0:T(8,128)(2,1)S(1)}) custom-call(bf16[1024,1024]{1,0:T(8,128)(2,1)S(1)} %pick_pair.1.refs_0_.refs_1_, bf16[512,1024]{1,0:T(8,128)(2,1)S(1)} %collective-permute-done.2.refs_1_), custom_call_target="tpu_custom_call" | custom-call | flops 1 | bytes 1 | tf_op jit(solution)/shard_map/products/pallas_call | solution.py:114
  37.4 0.4 collective-permute-start.10
  37.8 0.7 collective-permute-start.13
  38.5 1.3 %products.6 = (f32[1024,256]{1,0:T(8,128)S(1)}, bf16[1024,256]{1,0:T(8,128)(2,1)S(1)}) custom-call(bf16[1024,1024]{1,0:T(8,128)(2,1)S(1)} %pick_own.1.refs_0_, bf16[1024,1024]{1,0:T(8,128)(2,1)S(1)} %pick_pair.1.refs_0_.refs_1_, bf16[256,1024]{1,0:T(8,128)(2,1)S(1)} %collective-permute-done.8.refs_2_), custom_call_target="tpu_custom_call" | custom-call | flops 1 | bytes 1 | tf_op jit(solution)/shard_map/products/pallas_call | solution.py:114
  39.8 2.9 %collective-permute-done.3 = bf16[512,512]{1,0:T(8,128)(2,1)S(1)} collective-permute-done((bf16[512,512]{1,0:T(8,128)(2,1)S(1)}, bf16[512,512]{1,0:T(8,128)(2,1)S(1)}, u32[]{:S(2)}, u32[]{:S(2)}) %collective-permute-start.3) | collective-permute-done | bytes 524320 | tf_op jit(solution)/shard_map/ppermute | solution.py:95
  42.7 0.2 fusion.2
  43.0 1.7 %collective-permute-start.9 = (bf16[256,512]{1,0:T(8,128)(2,1)S(1)}, bf16[256,512]{1,0:T(8,128)(2,1)S(1)}, u32[]{:S(2)}, u32[]{:S(2)}) collective-permute-start(bf16[256,512]{1,0:T(8,128)(2,1)S(1)} %slice.120), channel_id=1, source_target_pairs={{0,4},{1,3},{2,6},{3,1},{4,0},{5,7},{6,2},{7,5},{8,12},{9,11},{10,... | collective-permute-start | bytes 786440 | tf_op jit(solution)/shard_map/ppermute | solution.py:95
  44.7 1.5 %collective-permute-start.15 = (bf16[1024,256]{1,0:T(8,128)(2,1)S(1)}, bf16[1024,256]{1,0:T(8,128)(2,1)S(1)}, u32[]{:S(2)}, u32[]{:S(2)}) collective-permute-start(bf16[1024,256]{1,0:T(8,128)(2,1)S(1)} %get-tuple-element.47), channel_id=1, source_target_pairs={{0,2},{1,5},{2,0},{3,7},{4,6},{5,1},{6,4},{7,3},{8,10},{9,13},{10,... | collective-permute-start | bytes 1572872 | tf_op jit(solution)/shard_map/ppermute | solution.py:95
  46.2 4.9 %collective-permute-done.10 = bf16[512,512]{1,0:T(8,128)(2,1)S(1)} collective-permute-done((bf16[512,512]{1,0:T(8,128)(2,1)S(1)}, bf16[512,512]{1,0:T(8,128)(2,1)S(1)}, u32[]{:S(2)}, u32[]{:S(2)}) %collective-permute-start.10) | collective-permute-done | bytes 524320 | tf_op jit(solution)/shard_map/ppermute | solution.py:95
  51.1 0.2 add_convert_fusion
  51.3 3.3 %collective-permute-start.12 = (bf16[256,512]{1,0:T(8,128)(2,1)S(1)}, bf16[256,512]{1,0:T(8,128)(2,1)S(1)}, u32[]{:S(2)}, u32[]{:S(2)}) collective-permute-start(bf16[256,512]{1,0:T(8,128)(2,1)S(1)} %get-tuple-element.63), channel_id=1, source_target_pairs={{0,12},{1,11},{2,14},{3,9},{4,8},{5,15},{6,10},{7,13},{8,4},{9,3},... | collective-permute-start | bytes 786440 | tf_op jit(solution)/shard_map/ppermute | solution.py:101
  54.7 0.1 collective-permute-start.11
  54.8 1.3 %products.7 = (f32[1024,256]{1,0:T(8,128)S(1)}, bf16[1024,256]{1,0:T(8,128)(2,1)S(1)}) custom-call(bf16[1024,1024]{1,0:T(8,128)(2,1)S(1)} %pick_own.1.refs_0_, bf16[1024,1024]{1,0:T(8,128)(2,1)S(1)} %pick_pair.1.refs_0_.refs_1_, bf16[256,1024]{1,0:T(8,128)(2,1)S(1)} %collective-permute-done.13.refs_2_), custom_call_target="tpu_custom_call" | custom-call | flops 1 | bytes 1 | tf_op jit(solution)/shard_map/products/pallas_call | solution.py:114
  56.1 1.3 %collective-permute-start.20 = (bf16[1024,256]{1,0:T(8,128)(2,1)S(1)}, bf16[1024,256]{1,0:T(8,128)(2,1)S(1)}, u32[]{:S(2)}, u32[]{:S(2)}) collective-permute-start(bf16[1024,256]{1,0:T(8,128)(2,1)S(1)} %get-tuple-element.49), channel_id=1, source_target_pairs={{0,2},{1,5},{2,0},{3,7},{4,6},{5,1},{6,4},{7,3},{8,10},{9,13},{10,... | collective-permute-start | bytes 1572872 | tf_op jit(solution)/shard_map/ppermute | solution.py:95
  57.4 4.5 %collective-permute-done.12.refs_3_ = bf16[256,512]{1,0:T(8,128)(2,1)S(1)} collective-permute-done((bf16[256,512]{1,0:T(8,128)(2,1)S(1)}, bf16[256,512]{1,0:T(8,128)(2,1)S(1)}, u32[]{:S(2)}, u32[]{:S(2)}) %collective-permute-start.12) | collective-permute-done | bytes 262176 | tf_op jit(solution)/shard_map/ppermute | solution.py:101
  61.9 3.7 %collective-permute-done.11.refs_2_ = bf16[256,512]{1,0:T(8,128)(2,1)S(1)} collective-permute-done((bf16[256,512]{1,0:T(8,128)(2,1)S(1)}, bf16[256,512]{1,0:T(8,128)(2,1)S(1)}, u32[]{:S(2)}, u32[]{:S(2)}) %collective-permute-start.11) | collective-permute-done | bytes 262176 | tf_op jit(solution)/shard_map/ppermute | solution.py:87
  65.7 0.1 fusion.1
  65.9 2.7 %collective-permute-start.18 = (bf16[256,256]{1,0:T(8,128)(2,1)S(1)}, bf16[256,256]{1,0:T(8,128)(2,1)S(1)}, u32[]{:S(2)}, u32[]{:S(2)}) collective-permute-start(bf16[256,256]{1,0:T(8,128)(2,1)S(1)} %get-tuple-element.60), channel_id=1, source_target_pairs={{0,12},{1,11},{2,14},{3,9},{4,8},{5,15},{6,10},{7,13},{8,4},{9,3},... | collective-permute-start | bytes 393224 | tf_op jit(solution)/shard_map/ppermute | solution.py:101
  68.6 0.9 %collective-permute-start.16 = (bf16[256,256]{1,0:T(8,128)(2,1)S(1)}, bf16[256,256]{1,0:T(8,128)(2,1)S(1)}, u32[]{:S(2)}, u32[]{:S(2)}) collective-permute-start(bf16[256,256]{1,0:T(8,128)(2,1)S(1)} %get-tuple-element.62), channel_id=1, source_target_pairs={{0,4},{1,3},{2,6},{3,1},{4,0},{5,7},{6,2},{7,5},{8,12},{9,11},{10,... | collective-permute-start | bytes 393224 | tf_op jit(solution)/shard_map/ppermute | solution.py:95
  69.4 2.8 %collective-permute-done.18.refs_8_ = bf16[256,256]{1,0:T(8,128)(2,1)S(1)} collective-permute-done((bf16[256,256]{1,0:T(8,128)(2,1)S(1)}, bf16[256,256]{1,0:T(8,128)(2,1)S(1)}, u32[]{:S(2)}, u32[]{:S(2)}) %collective-permute-start.18) | collective-permute-done | bytes 131104 | tf_op jit(solution)/shard_map/ppermute | solution.py:101
  72.2 1.3 %collective-permute-done.17.refs_7_ = bf16[256,256]{1,0:T(8,128)(2,1)S(1)} collective-permute-done((bf16[256,256]{1,0:T(8,128)(2,1)S(1)}, bf16[256,256]{1,0:T(8,128)(2,1)S(1)}, u32[]{:S(2)}, u32[]{:S(2)}) %collective-permute-start.17) | collective-permute-done | bytes 131104 | tf_op jit(solution)/shard_map/ppermute | solution.py:87
  73.6 0.1 fusion
  73.8 2.3 %collective-permute-start.23 = (bf16[256,256]{1,0:T(8,128)(2,1)S(1)}, bf16[256,256]{1,0:T(8,128)(2,1)S(1)}, u32[]{:S(2)}, u32[]{:S(2)}) collective-permute-start(bf16[256,256]{1,0:T(8,128)(2,1)S(1)} %get-tuple-element.57), channel_id=1, source_target_pairs={{0,12},{1,11},{2,14},{3,9},{4,8},{5,15},{6,10},{7,13},{8,4},{9,3},... | collective-permute-start | bytes 393224 | tf_op jit(solution)/shard_map/ppermute | solution.py:101
  76.2 0.3 collective-permute-start.22
  76.5 0.9 %collective-permute-start.21 = (bf16[256,256]{1,0:T(8,128)(2,1)S(1)}, bf16[256,256]{1,0:T(8,128)(2,1)S(1)}, u32[]{:S(2)}, u32[]{:S(2)}) collective-permute-start(bf16[256,256]{1,0:T(8,128)(2,1)S(1)} %get-tuple-element.59), channel_id=1, source_target_pairs={{0,4},{1,3},{2,6},{3,1},{4,0},{5,7},{6,2},{7,5},{8,12},{9,11},{10,... | collective-permute-start | bytes 393224 | tf_op jit(solution)/shard_map/ppermute | solution.py:95
  77.4 3.1 %collective-permute-done.23.refs_13_ = bf16[256,256]{1,0:T(8,128)(2,1)S(1)} collective-permute-done((bf16[256,256]{1,0:T(8,128)(2,1)S(1)}, bf16[256,256]{1,0:T(8,128)(2,1)S(1)}, u32[]{:S(2)}, u32[]{:S(2)}) %collective-permute-start.23) | collective-permute-done | bytes 131104 | tf_op jit(solution)/shard_map/ppermute | solution.py:101
  80.5 1.0 %collective-permute-done.22.refs_12_ = bf16[256,256]{1,0:T(8,128)(2,1)S(1)} collective-permute-done((bf16[256,256]{1,0:T(8,128)(2,1)S(1)}, bf16[256,256]{1,0:T(8,128)(2,1)S(1)}, u32[]{:S(2)}, u32[]{:S(2)}) %collective-permute-start.22) | collective-permute-done | bytes 131104 | tf_op jit(solution)/shard_map/ppermute | solution.py:87
  81.5 0.4 collective-permute-done.21.refs_11_
  82.1 1.4 %collective-permute-done.24.refs_14_ = bf16[512,256]{1,0:T(8,128)(2,1)S(1)} collective-permute-done((bf16[512,256]{1,0:T(8,128)(2,1)S(1)}, bf16[512,256]{1,0:T(8,128)(2,1)S(1)}, u32[]{:S(2)}, u32[]{:S(2)}) %collective-permute-start.24) | collective-permute-done | bytes 262176 | tf_op jit(solution)/shard_map/ppermute | solution.py:91
  83.5 1.7 %finish.1 = f32[128,4096]{1,0:T(8,128)} custom-call(f32[128,4096]{1,0:T(8,128)S(1)} %bitcast.6, f32[256,512]{1,0:T(8,128)S(1)} %slice.119.refs_0_, bf16[256,512]{1,0:T(8,128)(2,1)S(1)} %collective-permute-done.9.refs_1_, bf16[256,512]{1,0:T(8,128)(2,1)S(1)} %collective-permute-done.11.refs_2_, bf16[256,512]{1,0:T(8,128)(2,1)S(1)} %collective-permute-done.12.refs_3_, ...), custom_call_target="tpu_custom_call" | custom-call | flops 1 | bytes 1 | tf_op jit(solution)/shard_map/finish/pallas_call | solution.py:316
  (46 shorter events, 0.6 us)
Async XLA Ops:
  0.0 1.2 %copy-start = (bf16[1,8,128,512]{3,2,1,0:T(8,128)(2,1)S(1)}, bf16[1,8,128,512]{3,2,1,0:T(8,128)(2,1)}, u32[]{:S(2)}) copy-start(bf16[1,8,128,512]{3,2,1,0:T(8,128)(2,1)} %param.5) | copy-start | bytes 3145732
  1.2 1.0 %copy-start.2 = (bf16[1,512,512]{2,1,0:T(8,128)(2,1)S(1)}, bf16[1,512,512]{2,1,0:T(8,128)(2,1)}, u32[]{:S(2)}) copy-start(bf16[1,512,512]{2,1,0:T(8,128)(2,1)} %param.6) | copy-start | bytes 1572868
  2.7 5.2 %copy-start.3 = (s32[8]{0:T(128)S(1)}, s32[8]{0:T(128)}, u32[]{:S(2)}) copy-start(s32[8]{0:T(128)} %order_ref.3) | copy-start | bytes 100
  2.8 2.1 %collective-permute-start = (bf16[512,512]{1,0:T(8,128)(2,1)S(1)}, bf16[512,512]{1,0:T(8,128)(2,1)S(1)}, u32[]{:S(2)}, u32[]{:S(2)}) collective-permute-start(bf16[512,512]{1,0:T(8,128)(2,1)S(1)} %solve.2.give_ref), channel_id=1, source_target_pairs={{0,1},{1,0},{2,3},{3,2},{4,5},{5,4},{6,7},{7,6},{8,9},{9,8},{10,11... | collective-permute-start | bytes 1572872 | tf_op jit(solution)/shard_map/ppermute | solution.py:91
  3.7 4.2 %collective-permute-start.1 = (bf16[512,512]{1,0:T(8,128)(2,1)S(1)}, bf16[512,512]{1,0:T(8,128)(2,1)S(1)}, u32[]{:S(2)}, u32[]{:S(2)}) collective-permute-start(bf16[512,512]{1,0:T(8,128)(2,1)S(1)} %solve.3.rest_ref), channel_id=1, source_target_pairs={{0,1},{1,0},{2,3},{3,2},{4,5},{5,4},{6,7},{7,6},{8,9},{9,8},{10,11... | collective-permute-start | bytes 1572872 | tf_op jit(solution)/shard_map/ppermute | solution.py:91
  5.0 15.7 %collective-permute-start.4 = (bf16[256,1024]{1,0:T(8,128)(2,1)S(1)}, bf16[256,1024]{1,0:T(8,128)(2,1)S(1)}, u32[]{:S(2)}, u32[]{:S(2)}) collective-permute-start(bf16[256,1024]{1,0:T(8,128)(2,1)S(1)} %get-tuple-element.33), channel_id=1, source_target_pairs={{0,8},{8,0},{16,24},{24,16},{1,9},{9,1},{17,25},{25,17},{2,10},{10... | collective-permute-start | bytes 1572872 | tf_op jit(solution)/shard_map/ppermute | solution.py:87
  8.8 23.3 %collective-permute-start.2 = (bf16[512,1024]{1,0:T(8,128)(2,1)S(1)}, bf16[512,1024]{1,0:T(8,128)(2,1)S(1)}, u32[]{:S(2)}, u32[]{:S(2)}) collective-permute-start(bf16[512,1024]{1,0:T(8,128)(2,1)S(1)} %get-tuple-element.30), channel_id=1, source_target_pairs={{0,0},{8,16},{16,8},{24,24},{1,1},{9,17},{17,9},{25,25},{2,2},{10,... | collective-permute-start | bytes 3145736 | tf_op jit(solution)/shard_map/ppermute | solution.py:87
  9.6 21.9 %collective-permute-start.5 = (bf16[256,1024]{1,0:T(8,128)(2,1)S(1)}, bf16[256,1024]{1,0:T(8,128)(2,1)S(1)}, u32[]{:S(2)}, u32[]{:S(2)}) collective-permute-start(bf16[256,1024]{1,0:T(8,128)(2,1)S(1)} %get-tuple-element.34), channel_id=1, source_target_pairs={{0,8},{8,0},{16,24},{24,16},{1,9},{9,1},{17,25},{25,17},{2,10},{10... | collective-permute-start | bytes 1572872 | tf_op jit(solution)/shard_map/ppermute | solution.py:87
  20.7 10.8 %collective-permute-start.6 = (bf16[256,1024]{1,0:T(8,128)(2,1)S(1)}, bf16[256,1024]{1,0:T(8,128)(2,1)S(1)}, u32[]{:S(2)}, u32[]{:S(2)}) collective-permute-start(bf16[256,1024]{1,0:T(8,128)(2,1)S(1)} %collective-permute-done.4.refs_0_), channel_id=1, source_target_pairs={{0,1},{1,0},{2,3},{3,2},{4,5},{5,4},{6,7},{7,6},{8,9},{9,8},{10,11... | collective-permute-start | bytes 1572872 | tf_op jit(solution)/shard_map/ppermute | solution.py:91
  31.4 3.7 %collective-permute-start.7 = (bf16[256,1024]{1,0:T(8,128)(2,1)S(1)}, bf16[256,1024]{1,0:T(8,128)(2,1)S(1)}, u32[]{:S(2)}, u32[]{:S(2)}) collective-permute-start(bf16[256,1024]{1,0:T(8,128)(2,1)S(1)} %collective-permute-done.5.refs_1_), channel_id=1, source_target_pairs={{0,1},{1,0},{2,3},{3,2},{4,5},{5,4},{6,7},{7,6},{8,9},{9,8},{10,11... | collective-permute-start | bytes 1572872 | tf_op jit(solution)/shard_map/ppermute | solution.py:91
  31.4 7.1 %collective-permute-start.8 = (bf16[256,1024]{1,0:T(8,128)(2,1)S(1)}, bf16[256,1024]{1,0:T(8,128)(2,1)S(1)}, u32[]{:S(2)}, u32[]{:S(2)}) collective-permute-start(bf16[256,1024]{1,0:T(8,128)(2,1)S(1)} %collective-permute-done.4.refs_0_), channel_id=1, source_target_pairs={{0,0},{8,16},{16,8},{24,24},{1,1},{9,17},{17,9},{25,25},{2,2},{10,... | collective-permute-start | bytes 1572872 | tf_op jit(solution)/shard_map/ppermute | solution.py:87
  33.4 9.2 %collective-permute-start.3 = (bf16[512,512]{1,0:T(8,128)(2,1)S(1)}, bf16[512,512]{1,0:T(8,128)(2,1)S(1)}, u32[]{:S(2)}, u32[]{:S(2)}) collective-permute-start(bf16[512,512]{1,0:T(8,128)(2,1)S(1)} %get-tuple-element.32), channel_id=1, source_target_pairs={{0,2},{1,5},{2,0},{3,7},{4,6},{5,1},{6,4},{7,3},{8,10},{9,13},{10,... | collective-permute-start | bytes 1572872 | tf_op jit(solution)/shard_map/ppermute | solution.py:95
  37.4 13.7 %collective-permute-start.10 = (bf16[512,512]{1,0:T(8,128)(2,1)S(1)}, bf16[512,512]{1,0:T(8,128)(2,1)S(1)}, u32[]{:S(2)}, u32[]{:S(2)}) collective-permute-start(bf16[512,512]{1,0:T(8,128)(2,1)S(1)} %get-tuple-element.42), channel_id=1, source_target_pairs={{0,2},{1,5},{2,0},{3,7},{4,6},{5,1},{6,4},{7,3},{8,10},{9,13},{10,... | collective-permute-start | bytes 1572872 | tf_op jit(solution)/shard_map/ppermute | solution.py:95
  37.8 17.0 %collective-permute-start.13 = (bf16[256,1024]{1,0:T(8,128)(2,1)S(1)}, bf16[256,1024]{1,0:T(8,128)(2,1)S(1)}, u32[]{:S(2)}, u32[]{:S(2)}) collective-permute-start(bf16[256,1024]{1,0:T(8,128)(2,1)S(1)} %collective-permute-done.5.refs_1_), channel_id=1, source_target_pairs={{0,0},{8,16},{16,8},{24,24},{1,1},{9,17},{17,9},{25,25},{2,2},{10,... | collective-permute-start | bytes 1572872 | tf_op jit(solution)/shard_map/ppermute | solution.py:87
  43.0 14.4 %collective-permute-start.9 = (bf16[256,512]{1,0:T(8,128)(2,1)S(1)}, bf16[256,512]{1,0:T(8,128)(2,1)S(1)}, u32[]{:S(2)}, u32[]{:S(2)}) collective-permute-start(bf16[256,512]{1,0:T(8,128)(2,1)S(1)} %slice.120), channel_id=1, source_target_pairs={{0,4},{1,3},{2,6},{3,1},{4,0},{5,7},{6,2},{7,5},{8,12},{9,11},{10,... | collective-permute-start | bytes 786440 | tf_op jit(solution)/shard_map/ppermute | solution.py:95
  44.7 21.0 %collective-permute-start.15 = (bf16[1024,256]{1,0:T(8,128)(2,1)S(1)}, bf16[1024,256]{1,0:T(8,128)(2,1)S(1)}, u32[]{:S(2)}, u32[]{:S(2)}) collective-permute-start(bf16[1024,256]{1,0:T(8,128)(2,1)S(1)} %get-tuple-element.47), channel_id=1, source_target_pairs={{0,2},{1,5},{2,0},{3,7},{4,6},{5,1},{6,4},{7,3},{8,10},{9,13},{10,... | collective-permute-start | bytes 1572872 | tf_op jit(solution)/shard_map/ppermute | solution.py:95
  51.3 10.6 %collective-permute-start.12 = (bf16[256,512]{1,0:T(8,128)(2,1)S(1)}, bf16[256,512]{1,0:T(8,128)(2,1)S(1)}, u32[]{:S(2)}, u32[]{:S(2)}) collective-permute-start(bf16[256,512]{1,0:T(8,128)(2,1)S(1)} %get-tuple-element.63), channel_id=1, source_target_pairs={{0,12},{1,11},{2,14},{3,9},{4,8},{5,15},{6,10},{7,13},{8,4},{9,3},... | collective-permute-start | bytes 786440 | tf_op jit(solution)/shard_map/ppermute | solution.py:101
  54.7 11.0 %collective-permute-start.11 = (bf16[256,512]{1,0:T(8,128)(2,1)S(1)}, bf16[256,512]{1,0:T(8,128)(2,1)S(1)}, u32[]{:S(2)}, u32[]{:S(2)}) collective-permute-start(bf16[256,512]{1,0:T(8,128)(2,1)S(1)} %get-tuple-element.64), channel_id=1, source_target_pairs={{0,8},{8,0},{16,24},{24,16},{1,9},{9,1},{17,25},{25,17},{2,10},{10... | collective-permute-start | bytes 786440 | tf_op jit(solution)/shard_map/ppermute | solution.py:87
  56.1 17.5 %collective-permute-start.20 = (bf16[1024,256]{1,0:T(8,128)(2,1)S(1)}, bf16[1024,256]{1,0:T(8,128)(2,1)S(1)}, u32[]{:S(2)}, u32[]{:S(2)}) collective-permute-start(bf16[1024,256]{1,0:T(8,128)(2,1)S(1)} %get-tuple-element.49), channel_id=1, source_target_pairs={{0,2},{1,5},{2,0},{3,7},{4,6},{5,1},{6,4},{7,3},{8,10},{9,13},{10,... | collective-permute-start | bytes 1572872 | tf_op jit(solution)/shard_map/ppermute | solution.py:95
  65.9 6.3 %collective-permute-start.18 = (bf16[256,256]{1,0:T(8,128)(2,1)S(1)}, bf16[256,256]{1,0:T(8,128)(2,1)S(1)}, u32[]{:S(2)}, u32[]{:S(2)}) collective-permute-start(bf16[256,256]{1,0:T(8,128)(2,1)S(1)} %get-tuple-element.60), channel_id=1, source_target_pairs={{0,12},{1,11},{2,14},{3,9},{4,8},{5,15},{6,10},{7,13},{8,4},{9,3},... | collective-permute-start | bytes 393224 | tf_op jit(solution)/shard_map/ppermute | solution.py:101
  68.5 5.0 %collective-permute-start.17 = (bf16[256,256]{1,0:T(8,128)(2,1)S(1)}, bf16[256,256]{1,0:T(8,128)(2,1)S(1)}, u32[]{:S(2)}, u32[]{:S(2)}) collective-permute-start(bf16[256,256]{1,0:T(8,128)(2,1)S(1)} %get-tuple-element.61), channel_id=1, source_target_pairs={{0,8},{8,0},{16,24},{24,16},{1,9},{9,1},{17,25},{25,17},{2,10},{10... | collective-permute-start | bytes 393224 | tf_op jit(solution)/shard_map/ppermute | solution.py:87
  68.6 5.1 %collective-permute-start.16 = (bf16[256,256]{1,0:T(8,128)(2,1)S(1)}, bf16[256,256]{1,0:T(8,128)(2,1)S(1)}, u32[]{:S(2)}, u32[]{:S(2)}) collective-permute-start(bf16[256,256]{1,0:T(8,128)(2,1)S(1)} %get-tuple-element.62), channel_id=1, source_target_pairs={{0,4},{1,3},{2,6},{3,1},{4,0},{5,7},{6,2},{7,5},{8,12},{9,11},{10,... | collective-permute-start | bytes 393224 | tf_op jit(solution)/shard_map/ppermute | solution.py:95
  69.4 12.6 %collective-permute-start.14 = (bf16[512,512]{1,0:T(8,128)(2,1)S(1)}, bf16[512,512]{1,0:T(8,128)(2,1)S(1)}, u32[]{:S(2)}, u32[]{:S(2)}) collective-permute-start(bf16[512,512]{1,0:T(8,128)(2,1)S(1)} %pad_maximum_fusion), channel_id=1, source_target_pairs={{0,1},{1,0},{2,3},{3,2},{4,5},{5,4},{6,7},{7,6},{8,9},{9,8},{10,11... | collective-permute-start | bytes 1572872 | tf_op jit(solution)/shard_map/ppermute | solution.py:91
  73.8 9.7 %copy-start.1 = (f32[1,128,4096]{2,1,0:T(8,128)S(1)}, f32[1,128,4096]{2,1,0:T(8,128)}, u32[]{:S(2)}) copy-start(f32[1,128,4096]{2,1,0:T(8,128)} %param.8) | copy-start | bytes 6291460
  73.8 6.7 %collective-permute-start.23 = (bf16[256,256]{1,0:T(8,128)(2,1)S(1)}, bf16[256,256]{1,0:T(8,128)(2,1)S(1)}, u32[]{:S(2)}, u32[]{:S(2)}) collective-permute-start(bf16[256,256]{1,0:T(8,128)(2,1)S(1)} %get-tuple-element.57), channel_id=1, source_target_pairs={{0,12},{1,11},{2,14},{3,9},{4,8},{5,15},{6,10},{7,13},{8,4},{9,3},... | collective-permute-start | bytes 393224 | tf_op jit(solution)/shard_map/ppermute | solution.py:101
  76.2 5.4 %collective-permute-start.22 = (bf16[256,256]{1,0:T(8,128)(2,1)S(1)}, bf16[256,256]{1,0:T(8,128)(2,1)S(1)}, u32[]{:S(2)}, u32[]{:S(2)}) collective-permute-start(bf16[256,256]{1,0:T(8,128)(2,1)S(1)} %get-tuple-element.58), channel_id=1, source_target_pairs={{0,8},{8,0},{16,24},{24,16},{1,9},{9,1},{17,25},{25,17},{2,10},{10... | collective-permute-start | bytes 393224 | tf_op jit(solution)/shard_map/ppermute | solution.py:87
  76.5 5.4 %collective-permute-start.21 = (bf16[256,256]{1,0:T(8,128)(2,1)S(1)}, bf16[256,256]{1,0:T(8,128)(2,1)S(1)}, u32[]{:S(2)}, u32[]{:S(2)}) collective-permute-start(bf16[256,256]{1,0:T(8,128)(2,1)S(1)} %get-tuple-element.59), channel_id=1, source_target_pairs={{0,4},{1,3},{2,6},{3,1},{4,0},{5,7},{6,2},{7,5},{8,12},{9,11},{10,... | collective-permute-start | bytes 393224 | tf_op jit(solution)/shard_map/ppermute | solution.py:95
  77.4 4.7 %collective-permute-start.19 = (bf16[512,256]{1,0:T(8,128)(2,1)S(1)}, bf16[512,256]{1,0:T(8,128)(2,1)S(1)}, u32[]{:S(2)}, u32[]{:S(2)}) collective-permute-start(bf16[512,256]{1,0:T(8,128)(2,1)S(1)} %pad_maximum_fusion.1), channel_id=1, source_target_pairs={{0,1},{1,0},{2,3},{3,2},{4,5},{5,4},{6,7},{7,6},{8,9},{9,8},{10,11... | collective-permute-start | bytes 786440 | tf_op jit(solution)/shard_map/ppermute | solution.py:91
  81.9 1.6 %collective-permute-start.24 = (bf16[512,256]{1,0:T(8,128)(2,1)S(1)}, bf16[512,256]{1,0:T(8,128)(2,1)S(1)}, u32[]{:S(2)}, u32[]{:S(2)}) collective-permute-start(bf16[512,256]{1,0:T(8,128)(2,1)S(1)} %pad_maximum_fusion.2), channel_id=1, source_target_pairs={{0,1},{1,0},{2,3},{3,2},{4,5},{5,4},{6,7},{7,6},{8,9},{9,8},{10,11... | collective-permute-start | bytes 786440 | tf_op jit(solution)/shard_map/ppermute | solution.py:91
